TPU v7x, 32 devices: a whole 2x2x4 slice. The times are simulated.
32 devices in a mesh: freq: 4 (over y, x), tile: 8 (over z, core).
Axes of the slice: x: 2, y: 2, z: 4, core: 2. Of those that a mesh axis runs over, the one named last changes fastest.
Arguments:
- u_data: bfloat16 [8, 4096, 128], P('freq', 'tile'), may hold values from -6 to 6
- u_basis: bfloat16 [8, 16, 16, 2, 48, 256], P('freq', 'tile'), may hold values from -0.25 to 0.25
- v_basis: bfloat16 [8, 16, 16, 2, 48, 256], P('freq', None, 'tile'), may hold values from -0.21875 to 0.21875
- ranks: int32 [8, 16, 16], P('freq'), may hold values from 8 to 48, as said below
- time_mask: int32 [64, 64], replicated, may hold values 0 or 1
Outputs:
- result: bfloat16 [8, 4096, 128], P('freq', 'tile')
Inputs may be any that keep to these rules, and one draw needn't show every extreme that they name: For every tile and every m, ranks[2 m + 1, i, j] = 56 - ranks[2 m, i, j].
All inputs are finite; a program needn't handle non-finite values.
Results may differ from a plain program's by a relative error of at most 0.006.
Values may be sent and summed in bfloat16 or wider, within the bound.
No kernel may reach another device: no remote copies, remote signals or barrier semaphores. Data moves between devices by JAX's collectives and lax.ppermute only.
A program may use at most 128 MiB of HBM per device.

v0:
```python
import functools
import math

import jax
import jax.numpy as jnp
import numpy as np
from jax import lax
from jax.experimental import pallas as pl
from jax.experimental.pallas import tpu as pltpu
from jax.sharding import PartitionSpec as P

vmem_limit = 48 * 1024 * 1024
bf16 = jnp.bfloat16
f32 = jnp.float32

whole = pl.BlockSpec(memory_space=pltpu.VMEM)
scalars = pl.BlockSpec(memory_space=pltpu.SMEM)
far = pl.BlockSpec(memory_space=pltpu.HBM)
anywhere = pl.BlockSpec(memory_space=pl.ANY)


def hold(value):
    return pltpu.with_memory_space_constraint(value, pltpu.HBM)


def call(kernel, name, ins, outs, scratch, flops=0, moved=0, specs=None):
    shapes = [jax.ShapeDtypeStruct(shape, kind) for shape, kind in outs]
    return pl.pallas_call(
        kernel,
        in_specs=[spec for spec, _ in ins],
        out_specs=specs or [whole] * len(outs),
        out_shape=shapes,
        scratch_shapes=scratch,
        compiler_params=pltpu.CompilerParams(vmem_limit_bytes=vmem_limit),
        cost_estimate=pl.CostEstimate(flops=flops, bytes_accessed=moved, transcendentals=0),
        name=name,
    )(*[value for _, value in ins])


def dot(lhs, rhs, lhs_dim, rhs_dim, precision=None):
    return lax.dot_general(
        lhs, rhs, (((lhs_dim,), (rhs_dim,)), ((), ())),
        precision=precision, preferred_element_type=f32,
    )


def lag_tables(count, time_count, lanes):
    samples = np.arange(time_count)[:, None]
    lags = np.arange(count)[None, :]
    angle = 2.0 * math.pi / time_count * ((samples * lags) % time_count)
    table = np.zeros((time_count, lanes), np.float32)
    table[:, :count] = np.cos(angle) / time_count
    table[:, count : 2 * count] = np.sin(angle) / time_count
    return table


def lag_choice(count, quarter):
    side = count * 2 * quarter
    choice = np.zeros((2 * count, count, 2, count, 2, quarter), np.float32)
    for f in range(count):
        for g in range(count):
            sign = 1.0 if g >= f else -1.0
            lag = abs(g - f)
            choice[lag, f, 0, g, 0] = 1.0
            choice[lag, f, 1, g, 1] = 1.0
            choice[count + lag, f, 0, g, 1] = -sign
            choice[count + lag, f, 1, g, 0] = sign
    same = np.arange(quarter)[:, None] == np.arange(side)[None, :] % quarter
    return choice.reshape(2 * count, 2 * count * side), same.astype(np.float32)


def pack_rows(stage, slot, row, rank, first, second):
    size = first.shape[0]
    stage[slot, pl.ds(row, size), :] = first
    stage[slot, pl.ds(row + rank, size), :] = second


def unpack_rows(stage, slot, row, rank, total, coeffs, base):
    slots = total - total // 7
    first = stage[slot, pl.ds(row, slots), :]
    second = stage[slot, pl.ds(row + rank, slots), :]
    ids = lax.broadcasted_iota(jnp.int32, first.shape, 0)
    at = pl.ds(pl.multiple_of(base, 16), slots)
    coeffs[0, at, :] = jnp.where(ids < rank, first, 0.0).astype(bf16)
    coeffs[1, at, :] = jnp.where(ids < total - rank, second, 0.0).astype(bf16)


def side_by_side(real, imag):
    flat = (-1, real.shape[-1])
    return jnp.concatenate([real.reshape(flat), imag.reshape(flat)], axis=1)


def plain_product(coeffs, both):
    half, tile = coeffs.shape[1] // 2, both.shape[1] // 2
    product = dot(coeffs, both, 0, 0)
    lead, trail = product[:, :tile], product[:, tile:]
    return jnp.concatenate([lead[:half] - trail[half:], lead[half:] + trail[:half]], axis=0)


def parity(value, mask):
    odd = value & 0
    bit = 0
    while mask >> bit:
        if (mask >> bit) & 1:
            odd = odd ^ ((value >> bit) & 1)
        bit += 1
    return odd


def exchange_slots(devices):
    half = devices // 2
    spare, mixed = list(range(half, devices)), []
    alone = []
    for near in reversed(range(2, half)):
        found = [
            (far, mask)
            for far in spare
            for mask in range(3, devices, 2)
            if not parity(near, mask) and not parity(far, mask)
        ]
        if found and len(spare) > 2:
            far, mask = found[0]
            spare.remove(far)
            mixed += [(far, near, mask), (near, far, mask)]
        else:
            alone.append((near, near, 1))
    first = [(far, far, 1) for far in reversed(spare)]
    return first, mixed + alone + [(1, 1, 1)] * (devices > 1) + [(0, 0, 1)]


def partner(me, slot):
    even, odd, mask = slot
    if even == odd:
        return me ^ even
    return me ^ (even ^ (parity(me, mask) * (even ^ odd)))


def unstage(outs, slots_out, stage, m, devices, span, size, me):
    for out, slot in zip(outs, slots_out):
        for c in range(span):
            rows = stage[(m * devices + partner(me, slot)) * span + c, pl.ds(0, size), :]
            out[m, pl.ds(c * size, size), :] = rows.astype(bf16)


def adjoint_kernel(slots_out, turn, ranks_far, basis_far, u_far, *rest):
    shifts = sorted({n for slot in slots_out for n in slot[:2]})
    ranks, u_ref, basis, stage, sems = rest[-5:]
    outs = rest[-5 - len(slots_out) - turn : -5 - turn]
    turned = rest[-6] if turn else u_far
    freqs, rows, devices, cols, _, slots, tile = basis_far.shape
    total = slots + slots // 6
    half = turned.shape[3] // 2
    me = lax.axis_index("tile")
    rank_copy = pltpu.make_async_copy(ranks_far, ranks, sems.at[0])
    if turn:
        data_copy = pltpu.make_async_copy(u_far, u_ref, sems.at[1])
        data_copy.start()
    rank_copy.start()
    copies = [[] for _ in range(rows)]
    for i in range(rows):
        for f in range(freqs):
            for n, shift in enumerate(shifts):
                copy = pltpu.make_async_copy(
                    basis_far.at[f, i, me ^ shift],
                    basis.at[f, i, n],
                    sems.at[2 + (i * freqs + f) * len(shifts) + n],
                )
                copy.start(priority=n % 2)
                copies[i].append(copy)
    if turn:
        data_copy.wait()
        for f in range(freqs):
            for i in range(rows):
                values = u_ref[f, i * tile : (i + 1) * tile, :]
                wide = values.astype(f32)
                lane = lax.broadcasted_iota(jnp.int32, wide.shape, 1)
                rolled = pltpu.roll(wide, half, 1)
                turned[f, i, :tile, :] = values
                turned[f, i, tile:, :] = jnp.where(lane < half, rolled, -rolled).astype(bf16)
    rank_copy.wait()
    for i in range(rows):
        for copy in copies[i]:
            copy.wait()
        for m in range(freqs // 2):
            pair = []
            for f in (2 * m, 2 * m + 1):
                both = side_by_side(basis[f, i, :, :, 0], basis[f, i, :, :, 1])
                pair.append(dot(both, turned[f, i], 1, 0))
            for n, shift in enumerate(shifts):
                for c in range(cols):
                    rank = ranks[2 * m, me * rows + i, (me ^ shift) * cols + c]
                    cut = slice((n * cols + c) * slots, (n * cols + c + 1) * slots)
                    slot = (m * devices + (me ^ shift)) * cols + c
                    pack_rows(stage, slot, i * total, rank, pair[0][cut], pair[1][cut])
    for m in range(freqs // 2):
        unstage(outs, slots_out, stage, m, devices, cols, rows * total, me)


def image_kernel(slots_in, owners, ranks_near, basis, *rest):
    devices = len(slots_in)
    packed = rest[:devices]
    outs = rest[-owners - 5 : -5]
    ranks, stage, coeffs, z, sem = rest[-5:]
    freqs, _, rows, cols, _, slots, tile = basis.shape
    total = slots + slots // 6
    half = coeffs.shape[3] // 2
    quarter = half // owners
    size = rows * total
    me, mine = lax.axis_index("tile"), lax.axis_index("freq")
    rank_copy = pltpu.make_async_copy(ranks_near, ranks, sem)
    rank_copy.start()
    for m in range(freqs // 2):
        for s in range(devices):
            for c in range(cols):
                block = packed[s][m, pl.ds(c * size, size), :]
                stage[(m * devices + s) * cols + c, pl.ds(0, size), :] = block.astype(f32)
    rank_copy.wait()
    for m in range(freqs // 2):
        for c in range(cols):
            for s in range(devices):
                for i in range(rows):
                    row = partner(me, slots_in[s]) * rows + i
                    rank = ranks[0, (m * devices * rows + row) * cols + c]
                    slot = (m * devices + s) * cols + c
                    unpack_rows(stage, slot, i * total, rank, total, coeffs.at[c], row * slots)
            for n in range(2):
                f = 2 * m + n
                both = side_by_side(basis[f, :, :, c, 0], basis[f, :, :, c, 1])
                z[f, :, pl.ds(c * tile, tile)] = plain_product(coeffs[c, n], both)
    for r in range(owners):
        low = pl.multiple_of((mine ^ r) * quarter, quarter)
        for f in range(freqs):
            real = z[f, pl.ds(low, quarter), :]
            imag = z[f, pl.ds(half + low, quarter), :]
            outs[r][f] = jnp.concatenate([real, imag], axis=0).astype(bf16)


def prepare_kernel(rows, cols, ranks_far, mask, table, choice, same, *rest):
    short, high, low, ranks, full, sem = rest[-6:]
    freqs, row_tiles, col_tiles = ranks.shape
    me = lax.axis_index("tile")
    rank_copy = pltpu.make_async_copy(ranks_far, ranks, sem)
    rank_copy.start()
    exact = lax.Precision.HIGHEST
    full[...] = dot(mask[...].astype(f32), table[...], 0, 0, exact)
    quarter, side = same.shape
    mine = full[pl.ds(pl.multiple_of(lax.axis_index("freq") * quarter, quarter), quarter), :]
    entries = dot(mine[:, : choice.shape[0]], choice[...], 1, 0, exact)
    for n in range(side // quarter):
        block = entries[:, n * side : (n + 1) * side] * same[...]
        upper = block.astype(bf16)
        high[n * quarter : (n + 1) * quarter, :] = upper
        low[n * quarter : (n + 1) * quarter, :] = (block - upper.astype(f32)).astype(bf16)
    rank_copy.wait()
    at = 0
    for m in range(freqs // 2):
        for row in range(row_tiles):
            for c in range(cols):
                short[0, at] = ranks[2 * m, row, me * cols + c]
                at += 1
    for m in range(freqs // 2):
        for i in range(rows):
            for col in range(col_tiles):
                short[0, at] = ranks[2 * m, me * rows + i, col]
                at += 1


def mix_kernel(owners, high, low, *rest):
    arrived = rest[:owners][::-1]
    outs = rest[owners : 2 * owners]
    z, w = rest[2 * owners :]
    freqs, rows, span = arrived[0].shape
    mine = lax.axis_index("freq")
    size = freqs * rows
    for r in range(owners):
        z[pl.ds(pl.multiple_of((mine ^ r) * size, 16), size), :] = arrived[r][...].reshape(size, span)
    w[...] = dot(high[...], z[...], 1, 0) + dot(low[...], z[...], 1, 0)
    for r in range(owners):
        block = w[pl.ds(pl.multiple_of((mine ^ r) * size, 16), size), :]
        outs[r][...] = block.reshape(freqs, rows, span).astype(bf16)


def forward_kernel(slots_out, owners, ranks_near, basis, *rest):
    devices = len(slots_out)
    arrived = rest[:owners][::-1]
    outs = rest[owners : owners + devices]
    ranks, w, stage, sem = rest[owners + devices :]
    freqs, _, rows, cols, _, slots, tile = basis.shape
    total = slots + slots // 6
    half = w.shape[2] // 2
    quarter = half // owners
    me, mine = lax.axis_index("tile"), lax.axis_index("freq")
    rank_copy = pltpu.make_async_copy(ranks_near, ranks, sem)
    rank_copy.start()
    for r in range(owners):
        low = pl.multiple_of((mine ^ r) * quarter, quarter)
        for f in range(freqs):
            for c in range(cols):
                at = slice(c * tile, (c + 1) * tile)
                real, imag = arrived[r][f, :quarter, at], arrived[r][f, quarter:, at]
                w[f, c, pl.ds(low, quarter), :tile] = real
                w[f, c, pl.ds(half + low, quarter), :tile] = imag
                w[f, c, pl.ds(low, quarter), tile:] = imag
                w[f, c, pl.ds(half + low, quarter), tile:] = -real
    rank_copy.wait()
    for m in range(freqs // 2):
        for c in range(cols):
            pair = []
            for f in (2 * m, 2 * m + 1):
                both = side_by_side(basis[f, :, :, c, 0], basis[f, :, :, c, 1])
                pair.append(dot(both, w[f, c], 1, 1))
            for d in range(devices):
                for i in range(rows):
                    rank = ranks[0, (m * devices * rows + d * rows + i) * cols + c]
                    cut = slice((d * rows + i) * slots, (d * rows + i + 1) * slots)
                    slot = (m * devices + d) * cols + c
                    pack_rows(stage, slot, i * total, rank, pair[0][cut], pair[1][cut])
        unstage(outs, slots_out, stage, m, devices, cols, rows * total, me)


def result_kernel(slots_in, ranks_near, basis, *rest):
    devices = len(slots_in)
    packed = rest[:devices]
    out, ranks, stage, coeffs, sem = rest[devices:]
    freqs, rows, _, cols, _, slots, tile = basis.shape
    total = slots + slots // 6
    size = rows * total
    before = freqs // 2 * devices * rows * cols
    me = lax.axis_index("tile")
    rank_copy = pltpu.make_async_copy(ranks_near, ranks, sem)
    rank_copy.start()
    for m in range(freqs // 2):
        for s in range(devices):
            for c in range(cols):
                block = packed[s][m, pl.ds(c * size, size), :]
                stage[(m * devices + s) * cols + c, pl.ds(0, size), :] = block.astype(f32)
    rank_copy.wait()
    for m in range(freqs // 2):
        for i in range(rows):
            for s in range(devices):
                for c in range(cols):
                    col = partner(me, slots_in[s]) * cols + c
                    rank = ranks[0, before + (m * rows + i) * devices * cols + col]
                    slot = (m * devices + s) * cols + c
                    unpack_rows(stage, slot, i * total, rank, total, coeffs.at[i], col * slots)
            for n in range(2):
                f = 2 * m + n
                both = side_by_side(basis[f, i, :, :, 0], basis[f, i, :, :, 1])
                r = plain_product(coeffs[i, n], both)
                out[f, pl.ds(i * tile, tile), :] = r.T.astype(bf16)


def send(value, axis, slot):
    if slot[:2] == (0, 0):
        return value
    return lax.ppermute(value, axis, [(d, partner(d, slot)) for d in range(lax.axis_size(axis))])


def spread(values, axis, slots):
    return [(whole, send(value, axis, slot)) for value, slot in zip(values, slots)]


def to_owners(values):
    return spread(values[::-1], "freq", [(n, n, 1) for n in reversed(range(len(values)))])


def local(u_data, u_basis, v_basis, ranks, time_mask):
    freqs, row_count, width = u_data.shape
    rows, col_tiles, _, slots, tile = u_basis.shape[1:]
    row_tiles, cols = v_basis.shape[1:3]
    total = slots // 6 + slots
    pairs = freqs // 2
    devices = lax.axis_size("tile")
    owners = lax.axis_size("freq")
    stage_rows = rows * total + 2 * slots
    quarter = width // 2 // owners
    count = owners * freqs
    side = count * 2 * quarter
    by_cols = u_basis.reshape(freqs, rows, devices, cols, 2, slots, tile)
    by_rows = v_basis.reshape(freqs, devices, rows, cols, 2, slots, tile)
    per_device = [((pairs, cols * rows * total, width), bf16)] * devices
    per_owner = [((freqs, 2 * quarter, cols * tile), bf16)] * owners
    work = {"flops": 4 * row_count * slots * width * col_tiles * freqs * 2, "moved": u_basis.size * 2}
    count_short = pairs * (row_tiles * cols + rows * col_tiles)
    ranks_here = pltpu.SMEM((1, count_short), jnp.int32)
    stage = pltpu.VMEM((pairs * devices * cols, stage_rows, width), f32)
    one = pltpu.SemaphoreType.DMA

    table = lag_tables(count, time_mask.shape[0], 128)
    choice, same = lag_choice(count, quarter)
    def share(partners):
        return {name: value * partners // devices for name, value in work.items()}

    early, late = exchange_slots(devices)
    slots_all = early + late
    data, packed = (far, hold(u_data)), []
    for turn, part in ((1, early), (0, late)):
        partners = len(part)
        made = call(
            functools.partial(adjoint_kernel, part, turn),
            "adjoint",
            [(far, hold(ranks)), (far, hold(by_cols)), data],
            [((pairs, cols * rows * total, width), bf16)] * partners
            + [((freqs, rows, 2 * tile, width), bf16)] * turn,
            [
                pltpu.SMEM(ranks.shape, jnp.int32),
                pltpu.VMEM((freqs, row_count, width), bf16),
                pltpu.VMEM((freqs, rows, partners, cols, 2, slots, tile), bf16),
                stage,
                one((2 + freqs * rows * partners,)),
            ],
            **share(partners),
        )
        if turn:
            data = (whole, made[-1])
        packed += made[:partners]
    short, *window = call(
        functools.partial(prepare_kernel, rows, cols),
        "prepare",
        [(far, hold(ranks))]
        + [(whole, jnp.asarray(x)) for x in (time_mask, table, choice, same)]
        + [(anywhere, packed[-1])],
        [((1, count_short), jnp.int32)] + [((side, side), bf16)] * 2,
        [pltpu.SMEM(ranks.shape, jnp.int32), pltpu.VMEM((width // 2, 128), f32), one],
        specs=[scalars, whole, whole],
        flops=6 * quarter * 2 * count * 2 * count * side,
    )
    images = call(
        functools.partial(image_kernel, slots_all, owners),
        "image",
        [(whole, short), (whole, by_rows)] + spread(packed, "tile", slots_all),
        per_owner,
        [
            ranks_here,
            stage,
            pltpu.VMEM((cols, 2, row_tiles * slots, width), bf16),
            pltpu.VMEM((freqs, width, cols * tile), f32),
            one,
        ],
        **work,
    )
    mixed = call(
        functools.partial(mix_kernel, owners),
        "mix",
        [(whole, x) for x in window] + to_owners(images),
        per_owner,
        [pltpu.VMEM((side, cols * tile), bf16), pltpu.VMEM((side, cols * tile), f32)],
        flops=4 * side * side * cols * tile,
    )
    packed = call(
        functools.partial(forward_kernel, slots_all, owners),
        "forward",
        [(whole, short), (whole, by_rows)] + to_owners(mixed),
        per_device,
        [ranks_here, pltpu.VMEM((freqs, cols, width, 2 * tile), bf16), stage, one],
        **work,
    )
    [out] = call(
        functools.partial(result_kernel, slots_all),
        "result",
        [(whole, short), (whole, by_cols)] + spread(packed, "tile", slots_all),
        [((freqs, row_count, width), bf16)],
        [ranks_here, stage, pltpu.VMEM((rows, 2, col_tiles * slots, width), bf16), one],
        **work,
    )
    return out


def solution(mesh):
    placed = (
        P("freq", "tile", None),
        P("freq", "tile", None, None, None, None),
        P("freq", None, "tile", None, None, None),
        P("freq", None, None),
        P(),
    )
    return jax.shard_map(
        local, mesh=mesh, in_specs=placed, out_specs=P("freq", "tile", None), check_vma=False
    )
```

profile of v0, /device:TPU:0, one launch (start us, length us, event | category | flops | bytes accessed | tf_op | source)
XLA Modules:
  0.0 51.2 jit_solution(4266673568585617771)
XLA Ops:
  0.0 1.9 %adjoint.2 = (bf16[1,224,128]{2,1,0:T(8,128)(2,1)S(1)}, bf16[1,224,128]{2,1,0:T(8,128)(2,1)S(1)}, bf16[2,2,512,128]{3,2,1,0:T(8,128)(2,1)S(1)}) custom-call(s32[2,16,16]{2,1,0:T(8,128)} %ranks_far.5, bf16[2,2,8,2,2,48,256]{6,5,4,3,2,1,0:T(8,128)(2,1)} %bitcast.2, bf16[2,512,128]{2,1,0:T(8,128)(2,1)} %u_far.1), custom_call_target="tpu_custom_call" | custom-call | flops 201326592 | bytes 786432 | tf_op jit(solution)/shard_map/adjoint/pallas_call | solution.py:28
  2.0 4.6 %collective-permute-start = (bf16[1,224,128]{2,1,0:T(8,128)(2,1)S(1)}, bf16[1,224,128]{2,1,0:T(8,128)(2,1)S(1)}, u32[]{:S(2)}, u32[]{:S(2)}) collective-permute-start(bf16[1,224,128]{2,1,0:T(8,128)(2,1)S(1)} %get-tuple-element.38), channel_id=1, source_target_pairs={{0,7},{1,6},{2,5},{3,4},{4,3},{5,2},{6,1},{7,0},{8,15},{9,14},{10,... | collective-permute-start | bytes 172040 | tf_op jit(solution)/shard_map/ppermute | solution.py:356
  6.5 0.6 %collective-permute-start.1 = (bf16[1,224,128]{2,1,0:T(8,128)(2,1)S(1)}, bf16[1,224,128]{2,1,0:T(8,128)(2,1)S(1)}, u32[]{:S(2)}, u32[]{:S(2)}) collective-permute-start(bf16[1,224,128]{2,1,0:T(8,128)(2,1)S(1)} %get-tuple-element.39), channel_id=1, source_target_pairs={{0,6},{1,7},{2,4},{3,5},{4,2},{5,3},{6,0},{7,1},{8,14},{9,15},{10,... | collective-permute-start | bytes 172040 | tf_op jit(solution)/shard_map/ppermute | solution.py:356
  7.2 2.8 %adjoint.3 = (bf16[1,224,128]{2,1,0:T(8,128)(2,1)S(1)}, bf16[1,224,128]{2,1,0:T(8,128)(2,1)S(1)}, bf16[1,224,128]{2,1,0:T(8,128)(2,1)S(1)}, bf16[1,224,128]{2,1,...) custom-call(s32[2,16,16]{2,1,0:T(8,128)} %ranks_far.5, ...), custom_call_target="tpu_custom_call" | custom-call | flops 603979776 | bytes 2359296 | tf_op jit(solution)/shard_map/adjoint/pallas_call | solution.py:28
  10.0 0.4 collective-permute-start.2
  10.4 3.1 %collective-permute-start.3 = (bf16[1,224,128]{2,1,0:T(8,128)(2,1)S(1)}, bf16[1,224,128]{2,1,0:T(8,128)(2,1)S(1)}, u32[]{:S(2)}, u32[]{:S(2)}) collective-permute-start(bf16[1,224,128]{2,1,0:T(8,128)(2,1)S(1)} %get-tuple-element.41), channel_id=1, source_target_pairs={{0,3},{1,5},{2,6},{3,0},{4,7},{5,1},{6,2},{7,4},{8,11},{9,13},{10,... | collective-permute-start | bytes 172040 | tf_op jit(solution)/shard_map/ppermute | solution.py:356
  13.6 1.2 %collective-permute-start.5 = (bf16[1,224,128]{2,1,0:T(8,128)(2,1)S(1)}, bf16[1,224,128]{2,1,0:T(8,128)(2,1)S(1)}, u32[]{:S(2)}, u32[]{:S(2)}) collective-permute-start(bf16[1,224,128]{2,1,0:T(8,128)(2,1)S(1)} %get-tuple-element.43), channel_id=1, source_target_pairs={{0,2},{1,4},{2,0},{3,6},{4,1},{5,7},{6,3},{7,5},{8,10},{9,12},{10,... | collective-permute-start | bytes 172040 | tf_op jit(solution)/shard_map/ppermute | solution.py:356
  14.8 1.6 %prepare.1 = (s32[1,64]{1,0:T(1,128)S(1)}, bf16[256,256]{1,0:T(8,128)(2,1)S(1)}, bf16[256,256]{1,0:T(8,128)(2,1)S(1)}) custom-call(s32[2,16,16]{2,1,0:T(8,128)} %ranks_far.5, s32[64,64]{1,0:T(8,128)S(1)} %copy-done.3, f32[64,128]{1,0:T(8,128)S(1)} %copy-done.4, f32[16,4096]{1,0:T(8,128)S(1)} %copy-done.2, f32[16,256]{1,0:T(8,128)S(1)} %copy-done.5, ...), custom_call_target="tpu_custom_call" | custom-call | flops 6291456 | tf_op jit(solution)/shard_map/prepare/pallas_call | solution.py:28
  16.6 2.5 %collective-permute-done.4.rest_4_ = bf16[1,224,128]{2,1,0:T(8,128)(2,1)S(1)} collective-permute-done((bf16[1,224,128]{2,1,0:T(8,128)(2,1)S(1)}, bf16[1,224,128]{2,1,0:T(8,128)(2,1)S(1)}, u32[]{:S(2)}, u32[]{:S(2)}) %collective-permute-start.4) | collective-permute-done | bytes 57376 | tf_op jit(solution)/shard_map/ppermute | solution.py:356
  19.2 1.4 %image.1 = (bf16[2,32,512]{2,1,0:T(8,128)(2,1)S(1)}, bf16[2,32,512]{2,1,0:T(8,128)(2,1)S(1)}, bf16[2,32,512]{2,1,0:T(8,128)(2,1)S(1)}, bf16[2,32,512]{2,1,0:T(8,128)(2,1)S(1)}) custom-call(s32[1,64]{1,0:T(1,128)S(1)} %get-tuple-element.35.ranks_near, bf16[2,8,2,2,2,48,256]{6,5,4,3,2,1,0:T(8,128)(2,1)S(1)} %bitcast.5, ...), custom_call_target="tpu_custom_call" | custom-call | flops 805306368 | bytes 3145728 | tf_op jit(solution)/shard_map/image/pallas_call | solution.py:28
  20.6 2.5 %collective-permute-start.7 = (bf16[2,32,512]{2,1,0:T(8,128)(2,1)S(1)}, bf16[2,32,512]{2,1,0:T(8,128)(2,1)S(1)}, u32[]{:S(2)}, u32[]{:S(2)}) collective-permute-start(bf16[2,32,512]{2,1,0:T(8,128)(2,1)S(1)} %get-tuple-element.45), channel_id=1, source_target_pairs={{0,24},{8,16},{16,8},{24,0},{1,25},{9,17},{17,9},{25,1},{2,26},{10... | collective-permute-start | bytes 196616 | tf_op jit(solution)/shard_map/ppermute | solution.py:356
  23.1 0.5 collective-permute-start.8
  23.6 0.5 %collective-permute-start.9 = (bf16[2,32,512]{2,1,0:T(8,128)(2,1)S(1)}, bf16[2,32,512]{2,1,0:T(8,128)(2,1)S(1)}, u32[]{:S(2)}, u32[]{:S(2)}) collective-permute-start(bf16[2,32,512]{2,1,0:T(8,128)(2,1)S(1)} %get-tuple-element.47), channel_id=1, source_target_pairs={{0,8},{8,0},{16,24},{24,16},{1,9},{9,1},{17,25},{25,17},{2,10},{10... | collective-permute-start | bytes 196616 | tf_op jit(solution)/shard_map/ppermute | solution.py:356
  24.1 1.7 %collective-permute-done.7.rest_0_ = bf16[2,32,512]{2,1,0:T(8,128)(2,1)S(1)} collective-permute-done((bf16[2,32,512]{2,1,0:T(8,128)(2,1)S(1)}, bf16[2,32,512]{2,1,0:T(8,128)(2,1)S(1)}, u32[]{:S(2)}, u32[]{:S(2)}) %collective-permute-start.7) | collective-permute-done | bytes 65568 | tf_op jit(solution)/shard_map/ppermute | solution.py:356
  25.8 1.5 %collective-permute-done.8.rest_1_ = bf16[2,32,512]{2,1,0:T(8,128)(2,1)S(1)} collective-permute-done((bf16[2,32,512]{2,1,0:T(8,128)(2,1)S(1)}, bf16[2,32,512]{2,1,0:T(8,128)(2,1)S(1)}, u32[]{:S(2)}, u32[]{:S(2)}) %collective-permute-start.8) | collective-permute-done | bytes 65568 | tf_op jit(solution)/shard_map/ppermute | solution.py:356
  27.3 0.5 collective-permute-done.9.rest_2_
  27.8 0.4 mix.1
  28.2 1.6 %collective-permute-start.10 = (bf16[2,32,512]{2,1,0:T(8,128)(2,1)S(1)}, bf16[2,32,512]{2,1,0:T(8,128)(2,1)S(1)}, u32[]{:S(2)}, u32[]{:S(2)}) collective-permute-start(bf16[2,32,512]{2,1,0:T(8,128)(2,1)S(1)} %get-tuple-element.49), channel_id=1, source_target_pairs={{0,24},{8,16},{16,8},{24,0},{1,25},{9,17},{17,9},{25,1},{2,26},{10... | collective-permute-start | bytes 196616 | tf_op jit(solution)/shard_map/ppermute | solution.py:356
  29.8 0.7 %collective-permute-start.11 = (bf16[2,32,512]{2,1,0:T(8,128)(2,1)S(1)}, bf16[2,32,512]{2,1,0:T(8,128)(2,1)S(1)}, u32[]{:S(2)}, u32[]{:S(2)}) collective-permute-start(bf16[2,32,512]{2,1,0:T(8,128)(2,1)S(1)} %get-tuple-element.50), channel_id=1, source_target_pairs={{0,16},{8,24},{16,0},{24,8},{1,17},{9,25},{17,1},{25,9},{2,18},{10... | collective-permute-start | bytes 196616 | tf_op jit(solution)/shard_map/ppermute | solution.py:356
  30.5 1.2 %collective-permute-start.12 = (bf16[2,32,512]{2,1,0:T(8,128)(2,1)S(1)}, bf16[2,32,512]{2,1,0:T(8,128)(2,1)S(1)}, u32[]{:S(2)}, u32[]{:S(2)}) collective-permute-start(bf16[2,32,512]{2,1,0:T(8,128)(2,1)S(1)} %get-tuple-element.51), channel_id=1, source_target_pairs={{0,8},{8,0},{16,24},{24,16},{1,9},{9,1},{17,25},{25,17},{2,10},{10... | collective-permute-start | bytes 196616 | tf_op jit(solution)/shard_map/ppermute | solution.py:356
  31.8 1.9 %collective-permute-done.10.rest_0_ = bf16[2,32,512]{2,1,0:T(8,128)(2,1)S(1)} collective-permute-done((bf16[2,32,512]{2,1,0:T(8,128)(2,1)S(1)}, bf16[2,32,512]{2,1,0:T(8,128)(2,1)S(1)}, u32[]{:S(2)}, u32[]{:S(2)}) %collective-permute-start.10) | collective-permute-done | bytes 65568 | tf_op jit(solution)/shard_map/ppermute | solution.py:356
  33.6 0.7 %collective-permute-done.11.rest_1_ = bf16[2,32,512]{2,1,0:T(8,128)(2,1)S(1)} collective-permute-done((bf16[2,32,512]{2,1,0:T(8,128)(2,1)S(1)}, bf16[2,32,512]{2,1,0:T(8,128)(2,1)S(1)}, u32[]{:S(2)}, u32[]{:S(2)}) %collective-permute-start.11) | collective-permute-done | bytes 65568 | tf_op jit(solution)/shard_map/ppermute | solution.py:356
  34.3 0.5 collective-permute-done.12.rest_2_
  34.8 1.6 %forward.1 = (bf16[1,224,128]{2,1,0:T(8,128)(2,1)S(1)}, bf16[1,224,128]{2,1,0:T(8,128)(2,1)S(1)}, bf16[1,224,128]{2,1,0:T(8,128)(2,1)S(1)}, bf16[1,224,128]{2,1,...) custom-call(s32[1,64]{1,0:T(1,128)S(1)} %get-tuple-element.35.ranks_, ...), custom_call_target="tpu_custom_call" | custom-call | flops 805306368 | bytes 3145728 | tf_op jit(solution)/shard_map/forward/pallas_call | solution.py:28
  36.5 2.3 %collective-permute-start.14 = (bf16[1,224,128]{2,1,0:T(8,128)(2,1)S(1)}, bf16[1,224,128]{2,1,0:T(8,128)(2,1)S(1)}, u32[]{:S(2)}, u32[]{:S(2)}) collective-permute-start(bf16[1,224,128]{2,1,0:T(8,128)(2,1)S(1)} %get-tuple-element.54), channel_id=1, source_target_pairs={{0,6},{1,7},{2,4},{3,5},{4,2},{5,3},{6,0},{7,1},{8,14},{9,15},{10,... | collective-permute-start | bytes 172040 | tf_op jit(solution)/shard_map/ppermute | solution.py:356
  38.9 2.8 %collective-permute-start.16 = (bf16[1,224,128]{2,1,0:T(8,128)(2,1)S(1)}, bf16[1,224,128]{2,1,0:T(8,128)(2,1)S(1)}, u32[]{:S(2)}, u32[]{:S(2)}) collective-permute-start(bf16[1,224,128]{2,1,0:T(8,128)(2,1)S(1)} %get-tuple-element.56), channel_id=1, source_target_pairs={{0,3},{1,5},{2,6},{3,0},{4,7},{5,1},{6,2},{7,4},{8,11},{9,13},{10,... | collective-permute-start | bytes 172040 | tf_op jit(solution)/shard_map/ppermute | solution.py:356
  41.7 0.6 %collective-permute-start.17 = (bf16[1,224,128]{2,1,0:T(8,128)(2,1)S(1)}, bf16[1,224,128]{2,1,0:T(8,128)(2,1)S(1)}, u32[]{:S(2)}, u32[]{:S(2)}) collective-permute-start(bf16[1,224,128]{2,1,0:T(8,128)(2,1)S(1)} %get-tuple-element.57), channel_id=1, source_target_pairs={{0,5},{1,3},{2,7},{3,1},{4,6},{5,0},{6,4},{7,2},{8,13},{9,11},{10,... | collective-permute-start | bytes 172040 | tf_op jit(solution)/shard_map/ppermute | solution.py:356
  42.4 1.1 %collective-permute-start.18 = (bf16[1,224,128]{2,1,0:T(8,128)(2,1)S(1)}, bf16[1,224,128]{2,1,0:T(8,128)(2,1)S(1)}, u32[]{:S(2)}, u32[]{:S(2)}) collective-permute-start(bf16[1,224,128]{2,1,0:T(8,128)(2,1)S(1)} %get-tuple-element.58), channel_id=1, source_target_pairs={{0,2},{1,4},{2,0},{3,6},{4,1},{5,7},{6,3},{7,5},{8,10},{9,12},{10,... | collective-permute-start | bytes 172040 | tf_op jit(solution)/shard_map/ppermute | solution.py:356
  43.5 1.3 %collective-permute-start.19 = (bf16[1,224,128]{2,1,0:T(8,128)(2,1)S(1)}, bf16[1,224,128]{2,1,0:T(8,128)(2,1)S(1)}, u32[]{:S(2)}, u32[]{:S(2)}) collective-permute-start(bf16[1,224,128]{2,1,0:T(8,128)(2,1)S(1)} %get-tuple-element.59), channel_id=1, source_target_pairs={{0,1},{1,0},{2,3},{3,2},{4,5},{5,4},{6,7},{7,6},{8,9},{9,8},{10,11... | collective-permute-start | bytes 172040 | tf_op jit(solution)/shard_map/ppermute | solution.py:356
  44.8 2.4 %collective-permute-done.15.rest_2_ = bf16[1,224,128]{2,1,0:T(8,128)(2,1)S(1)} collective-permute-done((bf16[1,224,128]{2,1,0:T(8,128)(2,1)S(1)}, bf16[1,224,128]{2,1,0:T(8,128)(2,1)S(1)}, u32[]{:S(2)}, u32[]{:S(2)}) %collective-permute-start.15) | collective-permute-done | bytes 57376 | tf_op jit(solution)/shard_map/ppermute | solution.py:356
  47.2 1.8 %collective-permute-done.17.rest_4_ = bf16[1,224,128]{2,1,0:T(8,128)(2,1)S(1)} collective-permute-done((bf16[1,224,128]{2,1,0:T(8,128)(2,1)S(1)}, bf16[1,224,128]{2,1,0:T(8,128)(2,1)S(1)}, u32[]{:S(2)}, u32[]{:S(2)}) %collective-permute-start.17) | collective-permute-done | bytes 57376 | tf_op jit(solution)/shard_map/ppermute | solution.py:356
  49.1 2.1 %result.1 = bf16[2,512,128]{2,1,0:T(8,128)(2,1)} custom-call(s32[1,64]{1,0:T(1,128)S(1)} %get-tuple-element.35.ranks_near, bf16[2,2,8,2,2,48,256]{6,5,4,3,2,1,0:T(8,128)(2,1)S(1)} %bitcast.4, bf16[1,224,128]{2,1,0:T(8,128)(2,1)S(1)} %collective-permute-done.13.rest_0_, bf16[1,224,128]{2,1,0:T(8,128)(2,1)S(1)} %collective-permute-done.14.rest_1_, ...), custom_call_target="tpu_custom_call" | custom-call | flops 805306368 | bytes 3145728 | tf_op jit(solution)/shard_map/result/pallas_call | solution.py:28
  (27 shorter events, 0.6 us)
Async XLA Ops:
  0.0 14.8 %copy-start.2 = (f32[16,4096]{1,0:T(8,128)S(1)}, f32[16,4096]{1,0:T(8,128)}, u32[]{:S(2)}) copy-start(f32[16,4096]{1,0:T(8,128)} %constant.7.clone.choice) | copy-start | bytes 786436
  0.0 14.8 %copy-start.3 = (s32[64,64]{1,0:T(8,128)S(1)}, s32[64,64]{1,0:T(8,128)}, u32[]{:S(2)}) copy-start(s32[64,64]{1,0:T(8,128)} %mask.1) | copy-start | bytes 49156
  0.0 14.8 %copy-start.4 = (f32[64,128]{1,0:T(8,128)S(1)}, f32[64,128]{1,0:T(8,128)}, u32[]{:S(2)}) copy-start(f32[64,128]{1,0:T(8,128)} %constant.6.clone.table) | copy-start | bytes 98308
  0.0 14.8 %copy-start.5 = (f32[16,256]{1,0:T(8,128)S(1)}, f32[16,256]{1,0:T(8,128)}, u32[]{:S(2)}) copy-start(f32[16,256]{1,0:T(8,128)} %constant.8.clone.same) | copy-start | bytes 49156
  0.0 19.1 %copy-start.1 = (bf16[2,16,2,2,48,256]{5,4,3,2,1,0:T(8,128)(2,1)S(1)}, bf16[2,16,2,2,48,256]{5,4,3,2,1,0:T(8,128)(2,1)}, u32[]{:S(2)}) copy-start(bf16[2,16,2,2,48,256]{5,4,3,2,1,0:T(8,128)(2,1)} %param.10) | copy-start | bytes 9437188
  2.0 11.6 %collective-permute-start = (bf16[1,224,128]{2,1,0:T(8,128)(2,1)S(1)}, bf16[1,224,128]{2,1,0:T(8,128)(2,1)S(1)}, u32[]{:S(2)}, u32[]{:S(2)}) collective-permute-start(bf16[1,224,128]{2,1,0:T(8,128)(2,1)S(1)} %get-tuple-element.38), channel_id=1, source_target_pairs={{0,7},{1,6},{2,5},{3,4},{4,3},{5,2},{6,1},{7,0},{8,15},{9,14},{10,... | collective-permute-start | bytes 172040 | tf_op jit(solution)/shard_map/ppermute | solution.py:356
  6.5 8.2 %collective-permute-start.1 = (bf16[1,224,128]{2,1,0:T(8,128)(2,1)S(1)}, bf16[1,224,128]{2,1,0:T(8,128)(2,1)S(1)}, u32[]{:S(2)}, u32[]{:S(2)}) collective-permute-start(bf16[1,224,128]{2,1,0:T(8,128)(2,1)S(1)} %get-tuple-element.39), channel_id=1, source_target_pairs={{0,6},{1,7},{2,4},{3,5},{4,2},{5,3},{6,0},{7,1},{8,14},{9,15},{10,... | collective-permute-start | bytes 172040 | tf_op jit(solution)/shard_map/ppermute | solution.py:356
  10.0 6.6 %collective-permute-start.2 = (bf16[1,224,128]{2,1,0:T(8,128)(2,1)S(1)}, bf16[1,224,128]{2,1,0:T(8,128)(2,1)S(1)}, u32[]{:S(2)}, u32[]{:S(2)}) collective-permute-start(bf16[1,224,128]{2,1,0:T(8,128)(2,1)S(1)} %get-tuple-element.40), channel_id=1, source_target_pairs={{0,4},{1,2},{2,1},{3,7},{4,0},{5,6},{6,5},{7,3},{8,12},{9,10},{10,... | collective-permute-start | bytes 172040 | tf_op jit(solution)/shard_map/ppermute | solution.py:356
  10.4 6.2 %collective-permute-start.3 = (bf16[1,224,128]{2,1,0:T(8,128)(2,1)S(1)}, bf16[1,224,128]{2,1,0:T(8,128)(2,1)S(1)}, u32[]{:S(2)}, u32[]{:S(2)}) collective-permute-start(bf16[1,224,128]{2,1,0:T(8,128)(2,1)S(1)} %get-tuple-element.41), channel_id=1, source_target_pairs={{0,3},{1,5},{2,6},{3,0},{4,7},{5,1},{6,2},{7,4},{8,11},{9,13},{10,... | collective-permute-start | bytes 172040 | tf_op jit(solution)/shard_map/ppermute | solution.py:356
  13.5 5.6 %collective-permute-start.4 = (bf16[1,224,128]{2,1,0:T(8,128)(2,1)S(1)}, bf16[1,224,128]{2,1,0:T(8,128)(2,1)S(1)}, u32[]{:S(2)}, u32[]{:S(2)}) collective-permute-start(bf16[1,224,128]{2,1,0:T(8,128)(2,1)S(1)} %get-tuple-element.42), channel_id=1, source_target_pairs={{0,5},{1,3},{2,7},{3,1},{4,6},{5,0},{6,4},{7,2},{8,13},{9,11},{10,... | collective-permute-start | bytes 172040 | tf_op jit(solution)/shard_map/ppermute | solution.py:356
  13.6 5.6 %collective-permute-start.5 = (bf16[1,224,128]{2,1,0:T(8,128)(2,1)S(1)}, bf16[1,224,128]{2,1,0:T(8,128)(2,1)S(1)}, u32[]{:S(2)}, u32[]{:S(2)}) collective-permute-start(bf16[1,224,128]{2,1,0:T(8,128)(2,1)S(1)} %get-tuple-element.43), channel_id=1, source_target_pairs={{0,2},{1,4},{2,0},{3,6},{4,1},{5,7},{6,3},{7,5},{8,10},{9,12},{10,... | collective-permute-start | bytes 172040 | tf_op jit(solution)/shard_map/ppermute | solution.py:356
  14.8 4.4 %collective-permute-start.6 = (bf16[1,224,128]{2,1,0:T(8,128)(2,1)S(1)}, bf16[1,224,128]{2,1,0:T(8,128)(2,1)S(1)}, u32[]{:S(2)}, u32[]{:S(2)}) collective-permute-start(bf16[1,224,128]{2,1,0:T(8,128)(2,1)S(1)} %get-tuple-element.44), channel_id=1, source_target_pairs={{0,1},{1,0},{2,3},{3,2},{4,5},{5,4},{6,7},{7,6},{8,9},{9,8},{10,11... | collective-permute-start | bytes 172040 | tf_op jit(solution)/shard_map/ppermute | solution.py:356
  19.2 29.9 %copy-start = (bf16[2,2,16,2,48,256]{5,4,3,2,1,0:T(8,128)(2,1)S(1)}, bf16[2,2,16,2,48,256]{5,4,3,2,1,0:T(8,128)(2,1)}, u32[]{:S(2)}) copy-start(bf16[2,2,16,2,48,256]{5,4,3,2,1,0:T(8,128)(2,1)} %param.9) | copy-start | bytes 9437188
  20.6 5.3 %collective-permute-start.7 = (bf16[2,32,512]{2,1,0:T(8,128)(2,1)S(1)}, bf16[2,32,512]{2,1,0:T(8,128)(2,1)S(1)}, u32[]{:S(2)}, u32[]{:S(2)}) collective-permute-start(bf16[2,32,512]{2,1,0:T(8,128)(2,1)S(1)} %get-tuple-element.45), channel_id=1, source_target_pairs={{0,24},{8,16},{16,8},{24,0},{1,25},{9,17},{17,9},{25,1},{2,26},{10... | collective-permute-start | bytes 196616 | tf_op jit(solution)/shard_map/ppermute | solution.py:356
  23.1 4.3 %collective-permute-start.8 = (bf16[2,32,512]{2,1,0:T(8,128)(2,1)S(1)}, bf16[2,32,512]{2,1,0:T(8,128)(2,1)S(1)}, u32[]{:S(2)}, u32[]{:S(2)}) collective-permute-start(bf16[2,32,512]{2,1,0:T(8,128)(2,1)S(1)} %get-tuple-element.46), channel_id=1, source_target_pairs={{0,16},{8,24},{16,0},{24,8},{1,17},{9,25},{17,1},{25,9},{2,18},{10... | collective-permute-start | bytes 196616 | tf_op jit(solution)/shard_map/ppermute | solution.py:356
  23.6 4.3 %collective-permute-start.9 = (bf16[2,32,512]{2,1,0:T(8,128)(2,1)S(1)}, bf16[2,32,512]{2,1,0:T(8,128)(2,1)S(1)}, u32[]{:S(2)}, u32[]{:S(2)}) collective-permute-start(bf16[2,32,512]{2,1,0:T(8,128)(2,1)S(1)} %get-tuple-element.47), channel_id=1, source_target_pairs={{0,8},{8,0},{16,24},{24,16},{1,9},{9,1},{17,25},{25,17},{2,10},{10... | collective-permute-start | bytes 196616 | tf_op jit(solution)/shard_map/ppermute | solution.py:356
  28.2 5.4 %collective-permute-start.10 = (bf16[2,32,512]{2,1,0:T(8,128)(2,1)S(1)}, bf16[2,32,512]{2,1,0:T(8,128)(2,1)S(1)}, u32[]{:S(2)}, u32[]{:S(2)}) collective-permute-start(bf16[2,32,512]{2,1,0:T(8,128)(2,1)S(1)} %get-tuple-element.49), channel_id=1, source_target_pairs={{0,24},{8,16},{16,8},{24,0},{1,25},{9,17},{17,9},{25,1},{2,26},{10... | collective-permute-start | bytes 196616 | tf_op jit(solution)/shard_map/ppermute | solution.py:356
  29.8 4.5 %collective-permute-start.11 = (bf16[2,32,512]{2,1,0:T(8,128)(2,1)S(1)}, bf16[2,32,512]{2,1,0:T(8,128)(2,1)S(1)}, u32[]{:S(2)}, u32[]{:S(2)}) collective-permute-start(bf16[2,32,512]{2,1,0:T(8,128)(2,1)S(1)} %get-tuple-element.50), channel_id=1, source_target_pairs={{0,16},{8,24},{16,0},{24,8},{1,17},{9,25},{17,1},{25,9},{2,18},{10... | collective-permute-start | bytes 196616 | tf_op jit(solution)/shard_map/ppermute | solution.py:356
  30.5 4.3 %collective-permute-start.12 = (bf16[2,32,512]{2,1,0:T(8,128)(2,1)S(1)}, bf16[2,32,512]{2,1,0:T(8,128)(2,1)S(1)}, u32[]{:S(2)}, u32[]{:S(2)}) collective-permute-start(bf16[2,32,512]{2,1,0:T(8,128)(2,1)S(1)} %get-tuple-element.51), channel_id=1, source_target_pairs={{0,8},{8,0},{16,24},{24,16},{1,9},{9,1},{17,25},{25,17},{2,10},{10... | collective-permute-start | bytes 196616 | tf_op jit(solution)/shard_map/ppermute | solution.py:356
  36.4 6.0 %collective-permute-start.13 = (bf16[1,224,128]{2,1,0:T(8,128)(2,1)S(1)}, bf16[1,224,128]{2,1,0:T(8,128)(2,1)S(1)}, u32[]{:S(2)}, u32[]{:S(2)}) collective-permute-start(bf16[1,224,128]{2,1,0:T(8,128)(2,1)S(1)} %get-tuple-element.53), channel_id=1, source_target_pairs={{0,7},{1,6},{2,5},{3,4},{4,3},{5,2},{6,1},{7,0},{8,15},{9,14},{10,... | collective-permute-start | bytes 172040 | tf_op jit(solution)/shard_map/ppermute | solution.py:356
  36.5 7.0 %collective-permute-start.14 = (bf16[1,224,128]{2,1,0:T(8,128)(2,1)S(1)}, bf16[1,224,128]{2,1,0:T(8,128)(2,1)S(1)}, u32[]{:S(2)}, u32[]{:S(2)}) collective-permute-start(bf16[1,224,128]{2,1,0:T(8,128)(2,1)S(1)} %get-tuple-element.54), channel_id=1, source_target_pairs={{0,6},{1,7},{2,4},{3,5},{4,2},{5,3},{6,0},{7,1},{8,14},{9,15},{10,... | collective-permute-start | bytes 172040 | tf_op jit(solution)/shard_map/ppermute | solution.py:356
  38.8 8.4 %collective-permute-start.15 = (bf16[1,224,128]{2,1,0:T(8,128)(2,1)S(1)}, bf16[1,224,128]{2,1,0:T(8,128)(2,1)S(1)}, u32[]{:S(2)}, u32[]{:S(2)}) collective-permute-start(bf16[1,224,128]{2,1,0:T(8,128)(2,1)S(1)} %get-tuple-element.55), channel_id=1, source_target_pairs={{0,4},{1,2},{2,1},{3,7},{4,0},{5,6},{6,5},{7,3},{8,12},{9,10},{10,... | collective-permute-start | bytes 172040 | tf_op jit(solution)/shard_map/ppermute | solution.py:356
  38.9 8.3 %collective-permute-start.16 = (bf16[1,224,128]{2,1,0:T(8,128)(2,1)S(1)}, bf16[1,224,128]{2,1,0:T(8,128)(2,1)S(1)}, u32[]{:S(2)}, u32[]{:S(2)}) collective-permute-start(bf16[1,224,128]{2,1,0:T(8,128)(2,1)S(1)} %get-tuple-element.56), channel_id=1, source_target_pairs={{0,3},{1,5},{2,6},{3,0},{4,7},{5,1},{6,2},{7,4},{8,11},{9,13},{10,... | collective-permute-start | bytes 172040 | tf_op jit(solution)/shard_map/ppermute | solution.py:356
  41.7 7.4 %collective-permute-start.17 = (bf16[1,224,128]{2,1,0:T(8,128)(2,1)S(1)}, bf16[1,224,128]{2,1,0:T(8,128)(2,1)S(1)}, u32[]{:S(2)}, u32[]{:S(2)}) collective-permute-start(bf16[1,224,128]{2,1,0:T(8,128)(2,1)S(1)} %get-tuple-element.57), channel_id=1, source_target_pairs={{0,5},{1,3},{2,7},{3,1},{4,6},{5,0},{6,4},{7,2},{8,13},{9,11},{10,... | collective-permute-start | bytes 172040 | tf_op jit(solution)/shard_map/ppermute | solution.py:356
  42.4 6.7 %collective-permute-start.18 = (bf16[1,224,128]{2,1,0:T(8,128)(2,1)S(1)}, bf16[1,224,128]{2,1,0:T(8,128)(2,1)S(1)}, u32[]{:S(2)}, u32[]{:S(2)}) collective-permute-start(bf16[1,224,128]{2,1,0:T(8,128)(2,1)S(1)} %get-tuple-element.58), channel_id=1, source_target_pairs={{0,2},{1,4},{2,0},{3,6},{4,1},{5,7},{6,3},{7,5},{8,10},{9,12},{10,... | collective-permute-start | bytes 172040 | tf_op jit(solution)/shard_map/ppermute | solution.py:356
  43.5 5.6 %collective-permute-start.19 = (bf16[1,224,128]{2,1,0:T(8,128)(2,1)S(1)}, bf16[1,224,128]{2,1,0:T(8,128)(2,1)S(1)}, u32[]{:S(2)}, u32[]{:S(2)}) collective-permute-start(bf16[1,224,128]{2,1,0:T(8,128)(2,1)S(1)} %get-tuple-element.59), channel_id=1, source_target_pairs={{0,1},{1,0},{2,3},{3,2},{4,5},{5,4},{6,7},{7,6},{8,9},{9,8},{10,11... | collective-permute-start | bytes 172040 | tf_op jit(solution)/shard_map/ppermute | solution.py:356
where the time goes:
time: 51.5 us; the launch traced here: 51.2 us
  starting transfers between devices  25.5 us (50%)
  waiting for transfers between devices  13.8 us (27%)
  Pallas kernels  11.8 us (23%)
    ppermute x20, starting transfers between devices, send(): lax.ppermute(value, axis, [(d, partner(d, slot)) for d in range(lax.axis_...  25.5 us
    ppermute x20, waiting for transfers between devices, send(): lax.ppermute(value, axis, [(d, partner(d, slot)) for d in range(lax.axis_...  13.8 us
    pallas_call x7, Pallas kernels, call(): pl.pallas_call(kernel, in_specs=[spec for spec, _ in ins], out_specs=spec...  11.8 us
  transfers between devices with their start and end apart: 20, of which 10 were waited for; matrix products, arithmetic and copies ran while one was open for 0% of the time, Pallas kernels for 9%

commit v1 on v0

--- a/solution.py
+++ b/solution.py
@@ -133,6 +133,16 @@
     if even == odd:
         return me ^ even
     return me ^ (even ^ (parity(me, mask) * (even ^ odd)))
+
+
+def owner_slots(owners):
+    mixed = [(1, 2), (2, 1)] if owners > 2 else [(n, n) for n in range(1, owners)]
+    return [(n, n) for n in reversed(range(3, owners))] + mixed + [(0, 0)]
+
+
+def owner(mine, me, slot):
+    even, odd = slot
+    return mine ^ even if even == odd else mine ^ (even ^ ((me & 1) * (even ^ odd)))
 
 
 def unstage(outs, slots_out, stage, m, devices, span, size, me):
@@ -227,8 +237,8 @@
                 f = 2 * m + n
                 both = side_by_side(basis[f, :, :, c, 0], basis[f, :, :, c, 1])
                 z[f, :, pl.ds(c * tile, tile)] = plain_product(coeffs[c, n], both)
-    for r in range(owners):
-        low = pl.multiple_of((mine ^ r) * quarter, quarter)
+    for r, slot in enumerate(owner_slots(owners)):
+        low = pl.multiple_of(owner(mine, me, slot) * quarter, quarter)
         for f in range(freqs):
             real = z[f, pl.ds(low, quarter), :]
             imag = z[f, pl.ds(half + low, quarter), :]
@@ -266,23 +276,24 @@
 
 
 def mix_kernel(owners, high, low, *rest):
-    arrived = rest[:owners][::-1]
+    arrived = rest[:owners]
     outs = rest[owners : 2 * owners]
     z, w = rest[2 * owners :]
     freqs, rows, span = arrived[0].shape
-    mine = lax.axis_index("freq")
+    me, mine = lax.axis_index("tile"), lax.axis_index("freq")
     size = freqs * rows
+    places = [pl.multiple_of(owner(mine, me, slot) * size, 16) for slot in owner_slots(owners)]
     for r in range(owners):
-        z[pl.ds(pl.multiple_of((mine ^ r) * size, 16), size), :] = arrived[r][...].reshape(size, span)
+        z[pl.ds(places[r], size), :] = arrived[r][...].reshape(size, span)
     w[...] = dot(high[...], z[...], 1, 0) + dot(low[...], z[...], 1, 0)
     for r in range(owners):
-        block = w[pl.ds(pl.multiple_of((mine ^ r) * size, 16), size), :]
+        block = w[pl.ds(places[r], size), :]
         outs[r][...] = block.reshape(freqs, rows, span).astype(bf16)
 
 
 def forward_kernel(slots_out, owners, ranks_near, basis, *rest):
     devices = len(slots_out)
-    arrived = rest[:owners][::-1]
+    arrived = rest[:owners]
     outs = rest[owners : owners + devices]
     ranks, w, stage, sem = rest[owners + devices :]
     freqs, _, rows, cols, _, slots, tile = basis.shape
@@ -292,8 +303,8 @@
     me, mine = lax.axis_index("tile"), lax.axis_index("freq")
     rank_copy = pltpu.make_async_copy(ranks_near, ranks, sem)
     rank_copy.start()
-    for r in range(owners):
-        low = pl.multiple_of((mine ^ r) * quarter, quarter)
+    for r, slot in enumerate(owner_slots(owners)):
+        low = pl.multiple_of(owner(mine, me, slot) * quarter, quarter)
         for f in range(freqs):
             for c in range(cols):
                 at = slice(c * tile, (c + 1) * tile)
@@ -361,7 +372,18 @@
 
 
 def to_owners(values):
-    return spread(values[::-1], "freq", [(n, n, 1) for n in reversed(range(len(values)))])
+    owners, devices = lax.axis_size("freq"), lax.axis_size("tile")
+    landed = []
+    for value, slot in zip(values, owner_slots(owners)):
+        if slot != (0, 0):
+            pairs = [
+                (mine * devices + me, owner(mine, me, slot) * devices + me)
+                for mine in range(owners)
+                for me in range(devices)
+            ]
+            value = lax.ppermute(value, ("freq", "tile"), pairs)
+        landed.append((whole, value))
+    return landed
 
 
 def local(u_data, u_basis, v_basis, ranks, time_mask):

time: 51.5 us -> 51.6 us (level)
    ppermute x0 -> x6, starting transfers between devices: none -> 7.11 us  [to_owners(): value = lax.ppermute(value, ('freq', 'tile'), pairs)]
    ppermute x20 -> x14, waiting for transfers between devices: 13.8 us -> 6.72 us  [send(): lax.ppermute(value, axis, [(d, partner(d, slot)) for d in range(lax.axis_...]
    ppermute x0 -> x6, waiting for transfers between devices: none -> 6.72 us  [to_owners(): value = lax.ppermute(value, ('freq', 'tile'), pairs)]
    ppermute x20 -> x14, starting transfers between devices: 25.5 us -> 18.8 us  [send(): lax.ppermute(value, axis, [(d, partner(d, slot)) for d in range(lax.axis_...]
where the time goes in v1:
time: 51.6 us; the launch traced here: 51.3 us
  starting transfers between devices  25.9 us (50%)
  waiting for transfers between devices  13.4 us (26%)
  Pallas kernels  11.8 us (23%)
    ppermute x14, starting transfers between devices, send(): lax.ppermute(value, axis, [(d, partner(d, slot)) for d in range(lax.axis_...  18.8 us
    pallas_call x7, Pallas kernels, call(): pl.pallas_call(kernel, in_specs=[spec for spec, _ in ins], out_specs=spec...  11.8 us
    ppermute x6, starting transfers between devices, to_owners(): value = lax.ppermute(value, ('freq', 'tile'), pairs)  7.11 us
    ppermute x14, waiting for transfers between devices, send(): lax.ppermute(value, axis, [(d, partner(d, slot)) for d in range(lax.axis_...  6.72 us
    ppermute x6, waiting for transfers between devices, to_owners(): value = lax.ppermute(value, ('freq', 'tile'), pairs)  6.72 us
  transfers between devices with their start and end apart: 20, of which 10 were waited for; matrix products, arithmetic and copies ran while one was open for 0% of the time, Pallas kernels for 9%

profile of v1, /device:TPU:0, one launch (start us, length us, event | category | flops | bytes accessed | tf_op | source)
XLA Modules:
  0.0 51.3 jit_solution(9837562290675682758)
XLA Ops:
  0.0 1.9 %adjoint.2 = (bf16[1,224,128]{2,1,0:T(8,128)(2,1)S(1)}, bf16[1,224,128]{2,1,0:T(8,128)(2,1)S(1)}, bf16[2,2,512,128]{3,2,1,0:T(8,128)(2,1)S(1)}) custom-call(s32[2,16,16]{2,1,0:T(8,128)} %ranks_far.5, bf16[2,2,8,2,2,48,256]{6,5,4,3,2,1,0:T(8,128)(2,1)} %bitcast.2, bf16[2,512,128]{2,1,0:T(8,128)(2,1)} %u_far.1), custom_call_target="tpu_custom_call" | custom-call | flops 201326592 | bytes 786432 | tf_op jit(solution)/shard_map/adjoint/pallas_call | solution.py:28
  2.0 4.6 %collective-permute-start = (bf16[1,224,128]{2,1,0:T(8,128)(2,1)S(1)}, bf16[1,224,128]{2,1,0:T(8,128)(2,1)S(1)}, u32[]{:S(2)}, u32[]{:S(2)}) collective-permute-start(bf16[1,224,128]{2,1,0:T(8,128)(2,1)S(1)} %get-tuple-element.38), channel_id=1, source_target_pairs={{0,7},{1,6},{2,5},{3,4},{4,3},{5,2},{6,1},{7,0},{8,15},{9,14},{10,... | collective-permute-start | bytes 172040 | tf_op jit(solution)/shard_map/ppermute | solution.py:367
  6.5 0.6 %collective-permute-start.1 = (bf16[1,224,128]{2,1,0:T(8,128)(2,1)S(1)}, bf16[1,224,128]{2,1,0:T(8,128)(2,1)S(1)}, u32[]{:S(2)}, u32[]{:S(2)}) collective-permute-start(bf16[1,224,128]{2,1,0:T(8,128)(2,1)S(1)} %get-tuple-element.39), channel_id=1, source_target_pairs={{0,6},{1,7},{2,4},{3,5},{4,2},{5,3},{6,0},{7,1},{8,14},{9,15},{10,... | collective-permute-start | bytes 172040 | tf_op jit(solution)/shard_map/ppermute | solution.py:367
  7.2 2.8 %adjoint.3 = (bf16[1,224,128]{2,1,0:T(8,128)(2,1)S(1)}, bf16[1,224,128]{2,1,0:T(8,128)(2,1)S(1)}, bf16[1,224,128]{2,1,0:T(8,128)(2,1)S(1)}, bf16[1,224,128]{2,1,...) custom-call(s32[2,16,16]{2,1,0:T(8,128)} %ranks_far.5, ...), custom_call_target="tpu_custom_call" | custom-call | flops 603979776 | bytes 2359296 | tf_op jit(solution)/shard_map/adjoint/pallas_call | solution.py:28
  10.0 0.4 collective-permute-start.2
  10.4 3.1 %collective-permute-start.3 = (bf16[1,224,128]{2,1,0:T(8,128)(2,1)S(1)}, bf16[1,224,128]{2,1,0:T(8,128)(2,1)S(1)}, u32[]{:S(2)}, u32[]{:S(2)}) collective-permute-start(bf16[1,224,128]{2,1,0:T(8,128)(2,1)S(1)} %get-tuple-element.41), channel_id=1, source_target_pairs={{0,3},{1,5},{2,6},{3,0},{4,7},{5,1},{6,2},{7,4},{8,11},{9,13},{10,... | collective-permute-start | bytes 172040 | tf_op jit(solution)/shard_map/ppermute | solution.py:367
  13.6 1.2 %collective-permute-start.5 = (bf16[1,224,128]{2,1,0:T(8,128)(2,1)S(1)}, bf16[1,224,128]{2,1,0:T(8,128)(2,1)S(1)}, u32[]{:S(2)}, u32[]{:S(2)}) collective-permute-start(bf16[1,224,128]{2,1,0:T(8,128)(2,1)S(1)} %get-tuple-element.43), channel_id=1, source_target_pairs={{0,2},{1,4},{2,0},{3,6},{4,1},{5,7},{6,3},{7,5},{8,10},{9,12},{10,... | collective-permute-start | bytes 172040 | tf_op jit(solution)/shard_map/ppermute | solution.py:367
  14.8 1.6 %prepare.1 = (s32[1,64]{1,0:T(1,128)S(1)}, bf16[256,256]{1,0:T(8,128)(2,1)S(1)}, bf16[256,256]{1,0:T(8,128)(2,1)S(1)}) custom-call(s32[2,16,16]{2,1,0:T(8,128)} %ranks_far.5, s32[64,64]{1,0:T(8,128)S(1)} %copy-done.3, f32[64,128]{1,0:T(8,128)S(1)} %copy-done.4, f32[16,4096]{1,0:T(8,128)S(1)} %copy-done.2, f32[16,256]{1,0:T(8,128)S(1)} %copy-done.5, ...), custom_call_target="tpu_custom_call" | custom-call | flops 6291456 | tf_op jit(solution)/shard_map/prepare/pallas_call | solution.py:28
  16.6 2.5 %collective-permute-done.4.rest_4_ = bf16[1,224,128]{2,1,0:T(8,128)(2,1)S(1)} collective-permute-done((bf16[1,224,128]{2,1,0:T(8,128)(2,1)S(1)}, bf16[1,224,128]{2,1,0:T(8,128)(2,1)S(1)}, u32[]{:S(2)}, u32[]{:S(2)}) %collective-permute-start.4) | collective-permute-done | bytes 57376 | tf_op jit(solution)/shard_map/ppermute | solution.py:367
  19.2 1.4 %image.1 = (bf16[2,32,512]{2,1,0:T(8,128)(2,1)S(1)}, bf16[2,32,512]{2,1,0:T(8,128)(2,1)S(1)}, bf16[2,32,512]{2,1,0:T(8,128)(2,1)S(1)}, bf16[2,32,512]{2,1,0:T(8,128)(2,1)S(1)}) custom-call(s32[1,64]{1,0:T(1,128)S(1)} %get-tuple-element.35.ranks_near, bf16[2,8,2,2,2,48,256]{6,5,4,3,2,1,0:T(8,128)(2,1)S(1)} %bitcast.5, ...), custom_call_target="tpu_custom_call" | custom-call | flops 805306368 | bytes 3145728 | tf_op jit(solution)/shard_map/image/pallas_call | solution.py:28
  20.6 2.5 %collective-permute-start.7 = (bf16[2,32,512]{2,1,0:T(8,128)(2,1)S(1)}, bf16[2,32,512]{2,1,0:T(8,128)(2,1)S(1)}, u32[]{:S(2)}, u32[]{:S(2)}) collective-permute-start(bf16[2,32,512]{2,1,0:T(8,128)(2,1)S(1)} %get-tuple-element.45), channel_id=1, source_target_pairs={{0,24},{1,25},{2,26},{3,27},{4,28},{5,29},{6,30},{7,31},{8,16},{9,... | collective-permute-start | bytes 196616 | tf_op jit(solution)/shard_map/ppermute | solution.py:384
  23.1 0.5 %collective-permute-start.8 = (bf16[2,32,512]{2,1,0:T(8,128)(2,1)S(1)}, bf16[2,32,512]{2,1,0:T(8,128)(2,1)S(1)}, u32[]{:S(2)}, u32[]{:S(2)}) collective-permute-start(bf16[2,32,512]{2,1,0:T(8,128)(2,1)S(1)} %get-tuple-element.46), channel_id=1, source_target_pairs={{0,8},{1,17},{2,10},{3,19},{4,12},{5,21},{6,14},{7,23},{8,0},{9,25... | collective-permute-start | bytes 196616 | tf_op jit(solution)/shard_map/ppermute | solution.py:384
  23.6 0.5 collective-permute-start.9
  24.1 1.7 %collective-permute-done.7.rest_0_ = bf16[2,32,512]{2,1,0:T(8,128)(2,1)S(1)} collective-permute-done((bf16[2,32,512]{2,1,0:T(8,128)(2,1)S(1)}, bf16[2,32,512]{2,1,0:T(8,128)(2,1)S(1)}, u32[]{:S(2)}, u32[]{:S(2)}) %collective-permute-start.7) | collective-permute-done | bytes 65568 | tf_op jit(solution)/shard_map/ppermute | solution.py:384
  25.8 1.5 %collective-permute-done.8.rest_1_ = bf16[2,32,512]{2,1,0:T(8,128)(2,1)S(1)} collective-permute-done((bf16[2,32,512]{2,1,0:T(8,128)(2,1)S(1)}, bf16[2,32,512]{2,1,0:T(8,128)(2,1)S(1)}, u32[]{:S(2)}, u32[]{:S(2)}) %collective-permute-start.8) | collective-permute-done | bytes 65568 | tf_op jit(solution)/shard_map/ppermute | solution.py:384
  27.3 0.5 %collective-permute-done.9.rest_2_ = bf16[2,32,512]{2,1,0:T(8,128)(2,1)S(1)} collective-permute-done((bf16[2,32,512]{2,1,0:T(8,128)(2,1)S(1)}, bf16[2,32,512]{2,1,0:T(8,128)(2,1)S(1)}, u32[]{:S(2)}, u32[]{:S(2)}) %collective-permute-start.9) | collective-permute-done | bytes 65568 | tf_op jit(solution)/shard_map/ppermute | solution.py:384
  27.9 0.4 mix.1
  28.3 1.7 %collective-permute-start.10 = (bf16[2,32,512]{2,1,0:T(8,128)(2,1)S(1)}, bf16[2,32,512]{2,1,0:T(8,128)(2,1)S(1)}, u32[]{:S(2)}, u32[]{:S(2)}) collective-permute-start(bf16[2,32,512]{2,1,0:T(8,128)(2,1)S(1)} %get-tuple-element.49), channel_id=1, source_target_pairs={{0,24},{1,25},{2,26},{3,27},{4,28},{5,29},{6,30},{7,31},{8,16},{9,... | collective-permute-start | bytes 196616 | tf_op jit(solution)/shard_map/ppermute | solution.py:384
  29.9 0.6 %collective-permute-start.11 = (bf16[2,32,512]{2,1,0:T(8,128)(2,1)S(1)}, bf16[2,32,512]{2,1,0:T(8,128)(2,1)S(1)}, u32[]{:S(2)}, u32[]{:S(2)}) collective-permute-start(bf16[2,32,512]{2,1,0:T(8,128)(2,1)S(1)} %get-tuple-element.50), channel_id=1, source_target_pairs={{0,8},{1,17},{2,10},{3,19},{4,12},{5,21},{6,14},{7,23},{8,0},{9,25... | collective-permute-start | bytes 196616 | tf_op jit(solution)/shard_map/ppermute | solution.py:384
  30.5 1.3 %collective-permute-start.12 = (bf16[2,32,512]{2,1,0:T(8,128)(2,1)S(1)}, bf16[2,32,512]{2,1,0:T(8,128)(2,1)S(1)}, u32[]{:S(2)}, u32[]{:S(2)}) collective-permute-start(bf16[2,32,512]{2,1,0:T(8,128)(2,1)S(1)} %get-tuple-element.51), channel_id=1, source_target_pairs={{0,16},{1,9},{2,18},{3,11},{4,20},{5,13},{6,22},{7,15},{8,24},{9,1... | collective-permute-start | bytes 196616 | tf_op jit(solution)/shard_map/ppermute | solution.py:384
  31.8 2.3 %collective-permute-done.10.rest_0_ = bf16[2,32,512]{2,1,0:T(8,128)(2,1)S(1)} collective-permute-done((bf16[2,32,512]{2,1,0:T(8,128)(2,1)S(1)}, bf16[2,32,512]{2,1,0:T(8,128)(2,1)S(1)}, u32[]{:S(2)}, u32[]{:S(2)}) %collective-permute-start.10) | collective-permute-done | bytes 65568 | tf_op jit(solution)/shard_map/ppermute | solution.py:384
  34.2 0.6 %collective-permute-done.12.rest_2_ = bf16[2,32,512]{2,1,0:T(8,128)(2,1)S(1)} collective-permute-done((bf16[2,32,512]{2,1,0:T(8,128)(2,1)S(1)}, bf16[2,32,512]{2,1,0:T(8,128)(2,1)S(1)}, u32[]{:S(2)}, u32[]{:S(2)}) %collective-permute-start.12) | collective-permute-done | bytes 65568 | tf_op jit(solution)/shard_map/ppermute | solution.py:384
  34.8 1.6 %forward.1 = (bf16[1,224,128]{2,1,0:T(8,128)(2,1)S(1)}, bf16[1,224,128]{2,1,0:T(8,128)(2,1)S(1)}, bf16[1,224,128]{2,1,0:T(8,128)(2,1)S(1)}, bf16[1,224,128]{2,1,...) custom-call(s32[1,64]{1,0:T(1,128)S(1)} %get-tuple-element.35.ranks_, ...), custom_call_target="tpu_custom_call" | custom-call | flops 805306368 | bytes 3145728 | tf_op jit(solution)/shard_map/forward/pallas_call | solution.py:28
  36.4 1.8 %collective-permute-start.14 = (bf16[1,224,128]{2,1,0:T(8,128)(2,1)S(1)}, bf16[1,224,128]{2,1,0:T(8,128)(2,1)S(1)}, u32[]{:S(2)}, u32[]{:S(2)}) collective-permute-start(bf16[1,224,128]{2,1,0:T(8,128)(2,1)S(1)} %get-tuple-element.54), channel_id=1, source_target_pairs={{0,6},{1,7},{2,4},{3,5},{4,2},{5,3},{6,0},{7,1},{8,14},{9,15},{10,... | collective-permute-start | bytes 172040 | tf_op jit(solution)/shard_map/ppermute | solution.py:367
  38.2 0.7 %collective-permute-start.15 = (bf16[1,224,128]{2,1,0:T(8,128)(2,1)S(1)}, bf16[1,224,128]{2,1,0:T(8,128)(2,1)S(1)}, u32[]{:S(2)}, u32[]{:S(2)}) collective-permute-start(bf16[1,224,128]{2,1,0:T(8,128)(2,1)S(1)} %get-tuple-element.55), channel_id=1, source_target_pairs={{0,4},{1,2},{2,1},{3,7},{4,0},{5,6},{6,5},{7,3},{8,12},{9,10},{10,... | collective-permute-start | bytes 172040 | tf_op jit(solution)/shard_map/ppermute | solution.py:367
  39.0 2.7 %collective-permute-start.16 = (bf16[1,224,128]{2,1,0:T(8,128)(2,1)S(1)}, bf16[1,224,128]{2,1,0:T(8,128)(2,1)S(1)}, u32[]{:S(2)}, u32[]{:S(2)}) collective-permute-start(bf16[1,224,128]{2,1,0:T(8,128)(2,1)S(1)} %get-tuple-element.56), channel_id=1, source_target_pairs={{0,3},{1,5},{2,6},{3,0},{4,7},{5,1},{6,2},{7,4},{8,11},{9,13},{10,... | collective-permute-start | bytes 172040 | tf_op jit(solution)/shard_map/ppermute | solution.py:367
  41.7 0.6 %collective-permute-start.17 = (bf16[1,224,128]{2,1,0:T(8,128)(2,1)S(1)}, bf16[1,224,128]{2,1,0:T(8,128)(2,1)S(1)}, u32[]{:S(2)}, u32[]{:S(2)}) collective-permute-start(bf16[1,224,128]{2,1,0:T(8,128)(2,1)S(1)} %get-tuple-element.57), channel_id=1, source_target_pairs={{0,5},{1,3},{2,7},{3,1},{4,6},{5,0},{6,4},{7,2},{8,13},{9,11},{10,... | collective-permute-start | bytes 172040 | tf_op jit(solution)/shard_map/ppermute | solution.py:367
  42.3 1.3 %collective-permute-start.18 = (bf16[1,224,128]{2,1,0:T(8,128)(2,1)S(1)}, bf16[1,224,128]{2,1,0:T(8,128)(2,1)S(1)}, u32[]{:S(2)}, u32[]{:S(2)}) collective-permute-start(bf16[1,224,128]{2,1,0:T(8,128)(2,1)S(1)} %get-tuple-element.58), channel_id=1, source_target_pairs={{0,2},{1,4},{2,0},{3,6},{4,1},{5,7},{6,3},{7,5},{8,10},{9,12},{10,... | collective-permute-start | bytes 172040 | tf_op jit(solution)/shard_map/ppermute | solution.py:367
  43.6 1.5 %collective-permute-start.19 = (bf16[1,224,128]{2,1,0:T(8,128)(2,1)S(1)}, bf16[1,224,128]{2,1,0:T(8,128)(2,1)S(1)}, u32[]{:S(2)}, u32[]{:S(2)}) collective-permute-start(bf16[1,224,128]{2,1,0:T(8,128)(2,1)S(1)} %get-tuple-element.59), channel_id=1, source_target_pairs={{0,1},{1,0},{2,3},{3,2},{4,5},{5,4},{6,7},{7,6},{8,9},{9,8},{10,11... | collective-permute-start | bytes 172040 | tf_op jit(solution)/shard_map/ppermute | solution.py:367
  45.2 1.7 %collective-permute-done.15.rest_2_ = bf16[1,224,128]{2,1,0:T(8,128)(2,1)S(1)} collective-permute-done((bf16[1,224,128]{2,1,0:T(8,128)(2,1)S(1)}, bf16[1,224,128]{2,1,0:T(8,128)(2,1)S(1)}, u32[]{:S(2)}, u32[]{:S(2)}) %collective-permute-start.15) | collective-permute-done | bytes 57376 | tf_op jit(solution)/shard_map/ppermute | solution.py:367
  46.9 2.3 %collective-permute-done.17.rest_4_ = bf16[1,224,128]{2,1,0:T(8,128)(2,1)S(1)} collective-permute-done((bf16[1,224,128]{2,1,0:T(8,128)(2,1)S(1)}, bf16[1,224,128]{2,1,0:T(8,128)(2,1)S(1)}, u32[]{:S(2)}, u32[]{:S(2)}) %collective-permute-start.17) | collective-permute-done | bytes 57376 | tf_op jit(solution)/shard_map/ppermute | solution.py:367
  49.1 2.1 %result.1 = bf16[2,512,128]{2,1,0:T(8,128)(2,1)} custom-call(s32[1,64]{1,0:T(1,128)S(1)} %get-tuple-element.35.ranks_near, bf16[2,2,8,2,2,48,256]{6,5,4,3,2,1,0:T(8,128)(2,1)S(1)} %bitcast.4, bf16[1,224,128]{2,1,0:T(8,128)(2,1)S(1)} %collective-permute-done.13.rest_0_, bf16[1,224,128]{2,1,0:T(8,128)(2,1)S(1)} %collective-permute-done.14.rest_1_, ...), custom_call_target="tpu_custom_call" | custom-call | flops 805306368 | bytes 3145728 | tf_op jit(solution)/shard_map/result/pallas_call | solution.py:28
  (27 shorter events, 0.5 us)
Async XLA Ops:
  0.0 14.8 %copy-start.2 = (f32[16,4096]{1,0:T(8,128)S(1)}, f32[16,4096]{1,0:T(8,128)}, u32[]{:S(2)}) copy-start(f32[16,4096]{1,0:T(8,128)} %constant.7.clone.choice) | copy-start | bytes 786436
  0.0 14.8 %copy-start.3 = (s32[64,64]{1,0:T(8,128)S(1)}, s32[64,64]{1,0:T(8,128)}, u32[]{:S(2)}) copy-start(s32[64,64]{1,0:T(8,128)} %mask.1) | copy-start | bytes 49156
  0.0 14.8 %copy-start.4 = (f32[64,128]{1,0:T(8,128)S(1)}, f32[64,128]{1,0:T(8,128)}, u32[]{:S(2)}) copy-start(f32[64,128]{1,0:T(8,128)} %constant.6.clone.table) | copy-start | bytes 98308
  0.0 14.8 %copy-start.5 = (f32[16,256]{1,0:T(8,128)S(1)}, f32[16,256]{1,0:T(8,128)}, u32[]{:S(2)}) copy-start(f32[16,256]{1,0:T(8,128)} %constant.8.clone.same) | copy-start | bytes 49156
  0.0 19.1 %copy-start.1 = (bf16[2,16,2,2,48,256]{5,4,3,2,1,0:T(8,128)(2,1)S(1)}, bf16[2,16,2,2,48,256]{5,4,3,2,1,0:T(8,128)(2,1)}, u32[]{:S(2)}) copy-start(bf16[2,16,2,2,48,256]{5,4,3,2,1,0:T(8,128)(2,1)} %param.10) | copy-start | bytes 9437188
  2.0 11.6 %collective-permute-start = (bf16[1,224,128]{2,1,0:T(8,128)(2,1)S(1)}, bf16[1,224,128]{2,1,0:T(8,128)(2,1)S(1)}, u32[]{:S(2)}, u32[]{:S(2)}) collective-permute-start(bf16[1,224,128]{2,1,0:T(8,128)(2,1)S(1)} %get-tuple-element.38), channel_id=1, source_target_pairs={{0,7},{1,6},{2,5},{3,4},{4,3},{5,2},{6,1},{7,0},{8,15},{9,14},{10,... | collective-permute-start | bytes 172040 | tf_op jit(solution)/shard_map/ppermute | solution.py:367
  6.5 8.2 %collective-permute-start.1 = (bf16[1,224,128]{2,1,0:T(8,128)(2,1)S(1)}, bf16[1,224,128]{2,1,0:T(8,128)(2,1)S(1)}, u32[]{:S(2)}, u32[]{:S(2)}) collective-permute-start(bf16[1,224,128]{2,1,0:T(8,128)(2,1)S(1)} %get-tuple-element.39), channel_id=1, source_target_pairs={{0,6},{1,7},{2,4},{3,5},{4,2},{5,3},{6,0},{7,1},{8,14},{9,15},{10,... | collective-permute-start | bytes 172040 | tf_op jit(solution)/shard_map/ppermute | solution.py:367
  10.0 6.6 %collective-permute-start.2 = (bf16[1,224,128]{2,1,0:T(8,128)(2,1)S(1)}, bf16[1,224,128]{2,1,0:T(8,128)(2,1)S(1)}, u32[]{:S(2)}, u32[]{:S(2)}) collective-permute-start(bf16[1,224,128]{2,1,0:T(8,128)(2,1)S(1)} %get-tuple-element.40), channel_id=1, source_target_pairs={{0,4},{1,2},{2,1},{3,7},{4,0},{5,6},{6,5},{7,3},{8,12},{9,10},{10,... | collective-permute-start | bytes 172040 | tf_op jit(solution)/shard_map/ppermute | solution.py:367
  10.4 6.2 %collective-permute-start.3 = (bf16[1,224,128]{2,1,0:T(8,128)(2,1)S(1)}, bf16[1,224,128]{2,1,0:T(8,128)(2,1)S(1)}, u32[]{:S(2)}, u32[]{:S(2)}) collective-permute-start(bf16[1,224,128]{2,1,0:T(8,128)(2,1)S(1)} %get-tuple-element.41), channel_id=1, source_target_pairs={{0,3},{1,5},{2,6},{3,0},{4,7},{5,1},{6,2},{7,4},{8,11},{9,13},{10,... | collective-permute-start | bytes 172040 | tf_op jit(solution)/shard_map/ppermute | solution.py:367
  13.5 5.6 %collective-permute-start.4 = (bf16[1,224,128]{2,1,0:T(8,128)(2,1)S(1)}, bf16[1,224,128]{2,1,0:T(8,128)(2,1)S(1)}, u32[]{:S(2)}, u32[]{:S(2)}) collective-permute-start(bf16[1,224,128]{2,1,0:T(8,128)(2,1)S(1)} %get-tuple-element.42), channel_id=1, source_target_pairs={{0,5},{1,3},{2,7},{3,1},{4,6},{5,0},{6,4},{7,2},{8,13},{9,11},{10,... | collective-permute-start | bytes 172040 | tf_op jit(solution)/shard_map/ppermute | solution.py:367
  13.6 5.6 %collective-permute-start.5 = (bf16[1,224,128]{2,1,0:T(8,128)(2,1)S(1)}, bf16[1,224,128]{2,1,0:T(8,128)(2,1)S(1)}, u32[]{:S(2)}, u32[]{:S(2)}) collective-permute-start(bf16[1,224,128]{2,1,0:T(8,128)(2,1)S(1)} %get-tuple-element.43), channel_id=1, source_target_pairs={{0,2},{1,4},{2,0},{3,6},{4,1},{5,7},{6,3},{7,5},{8,10},{9,12},{10,... | collective-permute-start | bytes 172040 | tf_op jit(solution)/shard_map/ppermute | solution.py:367
  14.8 4.4 %collective-permute-start.6 = (bf16[1,224,128]{2,1,0:T(8,128)(2,1)S(1)}, bf16[1,224,128]{2,1,0:T(8,128)(2,1)S(1)}, u32[]{:S(2)}, u32[]{:S(2)}) collective-permute-start(bf16[1,224,128]{2,1,0:T(8,128)(2,1)S(1)} %get-tuple-element.44), channel_id=1, source_target_pairs={{0,1},{1,0},{2,3},{3,2},{4,5},{5,4},{6,7},{7,6},{8,9},{9,8},{10,11... | collective-permute-start | bytes 172040 | tf_op jit(solution)/shard_map/ppermute | solution.py:367
  19.2 30.0 %copy-start = (bf16[2,2,16,2,48,256]{5,4,3,2,1,0:T(8,128)(2,1)S(1)}, bf16[2,2,16,2,48,256]{5,4,3,2,1,0:T(8,128)(2,1)}, u32[]{:S(2)}) copy-start(bf16[2,2,16,2,48,256]{5,4,3,2,1,0:T(8,128)(2,1)} %param.9) | copy-start | bytes 9437188
  20.6 5.3 %collective-permute-start.7 = (bf16[2,32,512]{2,1,0:T(8,128)(2,1)S(1)}, bf16[2,32,512]{2,1,0:T(8,128)(2,1)S(1)}, u32[]{:S(2)}, u32[]{:S(2)}) collective-permute-start(bf16[2,32,512]{2,1,0:T(8,128)(2,1)S(1)} %get-tuple-element.45), channel_id=1, source_target_pairs={{0,24},{1,25},{2,26},{3,27},{4,28},{5,29},{6,30},{7,31},{8,16},{9,... | collective-permute-start | bytes 196616 | tf_op jit(solution)/shard_map/ppermute | solution.py:384
  23.1 4.3 %collective-permute-start.8 = (bf16[2,32,512]{2,1,0:T(8,128)(2,1)S(1)}, bf16[2,32,512]{2,1,0:T(8,128)(2,1)S(1)}, u32[]{:S(2)}, u32[]{:S(2)}) collective-permute-start(bf16[2,32,512]{2,1,0:T(8,128)(2,1)S(1)} %get-tuple-element.46), channel_id=1, source_target_pairs={{0,8},{1,17},{2,10},{3,19},{4,12},{5,21},{6,14},{7,23},{8,0},{9,25... | collective-permute-start | bytes 196616 | tf_op jit(solution)/shard_map/ppermute | solution.py:384
  23.6 4.3 %collective-permute-start.9 = (bf16[2,32,512]{2,1,0:T(8,128)(2,1)S(1)}, bf16[2,32,512]{2,1,0:T(8,128)(2,1)S(1)}, u32[]{:S(2)}, u32[]{:S(2)}) collective-permute-start(bf16[2,32,512]{2,1,0:T(8,128)(2,1)S(1)} %get-tuple-element.47), channel_id=1, source_target_pairs={{0,16},{1,9},{2,18},{3,11},{4,20},{5,13},{6,22},{7,15},{8,24},{9,1... | collective-permute-start | bytes 196616 | tf_op jit(solution)/shard_map/ppermute | solution.py:384
  28.3 5.8 %collective-permute-start.10 = (bf16[2,32,512]{2,1,0:T(8,128)(2,1)S(1)}, bf16[2,32,512]{2,1,0:T(8,128)(2,1)S(1)}, u32[]{:S(2)}, u32[]{:S(2)}) collective-permute-start(bf16[2,32,512]{2,1,0:T(8,128)(2,1)S(1)} %get-tuple-element.49), channel_id=1, source_target_pairs={{0,24},{1,25},{2,26},{3,27},{4,28},{5,29},{6,30},{7,31},{8,16},{9,... | collective-permute-start | bytes 196616 | tf_op jit(solution)/shard_map/ppermute | solution.py:384
  29.9 4.3 %collective-permute-start.11 = (bf16[2,32,512]{2,1,0:T(8,128)(2,1)S(1)}, bf16[2,32,512]{2,1,0:T(8,128)(2,1)S(1)}, u32[]{:S(2)}, u32[]{:S(2)}) collective-permute-start(bf16[2,32,512]{2,1,0:T(8,128)(2,1)S(1)} %get-tuple-element.50), channel_id=1, source_target_pairs={{0,8},{1,17},{2,10},{3,19},{4,12},{5,21},{6,14},{7,23},{8,0},{9,25... | collective-permute-start | bytes 196616 | tf_op jit(solution)/shard_map/ppermute | solution.py:384
  30.5 4.3 %collective-permute-start.12 = (bf16[2,32,512]{2,1,0:T(8,128)(2,1)S(1)}, bf16[2,32,512]{2,1,0:T(8,128)(2,1)S(1)}, u32[]{:S(2)}, u32[]{:S(2)}) collective-permute-start(bf16[2,32,512]{2,1,0:T(8,128)(2,1)S(1)} %get-tuple-element.51), channel_id=1, source_target_pairs={{0,16},{1,9},{2,18},{3,11},{4,20},{5,13},{6,22},{7,15},{8,24},{9,1... | collective-permute-start | bytes 196616 | tf_op jit(solution)/shard_map/ppermute | solution.py:384
  36.3 6.0 %collective-permute-start.13 = (bf16[1,224,128]{2,1,0:T(8,128)(2,1)S(1)}, bf16[1,224,128]{2,1,0:T(8,128)(2,1)S(1)}, u32[]{:S(2)}, u32[]{:S(2)}) collective-permute-start(bf16[1,224,128]{2,1,0:T(8,128)(2,1)S(1)} %get-tuple-element.53), channel_id=1, source_target_pairs={{0,7},{1,6},{2,5},{3,4},{4,3},{5,2},{6,1},{7,0},{8,15},{9,14},{10,... | collective-permute-start | bytes 172040 | tf_op jit(solution)/shard_map/ppermute | solution.py:367
  36.4 7.2 %collective-permute-start.14 = (bf16[1,224,128]{2,1,0:T(8,128)(2,1)S(1)}, bf16[1,224,128]{2,1,0:T(8,128)(2,1)S(1)}, u32[]{:S(2)}, u32[]{:S(2)}) collective-permute-start(bf16[1,224,128]{2,1,0:T(8,128)(2,1)S(1)} %get-tuple-element.54), channel_id=1, source_target_pairs={{0,6},{1,7},{2,4},{3,5},{4,2},{5,3},{6,0},{7,1},{8,14},{9,15},{10,... | collective-permute-start | bytes 172040 | tf_op jit(solution)/shard_map/ppermute | solution.py:367
  38.2 8.6 %collective-permute-start.15 = (bf16[1,224,128]{2,1,0:T(8,128)(2,1)S(1)}, bf16[1,224,128]{2,1,0:T(8,128)(2,1)S(1)}, u32[]{:S(2)}, u32[]{:S(2)}) collective-permute-start(bf16[1,224,128]{2,1,0:T(8,128)(2,1)S(1)} %get-tuple-element.55), channel_id=1, source_target_pairs={{0,4},{1,2},{2,1},{3,7},{4,0},{5,6},{6,5},{7,3},{8,12},{9,10},{10,... | collective-permute-start | bytes 172040 | tf_op jit(solution)/shard_map/ppermute | solution.py:367
  39.0 7.9 %collective-permute-start.16 = (bf16[1,224,128]{2,1,0:T(8,128)(2,1)S(1)}, bf16[1,224,128]{2,1,0:T(8,128)(2,1)S(1)}, u32[]{:S(2)}, u32[]{:S(2)}) collective-permute-start(bf16[1,224,128]{2,1,0:T(8,128)(2,1)S(1)} %get-tuple-element.56), channel_id=1, source_target_pairs={{0,3},{1,5},{2,6},{3,0},{4,7},{5,1},{6,2},{7,4},{8,11},{9,13},{10,... | collective-permute-start | bytes 172040 | tf_op jit(solution)/shard_map/ppermute | solution.py:367
  41.7 7.5 %collective-permute-start.17 = (bf16[1,224,128]{2,1,0:T(8,128)(2,1)S(1)}, bf16[1,224,128]{2,1,0:T(8,128)(2,1)S(1)}, u32[]{:S(2)}, u32[]{:S(2)}) collective-permute-start(bf16[1,224,128]{2,1,0:T(8,128)(2,1)S(1)} %get-tuple-element.57), channel_id=1, source_target_pairs={{0,5},{1,3},{2,7},{3,1},{4,6},{5,0},{6,4},{7,2},{8,13},{9,11},{10,... | collective-permute-start | bytes 172040 | tf_op jit(solution)/shard_map/ppermute | solution.py:367
  42.3 6.8 %collective-permute-start.18 = (bf16[1,224,128]{2,1,0:T(8,128)(2,1)S(1)}, bf16[1,224,128]{2,1,0:T(8,128)(2,1)S(1)}, u32[]{:S(2)}, u32[]{:S(2)}) collective-permute-start(bf16[1,224,128]{2,1,0:T(8,128)(2,1)S(1)} %get-tuple-element.58), channel_id=1, source_target_pairs={{0,2},{1,4},{2,0},{3,6},{4,1},{5,7},{6,3},{7,5},{8,10},{9,12},{10,... | collective-permute-start | bytes 172040 | tf_op jit(solution)/shard_map/ppermute | solution.py:367
  43.6 5.5 %collective-permute-start.19 = (bf16[1,224,128]{2,1,0:T(8,128)(2,1)S(1)}, bf16[1,224,128]{2,1,0:T(8,128)(2,1)S(1)}, u32[]{:S(2)}, u32[]{:S(2)}) collective-permute-start(bf16[1,224,128]{2,1,0:T(8,128)(2,1)S(1)} %get-tuple-element.59), channel_id=1, source_target_pairs={{0,1},{1,0},{2,3},{3,2},{4,5},{5,4},{6,7},{7,6},{8,9},{9,8},{10,11... | collective-permute-start | bytes 172040 | tf_op jit(solution)/shard_map/ppermute | solution.py:367

commit v2 on v1

--- a/solution.py
+++ b/solution.py
@@ -152,58 +152,86 @@
             out[m, pl.ds(c * size, size), :] = rows.astype(bf16)
 
 
-def adjoint_kernel(slots_out, turn, ranks_far, basis_far, u_far, *rest):
+def adjoint_part(slots_out, first_rank, ranks, turned, basis, outs, stage, waits):
     shifts = sorted({n for slot in slots_out for n in slot[:2]})
-    ranks, u_ref, basis, stage, sems = rest[-5:]
-    outs = rest[-5 - len(slots_out) - turn : -5 - turn]
-    turned = rest[-6] if turn else u_far
-    freqs, rows, devices, cols, _, slots, tile = basis_far.shape
+    freqs, rows, devices, cols, _, slots, tile = basis.shape
     total = slots + slots // 6
-    half = turned.shape[3] // 2
     me = lax.axis_index("tile")
-    rank_copy = pltpu.make_async_copy(ranks_far, ranks, sems.at[0])
-    if turn:
-        data_copy = pltpu.make_async_copy(u_far, u_ref, sems.at[1])
-        data_copy.start()
-    rank_copy.start()
-    copies = [[] for _ in range(rows)]
     for i in range(rows):
-        for f in range(freqs):
-            for n, shift in enumerate(shifts):
-                copy = pltpu.make_async_copy(
-                    basis_far.at[f, i, me ^ shift],
-                    basis.at[f, i, n],
-                    sems.at[2 + (i * freqs + f) * len(shifts) + n],
-                )
-                copy.start(priority=n % 2)
-                copies[i].append(copy)
-    if turn:
-        data_copy.wait()
-        for f in range(freqs):
-            for i in range(rows):
-                values = u_ref[f, i * tile : (i + 1) * tile, :]
-                wide = values.astype(f32)
-                lane = lax.broadcasted_iota(jnp.int32, wide.shape, 1)
-                rolled = pltpu.roll(wide, half, 1)
-                turned[f, i, :tile, :] = values
-                turned[f, i, tile:, :] = jnp.where(lane < half, rolled, -rolled).astype(bf16)
-    rank_copy.wait()
-    for i in range(rows):
-        for copy in copies[i]:
+        for copy in waits[i]:
             copy.wait()
         for m in range(freqs // 2):
             pair = []
             for f in (2 * m, 2 * m + 1):
-                both = side_by_side(basis[f, i, :, :, 0], basis[f, i, :, :, 1])
-                pair.append(dot(both, turned[f, i], 1, 0))
+                real = jnp.concatenate([basis[f, i, me ^ n, :, 0] for n in shifts], axis=0)
+                imag = jnp.concatenate([basis[f, i, me ^ n, :, 1] for n in shifts], axis=0)
+                pair.append(dot(side_by_side(real, imag), turned[f, i], 1, 0))
             for n, shift in enumerate(shifts):
                 for c in range(cols):
-                    rank = ranks[2 * m, me * rows + i, (me ^ shift) * cols + c]
+                    col = (me ^ shift) * cols + c
+                    rank = ranks[0, first_rank + (m * rows + i) * devices * cols + col]
                     cut = slice((n * cols + c) * slots, (n * cols + c + 1) * slots)
-                    slot = (m * devices + (me ^ shift)) * cols + c
-                    pack_rows(stage, slot, i * total, rank, pair[0][cut], pair[1][cut])
+                    pack_rows(stage, m * devices * cols + col, i * total, rank, pair[0][cut], pair[1][cut])
     for m in range(freqs // 2):
         unstage(outs, slots_out, stage, m, devices, cols, rows * total, me)
+
+
+def adjoint_kernel(slots_out, cols, ranks_far, u_far, basis_far, *rest):
+    outs = rest[: len(slots_out)]
+    turned, basis, short_out, ranks, short, u_ref, stage, sems = rest[len(slots_out) :]
+    freqs, rows, devices, _, _, slots, tile = basis.shape
+    row_tiles, col_tiles = ranks.shape[1:]
+    half = turned.shape[3] // 2
+    me = lax.axis_index("tile")
+    shifts = sorted({n for slot in slots_out for n in slot[:2]})
+    rank_copy = pltpu.make_async_copy(ranks_far, ranks, sems.at[0])
+    data_copy = pltpu.make_async_copy(u_far, u_ref, sems.at[1])
+    data_copy.start()
+    rank_copy.start()
+    early, late, at = [[] for _ in range(rows)], [], 3
+    for group in (shifts, [n for n in range(devices) if n not in shifts]):
+        for i in range(rows):
+            for f in range(freqs):
+                for n in group:
+                    copy = pltpu.make_async_copy(
+                        basis_far.at[f, i, me ^ n], basis.at[f, i, me ^ n], sems.at[at]
+                    )
+                    at += 1
+                    copy.start(priority=n % 2)
+                    (early[i] if group is shifts else late).append(copy)
+    rank_copy.wait()
+    first_rank = freqs // 2 * row_tiles * cols
+    for m in range(freqs // 2):
+        for row in range(row_tiles):
+            for c in range(cols):
+                short[0, (m * row_tiles + row) * cols + c] = ranks[2 * m, row, me * cols + c]
+        for i in range(rows):
+            for col in range(col_tiles):
+                short[0, first_rank + (m * rows + i) * col_tiles + col] = ranks[2 * m, me * rows + i, col]
+    short_copy = pltpu.make_async_copy(short, short_out, sems.at[2])
+    short_copy.start()
+    data_copy.wait()
+    for f in range(freqs):
+        for i in range(rows):
+            values = u_ref[f, i * tile : (i + 1) * tile, :]
+            wide = values.astype(f32)
+            lane = lax.broadcasted_iota(jnp.int32, wide.shape, 1)
+            rolled = pltpu.roll(wide, half, 1)
+            turned[f, i, :tile, :] = values
+            turned[f, i, tile:, :] = jnp.where(lane < half, rolled, -rolled).astype(bf16)
+    adjoint_part(slots_out, first_rank, short, turned, basis, outs, stage, early)
+    short_copy.wait()
+    for copy in late:
+        copy.wait()
+
+
+def adjoint_rest_kernel(slots_out, first_rank, short, turned, basis, *rest):
+    outs = rest[: len(slots_out)]
+    ranks, stage, sem = rest[len(slots_out) :]
+    rank_copy = pltpu.make_async_copy(short, ranks, sem)
+    rank_copy.start()
+    waits = [[rank_copy]] + [[]] * (basis.shape[1] - 1)
+    adjoint_part(slots_out, first_rank, ranks, turned, basis, outs, stage, waits)
 
 
 def image_kernel(slots_in, owners, ranks_near, basis, *rest):
@@ -245,12 +273,10 @@
             outs[r][f] = jnp.concatenate([real, imag], axis=0).astype(bf16)
 
 
-def prepare_kernel(rows, cols, ranks_far, mask, table, choice, same, *rest):
-    short, high, low, ranks, full, sem = rest[-6:]
-    freqs, row_tiles, col_tiles = ranks.shape
-    me = lax.axis_index("tile")
-    rank_copy = pltpu.make_async_copy(ranks_far, ranks, sem)
-    rank_copy.start()
+def prepare_kernel(basis_far, mask, table, choice, same, *rest):
+    basis, high, low, full, sem = rest[-5:]
+    basis_copy = pltpu.make_async_copy(basis_far, basis, sem)
+    basis_copy.start()
     exact = lax.Precision.HIGHEST
     full[...] = dot(mask[...].astype(f32), table[...], 0, 0, exact)
     quarter, side = same.shape
@@ -261,18 +287,7 @@
         upper = block.astype(bf16)
         high[n * quarter : (n + 1) * quarter, :] = upper
         low[n * quarter : (n + 1) * quarter, :] = (block - upper.astype(f32)).astype(bf16)
-    rank_copy.wait()
-    at = 0
-    for m in range(freqs // 2):
-        for row in range(row_tiles):
-            for c in range(cols):
-                short[0, at] = ranks[2 * m, row, me * cols + c]
-                at += 1
-    for m in range(freqs // 2):
-        for i in range(rows):
-            for col in range(col_tiles):
-                short[0, at] = ranks[2 * m, me * rows + i, col]
-                at += 1
+    basis_copy.wait()
 
 
 def mix_kernel(owners, high, low, *rest):
@@ -400,7 +415,8 @@
     side = count * 2 * quarter
     by_cols = u_basis.reshape(freqs, rows, devices, cols, 2, slots, tile)
     by_rows = v_basis.reshape(freqs, devices, rows, cols, 2, slots, tile)
-    per_device = [((pairs, cols * rows * total, width), bf16)] * devices
+    packed_kind = ((pairs, cols * rows * total, width), bf16)
+    per_device = [packed_kind] * devices
     per_owner = [((freqs, 2 * quarter, cols * tile), bf16)] * owners
     work = {"flops": 4 * row_count * slots * width * col_tiles * freqs * 2, "moved": u_basis.size * 2}
     count_short = pairs * (row_tiles * cols + rows * col_tiles)
@@ -415,42 +431,44 @@
 
     early, late = exchange_slots(devices)
     slots_all = early + late
-    data, packed = (far, hold(u_data)), []
-    for turn, part in ((1, early), (0, late)):
-        partners = len(part)
-        made = call(
-            functools.partial(adjoint_kernel, part, turn),
-            "adjoint",
-            [(far, hold(ranks)), (far, hold(by_cols)), data],
-            [((pairs, cols * rows * total, width), bf16)] * partners
-            + [((freqs, rows, 2 * tile, width), bf16)] * turn,
-            [
-                pltpu.SMEM(ranks.shape, jnp.int32),
-                pltpu.VMEM((freqs, row_count, width), bf16),
-                pltpu.VMEM((freqs, rows, partners, cols, 2, slots, tile), bf16),
-                stage,
-                one((2 + freqs * rows * partners,)),
-            ],
-            **share(partners),
-        )
-        if turn:
-            data = (whole, made[-1])
-        packed += made[:partners]
-    short, *window = call(
-        functools.partial(prepare_kernel, rows, cols),
+    *packed, data, basis, short = call(
+        functools.partial(adjoint_kernel, early, cols),
+        "adjoint",
+        [(far, hold(x)) for x in (ranks, u_data, by_cols)],
+        [packed_kind] * len(early)
+        + [((freqs, rows, 2 * tile, width), bf16), (by_cols.shape, bf16), ((1, count_short), jnp.int32)],
+        [
+            pltpu.SMEM(ranks.shape, jnp.int32),
+            ranks_here,
+            pltpu.VMEM((freqs, row_count, width), bf16),
+            stage,
+            one((3 + freqs * rows * devices,)),
+        ],
+        **share(len(early)),
+    )
+    packed += call(
+        functools.partial(adjoint_rest_kernel, late, pairs * row_tiles * cols),
+        "adjoint",
+        [(whole, short), (whole, data), (whole, basis)],
+        [packed_kind] * len(late),
+        [ranks_here, stage, one],
+        **share(len(late)),
+    )
+    near, *window = call(
+        prepare_kernel,
         "prepare",
-        [(far, hold(ranks))]
+        [(far, hold(by_rows))]
         + [(whole, jnp.asarray(x)) for x in (time_mask, table, choice, same)]
         + [(anywhere, packed[-1])],
-        [((1, count_short), jnp.int32)] + [((side, side), bf16)] * 2,
-        [pltpu.SMEM(ranks.shape, jnp.int32), pltpu.VMEM((width // 2, 128), f32), one],
-        specs=[scalars, whole, whole],
+        [(by_rows.shape, bf16)] + [((side, side), bf16)] * 2,
+        [pltpu.VMEM((width // 2, 128), f32), one],
         flops=6 * quarter * 2 * count * 2 * count * side,
+        moved=u_basis.size * 2,
     )
     images = call(
         functools.partial(image_kernel, slots_all, owners),
         "image",
-        [(whole, short), (whole, by_rows)] + spread(packed, "tile", slots_all),
+        [(whole, short), (whole, near)] + spread(packed, "tile", slots_all),
         per_owner,
         [
             ranks_here,
@@ -472,7 +490,7 @@
     packed = call(
         functools.partial(forward_kernel, slots_all, owners),
         "forward",
-        [(whole, short), (whole, by_rows)] + to_owners(mixed),
+        [(whole, short), (whole, near)] + to_owners(mixed),
         per_device,
         [ranks_here, pltpu.VMEM((freqs, cols, width, 2 * tile), bf16), stage, one],
         **work,
@@ -480,7 +498,7 @@
     [out] = call(
         functools.partial(result_kernel, slots_all),
         "result",
-        [(whole, short), (whole, by_cols)] + spread(packed, "tile", slots_all),
+        [(whole, short), (whole, basis)] + spread(packed, "tile", slots_all),
         [((freqs, row_count, width), bf16)],
         [ranks_here, stage, pltpu.VMEM((rows, 2, col_tiles * slots, width), bf16), one],
         **work,

time: 51.6 us -> 50.5 us (0.979)
  Pallas kernels: 11.8 us -> 11.2 us
    pallas_call x7, Pallas kernels: 11.8 us -> 11.2 us  [call(): pl.pallas_call(kernel, in_specs=[spec for spec, _ in ins], out_specs=spec...]
  transfers between devices with their start and end apart: 20 -> 20, of which waited for: 10 -> 9; matrix products, arithmetic and copies ran while one was open for 0% -> 0% of each run, Pallas kernels for 9% -> 6%
where the time goes in v2:
time: 50.5 us; the launch traced here: 50.3 us
  starting transfers between devices  25.9 us (51%)
  waiting for transfers between devices  13.1 us (26%)
  Pallas kernels  11.2 us (22%)
    ppermute x14, starting transfers between devices, send(): lax.ppermute(value, axis, [(d, partner(d, slot)) for d in range(lax.axis_...  18.8 us
    pallas_call x7, Pallas kernels, call(): pl.pallas_call(kernel, in_specs=[spec for spec, _ in ins], out_specs=spec...  11.2 us
    ppermute x6, starting transfers between devices, to_owners(): value = lax.ppermute(value, ('freq', 'tile'), pairs)  7.11 us
    ppermute x6, waiting for transfers between devices, to_owners(): value = lax.ppermute(value, ('freq', 'tile'), pairs)  6.71 us
    ppermute x14, waiting for transfers between devices, send(): lax.ppermute(value, axis, [(d, partner(d, slot)) for d in range(lax.axis_...  6.41 us
  transfers between devices with their start and end apart: 20, of which 9 were waited for; matrix products, arithmetic and copies ran while one was open for 0% of the time, Pallas kernels for 6%

profile of v2, /device:TPU:0, one launch (start us, length us, event | category | flops | bytes accessed | tf_op | source)
XLA Modules:
  0.0 50.3 jit_solution(4926222655220237544)
XLA Ops:
  0.0 2.5 %adjoint.2 = (bf16[1,224,128]{2,1,0:T(8,128)(2,1)S(1)}, bf16[1,224,128]{2,1,0:T(8,128)(2,1)S(1)}, bf16[2,2,512,128]{3,2,1,0:T(8,128)(2,1)S(1)}, bf16[2,2,8,2,2,4...) custom-call(s32[2,16,16]{2,1,0:T(8,128)} %ranks_far.1, bf16[2,512,128]{2,1,0:T(8,128)(2,1)} %u_far.1, ...), custom_call_target="tpu_custom_call" | custom-call | flops 201326592 | bytes 786432 | tf_op jit(solution)/shard_map/adjoint/pallas_call | solution.py:28
  2.5 4.6 %collective-permute-start = (bf16[1,224,128]{2,1,0:T(8,128)(2,1)S(1)}, bf16[1,224,128]{2,1,0:T(8,128)(2,1)S(1)}, u32[]{:S(2)}, u32[]{:S(2)}) collective-permute-start(bf16[1,224,128]{2,1,0:T(8,128)(2,1)S(1)} %get-tuple-element.42), channel_id=1, source_target_pairs={{0,7},{1,6},{2,5},{3,4},{4,3},{5,2},{6,1},{7,0},{8,15},{9,14},{10,... | collective-permute-start | bytes 172040 | tf_op jit(solution)/shard_map/ppermute | solution.py:382
  7.1 0.6 %collective-permute-start.1 = (bf16[1,224,128]{2,1,0:T(8,128)(2,1)S(1)}, bf16[1,224,128]{2,1,0:T(8,128)(2,1)S(1)}, u32[]{:S(2)}, u32[]{:S(2)}) collective-permute-start(bf16[1,224,128]{2,1,0:T(8,128)(2,1)S(1)} %get-tuple-element.43), channel_id=1, source_target_pairs={{0,6},{1,7},{2,4},{3,5},{4,2},{5,3},{6,0},{7,1},{8,14},{9,15},{10,... | collective-permute-start | bytes 172040 | tf_op jit(solution)/shard_map/ppermute | solution.py:382
  7.7 1.4 %adjoint.3 = (bf16[1,224,128]{2,1,0:T(8,128)(2,1)S(1)}, bf16[1,224,128]{2,1,0:T(8,128)(2,1)S(1)}, bf16[1,224,128]{2,1,0:T(8,128)(2,1)S(1)}, bf16[1,224,128]{2,1,...) custom-call(s32[1,64]{1,0:T(1,128)S(1)} %get-tuple-element.35.short.ranks_near, ...), custom_call_target="tpu_custom_call" | custom-call | flops 603979776 | bytes 2359296 | tf_op jit(solution)/shard_map/adjoint/pallas_call | solution.py:28
  9.1 0.4 collective-permute-start.2
  9.5 3.1 %collective-permute-start.3 = (bf16[1,224,128]{2,1,0:T(8,128)(2,1)S(1)}, bf16[1,224,128]{2,1,0:T(8,128)(2,1)S(1)}, u32[]{:S(2)}, u32[]{:S(2)}) collective-permute-start(bf16[1,224,128]{2,1,0:T(8,128)(2,1)S(1)} %get-tuple-element.45), channel_id=1, source_target_pairs={{0,3},{1,5},{2,6},{3,0},{4,7},{5,1},{6,2},{7,4},{8,11},{9,13},{10,... | collective-permute-start | bytes 172040 | tf_op jit(solution)/shard_map/ppermute | solution.py:382
  12.6 1.2 %collective-permute-start.5 = (bf16[1,224,128]{2,1,0:T(8,128)(2,1)S(1)}, bf16[1,224,128]{2,1,0:T(8,128)(2,1)S(1)}, u32[]{:S(2)}, u32[]{:S(2)}) collective-permute-start(bf16[1,224,128]{2,1,0:T(8,128)(2,1)S(1)} %get-tuple-element.47), channel_id=1, source_target_pairs={{0,2},{1,4},{2,0},{3,6},{4,1},{5,7},{6,3},{7,5},{8,10},{9,12},{10,... | collective-permute-start | bytes 172040 | tf_op jit(solution)/shard_map/ppermute | solution.py:382
  13.9 1.9 %prepare.1 = (bf16[2,8,2,2,2,48,256]{6,5,4,3,2,1,0:T(8,128)(2,1)S(1)}, bf16[256,256]{1,0:T(8,128)(2,1)S(1)}, bf16[256,256]{1,0:T(8,128)(2,1)S(1)}) custom-call(bf16[2,8,2,2,2,48,256]{6,5,4,3,2,1,0:T(8,128)(2,1)} %bitcast.2, s32[64,64]{1,0:T(8,128)S(1)} %copy-done.1, f32[64,128]{1,0:T(8,128)S(1)} %copy-done.2, f32[16,4096]{1,0:T(8,128)S(1)} %copy-done, ...), custom_call_target="tpu_custom_call" | custom-call | flops 6291456 | bytes 3145728 | tf_op jit(solution)/shard_map/prepare/pallas_call | solution.py:28
  15.8 2.4 %collective-permute-done.4.rest_4_ = bf16[1,224,128]{2,1,0:T(8,128)(2,1)S(1)} collective-permute-done((bf16[1,224,128]{2,1,0:T(8,128)(2,1)S(1)}, bf16[1,224,128]{2,1,0:T(8,128)(2,1)S(1)}, u32[]{:S(2)}, u32[]{:S(2)}) %collective-permute-start.4) | collective-permute-done | bytes 57376 | tf_op jit(solution)/shard_map/ppermute | solution.py:382
  18.2 1.4 %image.1 = (bf16[2,32,512]{2,1,0:T(8,128)(2,1)S(1)}, bf16[2,32,512]{2,1,0:T(8,128)(2,1)S(1)}, bf16[2,32,512]{2,1,0:T(8,128)(2,1)S(1)}, bf16[2,32,512]{2,1,0:T(8,128)(2,1)S(1)}) custom-call(s32[1,64]{1,0:T(1,128)S(1)} %get-tuple-element.35.short.ranks_near, bf16[2,8,2,2,2,48,256]{6,5,4,3,2,1,0:T(8,128)(2,1)S(1)} %get-tuple-element.39.basis, ...), custom_call_target="tpu_custom_call" | custom-call | flops 805306368 | bytes 3145728 | tf_op jit(solution)/shard_map/image/pallas_call | solution.py:28
  19.6 2.5 %collective-permute-start.7 = (bf16[2,32,512]{2,1,0:T(8,128)(2,1)S(1)}, bf16[2,32,512]{2,1,0:T(8,128)(2,1)S(1)}, u32[]{:S(2)}, u32[]{:S(2)}) collective-permute-start(bf16[2,32,512]{2,1,0:T(8,128)(2,1)S(1)} %get-tuple-element.49), channel_id=1, source_target_pairs={{0,24},{1,25},{2,26},{3,27},{4,28},{5,29},{6,30},{7,31},{8,16},{9,... | collective-permute-start | bytes 196616 | tf_op jit(solution)/shard_map/ppermute | solution.py:399
  22.1 0.5 %collective-permute-start.8 = (bf16[2,32,512]{2,1,0:T(8,128)(2,1)S(1)}, bf16[2,32,512]{2,1,0:T(8,128)(2,1)S(1)}, u32[]{:S(2)}, u32[]{:S(2)}) collective-permute-start(bf16[2,32,512]{2,1,0:T(8,128)(2,1)S(1)} %get-tuple-element.50), channel_id=1, source_target_pairs={{0,8},{1,17},{2,10},{3,19},{4,12},{5,21},{6,14},{7,23},{8,0},{9,25... | collective-permute-start | bytes 196616 | tf_op jit(solution)/shard_map/ppermute | solution.py:399
  22.7 0.5 %collective-permute-start.9 = (bf16[2,32,512]{2,1,0:T(8,128)(2,1)S(1)}, bf16[2,32,512]{2,1,0:T(8,128)(2,1)S(1)}, u32[]{:S(2)}, u32[]{:S(2)}) collective-permute-start(bf16[2,32,512]{2,1,0:T(8,128)(2,1)S(1)} %get-tuple-element.51), channel_id=1, source_target_pairs={{0,16},{1,9},{2,18},{3,11},{4,20},{5,13},{6,22},{7,15},{8,24},{9,1... | collective-permute-start | bytes 196616 | tf_op jit(solution)/shard_map/ppermute | solution.py:399
  23.2 1.7 %collective-permute-done.7.rest_0_ = bf16[2,32,512]{2,1,0:T(8,128)(2,1)S(1)} collective-permute-done((bf16[2,32,512]{2,1,0:T(8,128)(2,1)S(1)}, bf16[2,32,512]{2,1,0:T(8,128)(2,1)S(1)}, u32[]{:S(2)}, u32[]{:S(2)}) %collective-permute-start.7) | collective-permute-done | bytes 65568 | tf_op jit(solution)/shard_map/ppermute | solution.py:399
  24.9 1.5 %collective-permute-done.8.rest_1_ = bf16[2,32,512]{2,1,0:T(8,128)(2,1)S(1)} collective-permute-done((bf16[2,32,512]{2,1,0:T(8,128)(2,1)S(1)}, bf16[2,32,512]{2,1,0:T(8,128)(2,1)S(1)}, u32[]{:S(2)}, u32[]{:S(2)}) %collective-permute-start.8) | collective-permute-done | bytes 65568 | tf_op jit(solution)/shard_map/ppermute | solution.py:399
  26.4 0.5 %collective-permute-done.9.rest_2_ = bf16[2,32,512]{2,1,0:T(8,128)(2,1)S(1)} collective-permute-done((bf16[2,32,512]{2,1,0:T(8,128)(2,1)S(1)}, bf16[2,32,512]{2,1,0:T(8,128)(2,1)S(1)}, u32[]{:S(2)}, u32[]{:S(2)}) %collective-permute-start.9) | collective-permute-done | bytes 65568 | tf_op jit(solution)/shard_map/ppermute | solution.py:399
  26.9 0.4 mix.1
  27.3 1.7 %collective-permute-start.10 = (bf16[2,32,512]{2,1,0:T(8,128)(2,1)S(1)}, bf16[2,32,512]{2,1,0:T(8,128)(2,1)S(1)}, u32[]{:S(2)}, u32[]{:S(2)}) collective-permute-start(bf16[2,32,512]{2,1,0:T(8,128)(2,1)S(1)} %get-tuple-element.53), channel_id=1, source_target_pairs={{0,24},{1,25},{2,26},{3,27},{4,28},{5,29},{6,30},{7,31},{8,16},{9,... | collective-permute-start | bytes 196616 | tf_op jit(solution)/shard_map/ppermute | solution.py:399
  29.0 0.6 %collective-permute-start.11 = (bf16[2,32,512]{2,1,0:T(8,128)(2,1)S(1)}, bf16[2,32,512]{2,1,0:T(8,128)(2,1)S(1)}, u32[]{:S(2)}, u32[]{:S(2)}) collective-permute-start(bf16[2,32,512]{2,1,0:T(8,128)(2,1)S(1)} %get-tuple-element.54), channel_id=1, source_target_pairs={{0,8},{1,17},{2,10},{3,19},{4,12},{5,21},{6,14},{7,23},{8,0},{9,25... | collective-permute-start | bytes 196616 | tf_op jit(solution)/shard_map/ppermute | solution.py:399
  29.5 1.3 %collective-permute-start.12 = (bf16[2,32,512]{2,1,0:T(8,128)(2,1)S(1)}, bf16[2,32,512]{2,1,0:T(8,128)(2,1)S(1)}, u32[]{:S(2)}, u32[]{:S(2)}) collective-permute-start(bf16[2,32,512]{2,1,0:T(8,128)(2,1)S(1)} %get-tuple-element.55), channel_id=1, source_target_pairs={{0,16},{1,9},{2,18},{3,11},{4,20},{5,13},{6,22},{7,15},{8,24},{9,1... | collective-permute-start | bytes 196616 | tf_op jit(solution)/shard_map/ppermute | solution.py:399
  30.8 2.3 %collective-permute-done.10.rest_0_ = bf16[2,32,512]{2,1,0:T(8,128)(2,1)S(1)} collective-permute-done((bf16[2,32,512]{2,1,0:T(8,128)(2,1)S(1)}, bf16[2,32,512]{2,1,0:T(8,128)(2,1)S(1)}, u32[]{:S(2)}, u32[]{:S(2)}) %collective-permute-start.10) | collective-permute-done | bytes 65568 | tf_op jit(solution)/shard_map/ppermute | solution.py:399
  33.2 0.6 %collective-permute-done.12.rest_2_ = bf16[2,32,512]{2,1,0:T(8,128)(2,1)S(1)} collective-permute-done((bf16[2,32,512]{2,1,0:T(8,128)(2,1)S(1)}, bf16[2,32,512]{2,1,0:T(8,128)(2,1)S(1)}, u32[]{:S(2)}, u32[]{:S(2)}) %collective-permute-start.12) | collective-permute-done | bytes 65568 | tf_op jit(solution)/shard_map/ppermute | solution.py:399
  33.8 1.6 %forward.1 = (bf16[1,224,128]{2,1,0:T(8,128)(2,1)S(1)}, bf16[1,224,128]{2,1,0:T(8,128)(2,1)S(1)}, bf16[1,224,128]{2,1,0:T(8,128)(2,1)S(1)}, bf16[1,224,128]{2,1,...) custom-call(s32[1,64]{1,0:T(1,128)S(1)} %get-tuple-element.35.short., ...), custom_call_target="tpu_custom_call" | custom-call | flops 805306368 | bytes 3145728 | tf_op jit(solution)/shard_map/forward/pallas_call | solution.py:28
  35.5 1.8 %collective-permute-start.14 = (bf16[1,224,128]{2,1,0:T(8,128)(2,1)S(1)}, bf16[1,224,128]{2,1,0:T(8,128)(2,1)S(1)}, u32[]{:S(2)}, u32[]{:S(2)}) collective-permute-start(bf16[1,224,128]{2,1,0:T(8,128)(2,1)S(1)} %get-tuple-element.58), channel_id=1, source_target_pairs={{0,6},{1,7},{2,4},{3,5},{4,2},{5,3},{6,0},{7,1},{8,14},{9,15},{10,... | collective-permute-start | bytes 172040 | tf_op jit(solution)/shard_map/ppermute | solution.py:382
  37.3 0.7 %collective-permute-start.15 = (bf16[1,224,128]{2,1,0:T(8,128)(2,1)S(1)}, bf16[1,224,128]{2,1,0:T(8,128)(2,1)S(1)}, u32[]{:S(2)}, u32[]{:S(2)}) collective-permute-start(bf16[1,224,128]{2,1,0:T(8,128)(2,1)S(1)} %get-tuple-element.59), channel_id=1, source_target_pairs={{0,4},{1,2},{2,1},{3,7},{4,0},{5,6},{6,5},{7,3},{8,12},{9,10},{10,... | collective-permute-start | bytes 172040 | tf_op jit(solution)/shard_map/ppermute | solution.py:382
  38.0 2.7 %collective-permute-start.16 = (bf16[1,224,128]{2,1,0:T(8,128)(2,1)S(1)}, bf16[1,224,128]{2,1,0:T(8,128)(2,1)S(1)}, u32[]{:S(2)}, u32[]{:S(2)}) collective-permute-start(bf16[1,224,128]{2,1,0:T(8,128)(2,1)S(1)} %get-tuple-element.60), channel_id=1, source_target_pairs={{0,3},{1,5},{2,6},{3,0},{4,7},{5,1},{6,2},{7,4},{8,11},{9,13},{10,... | collective-permute-start | bytes 172040 | tf_op jit(solution)/shard_map/ppermute | solution.py:382
  40.7 0.6 %collective-permute-start.17 = (bf16[1,224,128]{2,1,0:T(8,128)(2,1)S(1)}, bf16[1,224,128]{2,1,0:T(8,128)(2,1)S(1)}, u32[]{:S(2)}, u32[]{:S(2)}) collective-permute-start(bf16[1,224,128]{2,1,0:T(8,128)(2,1)S(1)} %get-tuple-element.61), channel_id=1, source_target_pairs={{0,5},{1,3},{2,7},{3,1},{4,6},{5,0},{6,4},{7,2},{8,13},{9,11},{10,... | collective-permute-start | bytes 172040 | tf_op jit(solution)/shard_map/ppermute | solution.py:382
  41.4 1.3 %collective-permute-start.18 = (bf16[1,224,128]{2,1,0:T(8,128)(2,1)S(1)}, bf16[1,224,128]{2,1,0:T(8,128)(2,1)S(1)}, u32[]{:S(2)}, u32[]{:S(2)}) collective-permute-start(bf16[1,224,128]{2,1,0:T(8,128)(2,1)S(1)} %get-tuple-element.62), channel_id=1, source_target_pairs={{0,2},{1,4},{2,0},{3,6},{4,1},{5,7},{6,3},{7,5},{8,10},{9,12},{10,... | collective-permute-start | bytes 172040 | tf_op jit(solution)/shard_map/ppermute | solution.py:382
  42.7 1.5 %collective-permute-start.19 = (bf16[1,224,128]{2,1,0:T(8,128)(2,1)S(1)}, bf16[1,224,128]{2,1,0:T(8,128)(2,1)S(1)}, u32[]{:S(2)}, u32[]{:S(2)}) collective-permute-start(bf16[1,224,128]{2,1,0:T(8,128)(2,1)S(1)} %get-tuple-element.63), channel_id=1, source_target_pairs={{0,1},{1,0},{2,3},{3,2},{4,5},{5,4},{6,7},{7,6},{8,9},{9,8},{10,11... | collective-permute-start | bytes 172040 | tf_op jit(solution)/shard_map/ppermute | solution.py:382
  44.2 1.7 %collective-permute-done.15.rest_2_ = bf16[1,224,128]{2,1,0:T(8,128)(2,1)S(1)} collective-permute-done((bf16[1,224,128]{2,1,0:T(8,128)(2,1)S(1)}, bf16[1,224,128]{2,1,0:T(8,128)(2,1)S(1)}, u32[]{:S(2)}, u32[]{:S(2)}) %collective-permute-start.15) | collective-permute-done | bytes 57376 | tf_op jit(solution)/shard_map/ppermute | solution.py:382
  45.9 2.3 %collective-permute-done.17.rest_4_ = bf16[1,224,128]{2,1,0:T(8,128)(2,1)S(1)} collective-permute-done((bf16[1,224,128]{2,1,0:T(8,128)(2,1)S(1)}, bf16[1,224,128]{2,1,0:T(8,128)(2,1)S(1)}, u32[]{:S(2)}, u32[]{:S(2)}) %collective-permute-start.17) | collective-permute-done | bytes 57376 | tf_op jit(solution)/shard_map/ppermute | solution.py:382
  48.2 2.1 %result.1 = bf16[2,512,128]{2,1,0:T(8,128)(2,1)} custom-call(s32[1,64]{1,0:T(1,128)S(1)} %get-tuple-element.35.short.ranks_near, bf16[2,2,8,2,2,48,256]{6,5,4,3,2,1,0:T(8,128)(2,1)S(1)} %get-tuple-element.36.basis, bf16[1,224,128]{2,1,0:T(8,128)(2,1)S(1)} %collective-permute-done.13.rest_0_, bf16[1,224,128]{2,1,0:T(8,128)(2,1)S(1)} %collective-permute-done.14.rest_1_, ...), custom_call_target="tpu_custom_call" | custom-call | flops 805306368 | bytes 3145728 | tf_op jit(solution)/shard_map/result/pallas_call | solution.py:28
  (23 shorter events, 0.3 us)
Async XLA Ops:
  0.0 13.9 %copy-start = (f32[16,4096]{1,0:T(8,128)S(1)}, f32[16,4096]{1,0:T(8,128)}, u32[]{:S(2)}) copy-start(f32[16,4096]{1,0:T(8,128)} %constant.7.clone.choice) | copy-start | bytes 786436
  0.0 13.9 %copy-start.1 = (s32[64,64]{1,0:T(8,128)S(1)}, s32[64,64]{1,0:T(8,128)}, u32[]{:S(2)}) copy-start(s32[64,64]{1,0:T(8,128)} %mask.1) | copy-start | bytes 49156
  0.0 13.9 %copy-start.2 = (f32[64,128]{1,0:T(8,128)S(1)}, f32[64,128]{1,0:T(8,128)}, u32[]{:S(2)}) copy-start(f32[64,128]{1,0:T(8,128)} %constant.6.clone.table) | copy-start | bytes 98308
  0.0 13.9 %copy-start.3 = (f32[16,256]{1,0:T(8,128)S(1)}, f32[16,256]{1,0:T(8,128)}, u32[]{:S(2)}) copy-start(f32[16,256]{1,0:T(8,128)} %constant.8.clone.same) | copy-start | bytes 49156
  2.5 10.2 %collective-permute-start = (bf16[1,224,128]{2,1,0:T(8,128)(2,1)S(1)}, bf16[1,224,128]{2,1,0:T(8,128)(2,1)S(1)}, u32[]{:S(2)}, u32[]{:S(2)}) collective-permute-start(bf16[1,224,128]{2,1,0:T(8,128)(2,1)S(1)} %get-tuple-element.42), channel_id=1, source_target_pairs={{0,7},{1,6},{2,5},{3,4},{4,3},{5,2},{6,1},{7,0},{8,15},{9,14},{10,... | collective-permute-start | bytes 172040 | tf_op jit(solution)/shard_map/ppermute | solution.py:382
  7.1 6.8 %collective-permute-start.1 = (bf16[1,224,128]{2,1,0:T(8,128)(2,1)S(1)}, bf16[1,224,128]{2,1,0:T(8,128)(2,1)S(1)}, u32[]{:S(2)}, u32[]{:S(2)}) collective-permute-start(bf16[1,224,128]{2,1,0:T(8,128)(2,1)S(1)} %get-tuple-element.43), channel_id=1, source_target_pairs={{0,6},{1,7},{2,4},{3,5},{4,2},{5,3},{6,0},{7,1},{8,14},{9,15},{10,... | collective-permute-start | bytes 172040 | tf_op jit(solution)/shard_map/ppermute | solution.py:382
  9.1 6.7 %collective-permute-start.2 = (bf16[1,224,128]{2,1,0:T(8,128)(2,1)S(1)}, bf16[1,224,128]{2,1,0:T(8,128)(2,1)S(1)}, u32[]{:S(2)}, u32[]{:S(2)}) collective-permute-start(bf16[1,224,128]{2,1,0:T(8,128)(2,1)S(1)} %get-tuple-element.44), channel_id=1, source_target_pairs={{0,4},{1,2},{2,1},{3,7},{4,0},{5,6},{6,5},{7,3},{8,12},{9,10},{10,... | collective-permute-start | bytes 172040 | tf_op jit(solution)/shard_map/ppermute | solution.py:382
  9.5 6.3 %collective-permute-start.3 = (bf16[1,224,128]{2,1,0:T(8,128)(2,1)S(1)}, bf16[1,224,128]{2,1,0:T(8,128)(2,1)S(1)}, u32[]{:S(2)}, u32[]{:S(2)}) collective-permute-start(bf16[1,224,128]{2,1,0:T(8,128)(2,1)S(1)} %get-tuple-element.45), channel_id=1, source_target_pairs={{0,3},{1,5},{2,6},{3,0},{4,7},{5,1},{6,2},{7,4},{8,11},{9,13},{10,... | collective-permute-start | bytes 172040 | tf_op jit(solution)/shard_map/ppermute | solution.py:382
  12.6 5.6 %collective-permute-start.4 = (bf16[1,224,128]{2,1,0:T(8,128)(2,1)S(1)}, bf16[1,224,128]{2,1,0:T(8,128)(2,1)S(1)}, u32[]{:S(2)}, u32[]{:S(2)}) collective-permute-start(bf16[1,224,128]{2,1,0:T(8,128)(2,1)S(1)} %get-tuple-element.46), channel_id=1, source_target_pairs={{0,5},{1,3},{2,7},{3,1},{4,6},{5,0},{6,4},{7,2},{8,13},{9,11},{10,... | collective-permute-start | bytes 172040 | tf_op jit(solution)/shard_map/ppermute | solution.py:382
  12.6 5.6 %collective-permute-start.5 = (bf16[1,224,128]{2,1,0:T(8,128)(2,1)S(1)}, bf16[1,224,128]{2,1,0:T(8,128)(2,1)S(1)}, u32[]{:S(2)}, u32[]{:S(2)}) collective-permute-start(bf16[1,224,128]{2,1,0:T(8,128)(2,1)S(1)} %get-tuple-element.47), channel_id=1, source_target_pairs={{0,2},{1,4},{2,0},{3,6},{4,1},{5,7},{6,3},{7,5},{8,10},{9,12},{10,... | collective-permute-start | bytes 172040 | tf_op jit(solution)/shard_map/ppermute | solution.py:382
  13.8 4.4 %collective-permute-start.6 = (bf16[1,224,128]{2,1,0:T(8,128)(2,1)S(1)}, bf16[1,224,128]{2,1,0:T(8,128)(2,1)S(1)}, u32[]{:S(2)}, u32[]{:S(2)}) collective-permute-start(bf16[1,224,128]{2,1,0:T(8,128)(2,1)S(1)} %get-tuple-element.48), channel_id=1, source_target_pairs={{0,1},{1,0},{2,3},{3,2},{4,5},{5,4},{6,7},{7,6},{8,9},{9,8},{10,11... | collective-permute-start | bytes 172040 | tf_op jit(solution)/shard_map/ppermute | solution.py:382
  19.6 5.3 %collective-permute-start.7 = (bf16[2,32,512]{2,1,0:T(8,128)(2,1)S(1)}, bf16[2,32,512]{2,1,0:T(8,128)(2,1)S(1)}, u32[]{:S(2)}, u32[]{:S(2)}) collective-permute-start(bf16[2,32,512]{2,1,0:T(8,128)(2,1)S(1)} %get-tuple-element.49), channel_id=1, source_target_pairs={{0,24},{1,25},{2,26},{3,27},{4,28},{5,29},{6,30},{7,31},{8,16},{9,... | collective-permute-start | bytes 196616 | tf_op jit(solution)/shard_map/ppermute | solution.py:399
  22.1 4.3 %collective-permute-start.8 = (bf16[2,32,512]{2,1,0:T(8,128)(2,1)S(1)}, bf16[2,32,512]{2,1,0:T(8,128)(2,1)S(1)}, u32[]{:S(2)}, u32[]{:S(2)}) collective-permute-start(bf16[2,32,512]{2,1,0:T(8,128)(2,1)S(1)} %get-tuple-element.50), channel_id=1, source_target_pairs={{0,8},{1,17},{2,10},{3,19},{4,12},{5,21},{6,14},{7,23},{8,0},{9,25... | collective-permute-start | bytes 196616 | tf_op jit(solution)/shard_map/ppermute | solution.py:399
  22.7 4.3 %collective-permute-start.9 = (bf16[2,32,512]{2,1,0:T(8,128)(2,1)S(1)}, bf16[2,32,512]{2,1,0:T(8,128)(2,1)S(1)}, u32[]{:S(2)}, u32[]{:S(2)}) collective-permute-start(bf16[2,32,512]{2,1,0:T(8,128)(2,1)S(1)} %get-tuple-element.51), channel_id=1, source_target_pairs={{0,16},{1,9},{2,18},{3,11},{4,20},{5,13},{6,22},{7,15},{8,24},{9,1... | collective-permute-start | bytes 196616 | tf_op jit(solution)/shard_map/ppermute | solution.py:399
  27.3 5.8 %collective-permute-start.10 = (bf16[2,32,512]{2,1,0:T(8,128)(2,1)S(1)}, bf16[2,32,512]{2,1,0:T(8,128)(2,1)S(1)}, u32[]{:S(2)}, u32[]{:S(2)}) collective-permute-start(bf16[2,32,512]{2,1,0:T(8,128)(2,1)S(1)} %get-tuple-element.53), channel_id=1, source_target_pairs={{0,24},{1,25},{2,26},{3,27},{4,28},{5,29},{6,30},{7,31},{8,16},{9,... | collective-permute-start | bytes 196616 | tf_op jit(solution)/shard_map/ppermute | solution.py:399
  29.0 4.3 %collective-permute-start.11 = (bf16[2,32,512]{2,1,0:T(8,128)(2,1)S(1)}, bf16[2,32,512]{2,1,0:T(8,128)(2,1)S(1)}, u32[]{:S(2)}, u32[]{:S(2)}) collective-permute-start(bf16[2,32,512]{2,1,0:T(8,128)(2,1)S(1)} %get-tuple-element.54), channel_id=1, source_target_pairs={{0,8},{1,17},{2,10},{3,19},{4,12},{5,21},{6,14},{7,23},{8,0},{9,25... | collective-permute-start | bytes 196616 | tf_op jit(solution)/shard_map/ppermute | solution.py:399
  29.5 4.3 %collective-permute-start.12 = (bf16[2,32,512]{2,1,0:T(8,128)(2,1)S(1)}, bf16[2,32,512]{2,1,0:T(8,128)(2,1)S(1)}, u32[]{:S(2)}, u32[]{:S(2)}) collective-permute-start(bf16[2,32,512]{2,1,0:T(8,128)(2,1)S(1)} %get-tuple-element.55), channel_id=1, source_target_pairs={{0,16},{1,9},{2,18},{3,11},{4,20},{5,13},{6,22},{7,15},{8,24},{9,1... | collective-permute-start | bytes 196616 | tf_op jit(solution)/shard_map/ppermute | solution.py:399
  35.4 6.0 %collective-permute-start.13 = (bf16[1,224,128]{2,1,0:T(8,128)(2,1)S(1)}, bf16[1,224,128]{2,1,0:T(8,128)(2,1)S(1)}, u32[]{:S(2)}, u32[]{:S(2)}) collective-permute-start(bf16[1,224,128]{2,1,0:T(8,128)(2,1)S(1)} %get-tuple-element.57), channel_id=1, source_target_pairs={{0,7},{1,6},{2,5},{3,4},{4,3},{5,2},{6,1},{7,0},{8,15},{9,14},{10,... | collective-permute-start | bytes 172040 | tf_op jit(solution)/shard_map/ppermute | solution.py:382
  35.5 7.2 %collective-permute-start.14 = (bf16[1,224,128]{2,1,0:T(8,128)(2,1)S(1)}, bf16[1,224,128]{2,1,0:T(8,128)(2,1)S(1)}, u32[]{:S(2)}, u32[]{:S(2)}) collective-permute-start(bf16[1,224,128]{2,1,0:T(8,128)(2,1)S(1)} %get-tuple-element.58), channel_id=1, source_target_pairs={{0,6},{1,7},{2,4},{3,5},{4,2},{5,3},{6,0},{7,1},{8,14},{9,15},{10,... | collective-permute-start | bytes 172040 | tf_op jit(solution)/shard_map/ppermute | solution.py:382
  37.3 8.6 %collective-permute-start.15 = (bf16[1,224,128]{2,1,0:T(8,128)(2,1)S(1)}, bf16[1,224,128]{2,1,0:T(8,128)(2,1)S(1)}, u32[]{:S(2)}, u32[]{:S(2)}) collective-permute-start(bf16[1,224,128]{2,1,0:T(8,128)(2,1)S(1)} %get-tuple-element.59), channel_id=1, source_target_pairs={{0,4},{1,2},{2,1},{3,7},{4,0},{5,6},{6,5},{7,3},{8,12},{9,10},{10,... | collective-permute-start | bytes 172040 | tf_op jit(solution)/shard_map/ppermute | solution.py:382
  38.0 7.9 %collective-permute-start.16 = (bf16[1,224,128]{2,1,0:T(8,128)(2,1)S(1)}, bf16[1,224,128]{2,1,0:T(8,128)(2,1)S(1)}, u32[]{:S(2)}, u32[]{:S(2)}) collective-permute-start(bf16[1,224,128]{2,1,0:T(8,128)(2,1)S(1)} %get-tuple-element.60), channel_id=1, source_target_pairs={{0,3},{1,5},{2,6},{3,0},{4,7},{5,1},{6,2},{7,4},{8,11},{9,13},{10,... | collective-permute-start | bytes 172040 | tf_op jit(solution)/shard_map/ppermute | solution.py:382
  40.7 7.5 %collective-permute-start.17 = (bf16[1,224,128]{2,1,0:T(8,128)(2,1)S(1)}, bf16[1,224,128]{2,1,0:T(8,128)(2,1)S(1)}, u32[]{:S(2)}, u32[]{:S(2)}) collective-permute-start(bf16[1,224,128]{2,1,0:T(8,128)(2,1)S(1)} %get-tuple-element.61), channel_id=1, source_target_pairs={{0,5},{1,3},{2,7},{3,1},{4,6},{5,0},{6,4},{7,2},{8,13},{9,11},{10,... | collective-permute-start | bytes 172040 | tf_op jit(solution)/shard_map/ppermute | solution.py:382
  41.4 6.8 %collective-permute-start.18 = (bf16[1,224,128]{2,1,0:T(8,128)(2,1)S(1)}, bf16[1,224,128]{2,1,0:T(8,128)(2,1)S(1)}, u32[]{:S(2)}, u32[]{:S(2)}) collective-permute-start(bf16[1,224,128]{2,1,0:T(8,128)(2,1)S(1)} %get-tuple-element.62), channel_id=1, source_target_pairs={{0,2},{1,4},{2,0},{3,6},{4,1},{5,7},{6,3},{7,5},{8,10},{9,12},{10,... | collective-permute-start | bytes 172040 | tf_op jit(solution)/shard_map/ppermute | solution.py:382
  42.7 5.5 %collective-permute-start.19 = (bf16[1,224,128]{2,1,0:T(8,128)(2,1)S(1)}, bf16[1,224,128]{2,1,0:T(8,128)(2,1)S(1)}, u32[]{:S(2)}, u32[]{:S(2)}) collective-permute-start(bf16[1,224,128]{2,1,0:T(8,128)(2,1)S(1)} %get-tuple-element.63), channel_id=1, source_target_pairs={{0,1},{1,0},{2,3},{3,2},{4,5},{5,4},{6,7},{7,6},{8,9},{9,8},{10,11... | collective-permute-start | bytes 172040 | tf_op jit(solution)/shard_map/ppermute | solution.py:382

commit v3 on v2

--- a/solution.py
+++ b/solution.py
@@ -234,6 +234,17 @@
     adjoint_part(slots_out, first_rank, ranks, turned, basis, outs, stage, waits)
 
 
+def gathered(slots_in):
+    shifts = sorted({n for slot in slots_in for n in slot[:2]})
+
+    def place(me, slot):
+        even, odd, mask = slot
+        first, second = shifts.index(even), shifts.index(odd)
+        return first if even == odd else first + parity(me, mask) * (second - first)
+
+    return shifts, place
+
+
 def image_kernel(slots_in, owners, ranks_near, basis, *rest):
     devices = len(slots_in)
     packed = rest[:devices]
@@ -344,36 +355,41 @@
         unstage(outs, slots_out, stage, m, devices, cols, rows * total, me)
 
 
-def result_kernel(slots_in, ranks_near, basis, *rest):
-    devices = len(slots_in)
-    packed = rest[:devices]
-    out, ranks, stage, coeffs, sem = rest[devices:]
-    freqs, rows, _, cols, _, slots, tile = basis.shape
+def result_kernel(slots_in, last, ranks_near, basis, *rest):
+    count = len(slots_in)
+    shifts, place = gathered(slots_in)
+    packed, rest = rest[:count], rest[count:]
+    out, ranks, stage, coeffs, sem = rest[-5:]
+    freqs, rows, devices, cols, _, slots, tile = basis.shape
     total = slots + slots // 6
     size = rows * total
-    before = freqs // 2 * devices * rows * cols
+    first_rank = freqs // 2 * devices * rows * cols
     me = lax.axis_index("tile")
     rank_copy = pltpu.make_async_copy(ranks_near, ranks, sem)
     rank_copy.start()
     for m in range(freqs // 2):
-        for s in range(devices):
+        for n in range(count):
             for c in range(cols):
-                block = packed[s][m, pl.ds(c * size, size), :]
-                stage[(m * devices + s) * cols + c, pl.ds(0, size), :] = block.astype(f32)
+                block = packed[n][m, pl.ds(c * size, size), :]
+                stage[(m * count + n) * cols + c, pl.ds(0, size), :] = block.astype(f32)
     rank_copy.wait()
     for m in range(freqs // 2):
         for i in range(rows):
-            for s in range(devices):
+            for n, slot in enumerate(slots_in):
                 for c in range(cols):
-                    col = partner(me, slots_in[s]) * cols + c
-                    rank = ranks[0, before + (m * rows + i) * devices * cols + col]
-                    slot = (m * devices + s) * cols + c
-                    unpack_rows(stage, slot, i * total, rank, total, coeffs.at[i], col * slots)
+                    col = partner(me, slot) * cols + c
+                    rank = ranks[0, first_rank + (m * rows + i) * devices * cols + col]
+                    base = (place(me, slot) * cols + c) * slots
+                    unpack_rows(stage, (m * count + n) * cols + c, i * total, rank, total, coeffs.at[i], base)
             for n in range(2):
                 f = 2 * m + n
-                both = side_by_side(basis[f, i, :, :, 0], basis[f, i, :, :, 1])
-                r = plain_product(coeffs[i, n], both)
-                out[f, pl.ds(i * tile, tile), :] = r.T.astype(bf16)
+                real = jnp.concatenate([basis[f, i, me ^ shift, :, 0] for shift in shifts], axis=0)
+                imag = jnp.concatenate([basis[f, i, me ^ shift, :, 1] for shift in shifts], axis=0)
+                part = plain_product(coeffs[i, n], side_by_side(real, imag))
+                if last:
+                    out[f, pl.ds(i * tile, tile), :] = (part + rest[0][f, i]).T.astype(bf16)
+                else:
+                    out[f, i] = part
 
 
 def send(value, axis, slot):
@@ -465,6 +481,17 @@
         flops=6 * quarter * 2 * count * 2 * count * side,
         moved=u_basis.size * 2,
     )
+    cut = len(early) + len([slot for slot in late if slot[0] != slot[1]]) // 4 * 2
+    own = len(slots_all) - 1
+    groups = [list(range(cut)) + [own], list(range(cut, own))]
+
+    def landed(packed):
+        arrived = spread(packed, "tile", slots_all)
+        return [[arrived[n] for n in group] for group in groups]
+
+    def stage_for(partners):
+        return pltpu.VMEM((pairs * partners * cols, stage_rows, width), f32)
+
     images = call(
         functools.partial(image_kernel, slots_all, owners),
         "image",
@@ -495,15 +522,23 @@
         [ranks_here, pltpu.VMEM((freqs, cols, width, 2 * tile), bf16), stage, one],
         **work,
     )
-    [out] = call(
-        functools.partial(result_kernel, slots_all),
-        "result",
-        [(whole, short), (whole, basis)] + spread(packed, "tile", slots_all),
-        [((freqs, row_count, width), bf16)],
-        [ranks_here, stage, pltpu.VMEM((rows, 2, col_tiles * slots, width), bf16), one],
-        **work,
-    )
-    return out
+    out = []
+    for group, arrived in zip(groups, landed(packed)):
+        last = group is groups[-1]
+        out = call(
+            functools.partial(result_kernel, [slots_all[n] for n in group], last),
+            "result",
+            [(whole, short), (whole, basis)] + arrived + [(whole, x) for x in out],
+            [((freqs, row_count, width), bf16) if last else ((freqs, rows, width, tile), f32)],
+            [
+                ranks_here,
+                stage_for(len(group)),
+                pltpu.VMEM((rows, 2, len(group) * cols * slots, width), bf16),
+                one,
+            ],
+            **share(len(group)),
+        )
+    return out[0]
 
 
 def solution(mesh):

time: 50.5 us -> 50.2 us (level)
  waiting for transfers between devices: 13.1 us -> 12 us
  Pallas kernels: 11.2 us -> 12.1 us
    ppermute x14, waiting for transfers between devices: 6.41 us -> 5.27 us  [send(): lax.ppermute(value, axis, [(d, partner(d, slot)) for d in range(lax.axis_...]
    pallas_call x7 -> x8, Pallas kernels: 11.2 us -> 12.1 us  [call(): pl.pallas_call(kernel, in_specs=[spec for spec, _ in ins], out_specs=spec...]
  transfers between devices with their start and end apart: 20 -> 20, of which waited for: 9 -> 9; matrix products, arithmetic and copies ran while one was open for 0% -> 0% of each run, Pallas kernels for 6% -> 9%
where the time goes in v3:
time: 50.2 us; the launch traced here: 50.1 us
  starting transfers between devices  25.9 us (52%)
  Pallas kernels  12.1 us (24%)
  waiting for transfers between devices  12 us (24%)
    ppermute x14, starting transfers between devices, send(): lax.ppermute(value, axis, [(d, partner(d, slot)) for d in range(lax.axis_...  18.8 us
    pallas_call x8, Pallas kernels, call(): pl.pallas_call(kernel, in_specs=[spec for spec, _ in ins], out_specs=spec...  12.1 us
    ppermute x6, starting transfers between devices, to_owners(): value = lax.ppermute(value, ('freq', 'tile'), pairs)  7.11 us
    ppermute x6, waiting for transfers between devices, to_owners(): value = lax.ppermute(value, ('freq', 'tile'), pairs)  6.72 us
    ppermute x14, waiting for transfers between devices, send(): lax.ppermute(value, axis, [(d, partner(d, slot)) for d in range(lax.axis_...  5.27 us
  transfers between devices with their start and end apart: 20, of which 9 were waited for; matrix products, arithmetic and copies ran while one was open for 0% of the time, Pallas kernels for 9%

profile of v3, /device:TPU:0, one launch (start us, length us, event | category | flops | bytes accessed | tf_op | source)
XLA Modules:
  0.0 50.1 jit_solution(3364234100849699836)
XLA Ops:
  0.0 2.5 %adjoint.2 = (bf16[1,224,128]{2,1,0:T(8,128)(2,1)S(1)}, bf16[1,224,128]{2,1,0:T(8,128)(2,1)S(1)}, bf16[2,2,512,128]{3,2,1,0:T(8,128)(2,1)S(1)}, bf16[2,2,8,2,2,4...) custom-call(s32[2,16,16]{2,1,0:T(8,128)} %ranks_far.1, bf16[2,512,128]{2,1,0:T(8,128)(2,1)} %u_far.1, ...), custom_call_target="tpu_custom_call" | custom-call | flops 201326592 | bytes 786432 | tf_op jit(solution)/shard_map/adjoint/pallas_call | solution.py:28
  2.5 4.6 %collective-permute-start = (bf16[1,224,128]{2,1,0:T(8,128)(2,1)S(1)}, bf16[1,224,128]{2,1,0:T(8,128)(2,1)S(1)}, u32[]{:S(2)}, u32[]{:S(2)}) collective-permute-start(bf16[1,224,128]{2,1,0:T(8,128)(2,1)S(1)} %get-tuple-element.42), channel_id=1, source_target_pairs={{0,7},{1,6},{2,5},{3,4},{4,3},{5,2},{6,1},{7,0},{8,15},{9,14},{10,... | collective-permute-start | bytes 172040 | tf_op jit(solution)/shard_map/ppermute | solution.py:398
  7.1 0.6 %collective-permute-start.1 = (bf16[1,224,128]{2,1,0:T(8,128)(2,1)S(1)}, bf16[1,224,128]{2,1,0:T(8,128)(2,1)S(1)}, u32[]{:S(2)}, u32[]{:S(2)}) collective-permute-start(bf16[1,224,128]{2,1,0:T(8,128)(2,1)S(1)} %get-tuple-element.43), channel_id=1, source_target_pairs={{0,6},{1,7},{2,4},{3,5},{4,2},{5,3},{6,0},{7,1},{8,14},{9,15},{10,... | collective-permute-start | bytes 172040 | tf_op jit(solution)/shard_map/ppermute | solution.py:398
  7.7 1.4 %adjoint.3 = (bf16[1,224,128]{2,1,0:T(8,128)(2,1)S(1)}, bf16[1,224,128]{2,1,0:T(8,128)(2,1)S(1)}, bf16[1,224,128]{2,1,0:T(8,128)(2,1)S(1)}, bf16[1,224,128]{2,1,...) custom-call(s32[1,64]{1,0:T(1,128)S(1)} %get-tuple-element.35.short.ranks_near, ...), custom_call_target="tpu_custom_call" | custom-call | flops 603979776 | bytes 2359296 | tf_op jit(solution)/shard_map/adjoint/pallas_call | solution.py:28
  9.1 0.4 collective-permute-start.2
  9.5 3.1 %collective-permute-start.3 = (bf16[1,224,128]{2,1,0:T(8,128)(2,1)S(1)}, bf16[1,224,128]{2,1,0:T(8,128)(2,1)S(1)}, u32[]{:S(2)}, u32[]{:S(2)}) collective-permute-start(bf16[1,224,128]{2,1,0:T(8,128)(2,1)S(1)} %get-tuple-element.45), channel_id=1, source_target_pairs={{0,3},{1,5},{2,6},{3,0},{4,7},{5,1},{6,2},{7,4},{8,11},{9,13},{10,... | collective-permute-start | bytes 172040 | tf_op jit(solution)/shard_map/ppermute | solution.py:398
  12.6 1.2 %collective-permute-start.5 = (bf16[1,224,128]{2,1,0:T(8,128)(2,1)S(1)}, bf16[1,224,128]{2,1,0:T(8,128)(2,1)S(1)}, u32[]{:S(2)}, u32[]{:S(2)}) collective-permute-start(bf16[1,224,128]{2,1,0:T(8,128)(2,1)S(1)} %get-tuple-element.47), channel_id=1, source_target_pairs={{0,2},{1,4},{2,0},{3,6},{4,1},{5,7},{6,3},{7,5},{8,10},{9,12},{10,... | collective-permute-start | bytes 172040 | tf_op jit(solution)/shard_map/ppermute | solution.py:398
  13.9 1.9 %prepare.1 = (bf16[2,8,2,2,2,48,256]{6,5,4,3,2,1,0:T(8,128)(2,1)S(1)}, bf16[256,256]{1,0:T(8,128)(2,1)S(1)}, bf16[256,256]{1,0:T(8,128)(2,1)S(1)}) custom-call(bf16[2,8,2,2,2,48,256]{6,5,4,3,2,1,0:T(8,128)(2,1)} %bitcast.2, s32[64,64]{1,0:T(8,128)S(1)} %copy-done.1, f32[64,128]{1,0:T(8,128)S(1)} %copy-done.2, f32[16,4096]{1,0:T(8,128)S(1)} %copy-done, ...), custom_call_target="tpu_custom_call" | custom-call | flops 6291456 | bytes 3145728 | tf_op jit(solution)/shard_map/prepare/pallas_call | solution.py:28
  15.8 2.4 %collective-permute-done.4.rest_4_ = bf16[1,224,128]{2,1,0:T(8,128)(2,1)S(1)} collective-permute-done((bf16[1,224,128]{2,1,0:T(8,128)(2,1)S(1)}, bf16[1,224,128]{2,1,0:T(8,128)(2,1)S(1)}, u32[]{:S(2)}, u32[]{:S(2)}) %collective-permute-start.4) | collective-permute-done | bytes 57376 | tf_op jit(solution)/shard_map/ppermute | solution.py:398
  18.2 1.4 %image.1 = (bf16[2,32,512]{2,1,0:T(8,128)(2,1)S(1)}, bf16[2,32,512]{2,1,0:T(8,128)(2,1)S(1)}, bf16[2,32,512]{2,1,0:T(8,128)(2,1)S(1)}, bf16[2,32,512]{2,1,0:T(8,128)(2,1)S(1)}) custom-call(s32[1,64]{1,0:T(1,128)S(1)} %get-tuple-element.35.short.ranks_near, bf16[2,8,2,2,2,48,256]{6,5,4,3,2,1,0:T(8,128)(2,1)S(1)} %get-tuple-element.39.basis, ...), custom_call_target="tpu_custom_call" | custom-call | flops 805306368 | bytes 3145728 | tf_op jit(solution)/shard_map/image/pallas_call | solution.py:28
  19.6 2.5 %collective-permute-start.7 = (bf16[2,32,512]{2,1,0:T(8,128)(2,1)S(1)}, bf16[2,32,512]{2,1,0:T(8,128)(2,1)S(1)}, u32[]{:S(2)}, u32[]{:S(2)}) collective-permute-start(bf16[2,32,512]{2,1,0:T(8,128)(2,1)S(1)} %get-tuple-element.49), channel_id=1, source_target_pairs={{0,24},{1,25},{2,26},{3,27},{4,28},{5,29},{6,30},{7,31},{8,16},{9,... | collective-permute-start | bytes 196616 | tf_op jit(solution)/shard_map/ppermute | solution.py:415
  22.1 0.5 %collective-permute-start.8 = (bf16[2,32,512]{2,1,0:T(8,128)(2,1)S(1)}, bf16[2,32,512]{2,1,0:T(8,128)(2,1)S(1)}, u32[]{:S(2)}, u32[]{:S(2)}) collective-permute-start(bf16[2,32,512]{2,1,0:T(8,128)(2,1)S(1)} %get-tuple-element.50), channel_id=1, source_target_pairs={{0,8},{1,17},{2,10},{3,19},{4,12},{5,21},{6,14},{7,23},{8,0},{9,25... | collective-permute-start | bytes 196616 | tf_op jit(solution)/shard_map/ppermute | solution.py:415
  22.7 0.5 %collective-permute-start.9 = (bf16[2,32,512]{2,1,0:T(8,128)(2,1)S(1)}, bf16[2,32,512]{2,1,0:T(8,128)(2,1)S(1)}, u32[]{:S(2)}, u32[]{:S(2)}) collective-permute-start(bf16[2,32,512]{2,1,0:T(8,128)(2,1)S(1)} %get-tuple-element.51), channel_id=1, source_target_pairs={{0,16},{1,9},{2,18},{3,11},{4,20},{5,13},{6,22},{7,15},{8,24},{9,1... | collective-permute-start | bytes 196616 | tf_op jit(solution)/shard_map/ppermute | solution.py:415
  23.2 1.7 %collective-permute-done.7.rest_0_ = bf16[2,32,512]{2,1,0:T(8,128)(2,1)S(1)} collective-permute-done((bf16[2,32,512]{2,1,0:T(8,128)(2,1)S(1)}, bf16[2,32,512]{2,1,0:T(8,128)(2,1)S(1)}, u32[]{:S(2)}, u32[]{:S(2)}) %collective-permute-start.7) | collective-permute-done | bytes 65568 | tf_op jit(solution)/shard_map/ppermute | solution.py:415
  24.9 1.5 %collective-permute-done.8.rest_1_ = bf16[2,32,512]{2,1,0:T(8,128)(2,1)S(1)} collective-permute-done((bf16[2,32,512]{2,1,0:T(8,128)(2,1)S(1)}, bf16[2,32,512]{2,1,0:T(8,128)(2,1)S(1)}, u32[]{:S(2)}, u32[]{:S(2)}) %collective-permute-start.8) | collective-permute-done | bytes 65568 | tf_op jit(solution)/shard_map/ppermute | solution.py:415
  26.4 0.5 %collective-permute-done.9.rest_2_ = bf16[2,32,512]{2,1,0:T(8,128)(2,1)S(1)} collective-permute-done((bf16[2,32,512]{2,1,0:T(8,128)(2,1)S(1)}, bf16[2,32,512]{2,1,0:T(8,128)(2,1)S(1)}, u32[]{:S(2)}, u32[]{:S(2)}) %collective-permute-start.9) | collective-permute-done | bytes 65568 | tf_op jit(solution)/shard_map/ppermute | solution.py:415
  27.3 1.7 %collective-permute-start.10 = (bf16[2,32,512]{2,1,0:T(8,128)(2,1)S(1)}, bf16[2,32,512]{2,1,0:T(8,128)(2,1)S(1)}, u32[]{:S(2)}, u32[]{:S(2)}) collective-permute-start(bf16[2,32,512]{2,1,0:T(8,128)(2,1)S(1)} %get-tuple-element.53), channel_id=1, source_target_pairs={{0,24},{1,25},{2,26},{3,27},{4,28},{5,29},{6,30},{7,31},{8,16},{9,... | collective-permute-start | bytes 196616 | tf_op jit(solution)/shard_map/ppermute | solution.py:415
  29.0 0.6 %collective-permute-start.11 = (bf16[2,32,512]{2,1,0:T(8,128)(2,1)S(1)}, bf16[2,32,512]{2,1,0:T(8,128)(2,1)S(1)}, u32[]{:S(2)}, u32[]{:S(2)}) collective-permute-start(bf16[2,32,512]{2,1,0:T(8,128)(2,1)S(1)} %get-tuple-element.54), channel_id=1, source_target_pairs={{0,8},{1,17},{2,10},{3,19},{4,12},{5,21},{6,14},{7,23},{8,0},{9,25... | collective-permute-start | bytes 196616 | tf_op jit(solution)/shard_map/ppermute | solution.py:415
  29.5 1.3 %collective-permute-start.12 = (bf16[2,32,512]{2,1,0:T(8,128)(2,1)S(1)}, bf16[2,32,512]{2,1,0:T(8,128)(2,1)S(1)}, u32[]{:S(2)}, u32[]{:S(2)}) collective-permute-start(bf16[2,32,512]{2,1,0:T(8,128)(2,1)S(1)} %get-tuple-element.55), channel_id=1, source_target_pairs={{0,16},{1,9},{2,18},{3,11},{4,20},{5,13},{6,22},{7,15},{8,24},{9,1... | collective-permute-start | bytes 196616 | tf_op jit(solution)/shard_map/ppermute | solution.py:415
  30.9 2.3 %collective-permute-done.10.rest_0_ = bf16[2,32,512]{2,1,0:T(8,128)(2,1)S(1)} collective-permute-done((bf16[2,32,512]{2,1,0:T(8,128)(2,1)S(1)}, bf16[2,32,512]{2,1,0:T(8,128)(2,1)S(1)}, u32[]{:S(2)}, u32[]{:S(2)}) %collective-permute-start.10) | collective-permute-done | bytes 65568 | tf_op jit(solution)/shard_map/ppermute | solution.py:415
  33.2 0.6 %collective-permute-done.12.rest_2_ = bf16[2,32,512]{2,1,0:T(8,128)(2,1)S(1)} collective-permute-done((bf16[2,32,512]{2,1,0:T(8,128)(2,1)S(1)}, bf16[2,32,512]{2,1,0:T(8,128)(2,1)S(1)}, u32[]{:S(2)}, u32[]{:S(2)}) %collective-permute-start.12) | collective-permute-done | bytes 65568 | tf_op jit(solution)/shard_map/ppermute | solution.py:415
  33.8 1.6 %forward.1 = (bf16[1,224,128]{2,1,0:T(8,128)(2,1)S(1)}, bf16[1,224,128]{2,1,0:T(8,128)(2,1)S(1)}, bf16[1,224,128]{2,1,0:T(8,128)(2,1)S(1)}, bf16[1,224,128]{2,1,...) custom-call(s32[1,64]{1,0:T(1,128)S(1)} %get-tuple-element.35.short., ...), custom_call_target="tpu_custom_call" | custom-call | flops 805306368 | bytes 3145728 | tf_op jit(solution)/shard_map/forward/pallas_call | solution.py:28
  35.5 1.8 %collective-permute-start.17 = (bf16[1,224,128]{2,1,0:T(8,128)(2,1)S(1)}, bf16[1,224,128]{2,1,0:T(8,128)(2,1)S(1)}, u32[]{:S(2)}, u32[]{:S(2)}) collective-permute-start(bf16[1,224,128]{2,1,0:T(8,128)(2,1)S(1)} %get-tuple-element.61), channel_id=1, source_target_pairs={{0,6},{1,7},{2,4},{3,5},{4,2},{5,3},{6,0},{7,1},{8,14},{9,15},{10,... | collective-permute-start | bytes 172040 | tf_op jit(solution)/shard_map/ppermute | solution.py:398
  37.3 0.8 %collective-permute-start.18 = (bf16[1,224,128]{2,1,0:T(8,128)(2,1)S(1)}, bf16[1,224,128]{2,1,0:T(8,128)(2,1)S(1)}, u32[]{:S(2)}, u32[]{:S(2)}) collective-permute-start(bf16[1,224,128]{2,1,0:T(8,128)(2,1)S(1)} %get-tuple-element.62), channel_id=1, source_target_pairs={{0,4},{1,2},{2,1},{3,7},{4,0},{5,6},{6,5},{7,3},{8,12},{9,10},{10,... | collective-permute-start | bytes 172040 | tf_op jit(solution)/shard_map/ppermute | solution.py:398
  38.0 2.7 %collective-permute-start.19 = (bf16[1,224,128]{2,1,0:T(8,128)(2,1)S(1)}, bf16[1,224,128]{2,1,0:T(8,128)(2,1)S(1)}, u32[]{:S(2)}, u32[]{:S(2)}) collective-permute-start(bf16[1,224,128]{2,1,0:T(8,128)(2,1)S(1)} %get-tuple-element.63), channel_id=1, source_target_pairs={{0,3},{1,5},{2,6},{3,0},{4,7},{5,1},{6,2},{7,4},{8,11},{9,13},{10,... | collective-permute-start | bytes 172040 | tf_op jit(solution)/shard_map/ppermute | solution.py:398
  40.7 0.7 %collective-permute-start.13 = (bf16[1,224,128]{2,1,0:T(8,128)(2,1)S(1)}, bf16[1,224,128]{2,1,0:T(8,128)(2,1)S(1)}, u32[]{:S(2)}, u32[]{:S(2)}) collective-permute-start(bf16[1,224,128]{2,1,0:T(8,128)(2,1)S(1)} %get-tuple-element.57), channel_id=1, source_target_pairs={{0,5},{1,3},{2,7},{3,1},{4,6},{5,0},{6,4},{7,2},{8,13},{9,11},{10,... | collective-permute-start | bytes 172040 | tf_op jit(solution)/shard_map/ppermute | solution.py:398
  41.4 1.3 %collective-permute-start.14 = (bf16[1,224,128]{2,1,0:T(8,128)(2,1)S(1)}, bf16[1,224,128]{2,1,0:T(8,128)(2,1)S(1)}, u32[]{:S(2)}, u32[]{:S(2)}) collective-permute-start(bf16[1,224,128]{2,1,0:T(8,128)(2,1)S(1)} %get-tuple-element.58), channel_id=1, source_target_pairs={{0,2},{1,4},{2,0},{3,6},{4,1},{5,7},{6,3},{7,5},{8,10},{9,12},{10,... | collective-permute-start | bytes 172040 | tf_op jit(solution)/shard_map/ppermute | solution.py:398
  42.7 1.5 %collective-permute-start.15 = (bf16[1,224,128]{2,1,0:T(8,128)(2,1)S(1)}, bf16[1,224,128]{2,1,0:T(8,128)(2,1)S(1)}, u32[]{:S(2)}, u32[]{:S(2)}) collective-permute-start(bf16[1,224,128]{2,1,0:T(8,128)(2,1)S(1)} %get-tuple-element.59), channel_id=1, source_target_pairs={{0,1},{1,0},{2,3},{3,2},{4,5},{5,4},{6,7},{7,6},{8,9},{9,8},{10,11... | collective-permute-start | bytes 172040 | tf_op jit(solution)/shard_map/ppermute | solution.py:398
  44.2 1.7 %collective-permute-done.18.rest_2_ = bf16[1,224,128]{2,1,0:T(8,128)(2,1)S(1)} collective-permute-done((bf16[1,224,128]{2,1,0:T(8,128)(2,1)S(1)}, bf16[1,224,128]{2,1,0:T(8,128)(2,1)S(1)}, u32[]{:S(2)}, u32[]{:S(2)}) %collective-permute-start.18) | collective-permute-done | bytes 57376 | tf_op jit(solution)/shard_map/ppermute | solution.py:398
  45.9 1.1 %result.2.rest_3_ = f32[2,2,128,256]{3,2,1,0:T(8,128)S(1)} custom-call(s32[1,64]{1,0:T(1,128)S(1)} %get-tuple-element.35.short.ranks_near, bf16[2,2,8,2,2,48,256]{6,5,4,3,2,1,0:T(8,128)(2,1)S(1)} %get-tuple-element.36.basis, bf16[1,224,128]{2,1,0:T(8,128)(2,1)S(1)} %collective-permute-done.16.rest_0_, ...), custom_call_target="tpu_custom_call" | custom-call | flops 503316480 | bytes 1966080 | tf_op jit(solution)/shard_map/result/pallas_call | solution.py:28
  47.1 1.1 %collective-permute-done.13.rest_0_ = bf16[1,224,128]{2,1,0:T(8,128)(2,1)S(1)} collective-permute-done((bf16[1,224,128]{2,1,0:T(8,128)(2,1)S(1)}, bf16[1,224,128]{2,1,0:T(8,128)(2,1)S(1)}, u32[]{:S(2)}, u32[]{:S(2)}) %collective-permute-start.13) | collective-permute-done | bytes 57376 | tf_op jit(solution)/shard_map/ppermute | solution.py:398
  48.2 1.9 %result.3 = bf16[2,512,128]{2,1,0:T(8,128)(2,1)} custom-call(s32[1,64]{1,0:T(1,128)S(1)} %get-tuple-element.35.short.ranks_near, bf16[2,2,8,2,2,48,256]{6,5,4,3,2,1,0:T(8,128)(2,1)S(1)} %get-tuple-element.36.basis, bf16[1,224,128]{2,1,0:T(8,128)(2,1)S(1)} %collective-permute-done.13.rest_0_, bf16[1,224,128]{2,1,0:T(8,128)(2,1)S(1)} %collective-permute-done.14.rest_1_, ...), custom_call_target="tpu_custom_call" | custom-call | flops 301989888 | bytes 1179648 | tf_op jit(solution)/shard_map/result/pallas_call | solution.py:28
  (24 shorter events, 0.7 us)
Async XLA Ops:
  0.0 13.9 %copy-start = (f32[16,4096]{1,0:T(8,128)S(1)}, f32[16,4096]{1,0:T(8,128)}, u32[]{:S(2)}) copy-start(f32[16,4096]{1,0:T(8,128)} %constant.7.clone.choice) | copy-start | bytes 786436
  0.0 13.9 %copy-start.1 = (s32[64,64]{1,0:T(8,128)S(1)}, s32[64,64]{1,0:T(8,128)}, u32[]{:S(2)}) copy-start(s32[64,64]{1,0:T(8,128)} %mask.1) | copy-start | bytes 49156
  0.0 13.9 %copy-start.2 = (f32[64,128]{1,0:T(8,128)S(1)}, f32[64,128]{1,0:T(8,128)}, u32[]{:S(2)}) copy-start(f32[64,128]{1,0:T(8,128)} %constant.6.clone.table) | copy-start | bytes 98308
  0.0 13.9 %copy-start.3 = (f32[16,256]{1,0:T(8,128)S(1)}, f32[16,256]{1,0:T(8,128)}, u32[]{:S(2)}) copy-start(f32[16,256]{1,0:T(8,128)} %constant.8.clone.same) | copy-start | bytes 49156
  2.5 10.2 %collective-permute-start = (bf16[1,224,128]{2,1,0:T(8,128)(2,1)S(1)}, bf16[1,224,128]{2,1,0:T(8,128)(2,1)S(1)}, u32[]{:S(2)}, u32[]{:S(2)}) collective-permute-start(bf16[1,224,128]{2,1,0:T(8,128)(2,1)S(1)} %get-tuple-element.42), channel_id=1, source_target_pairs={{0,7},{1,6},{2,5},{3,4},{4,3},{5,2},{6,1},{7,0},{8,15},{9,14},{10,... | collective-permute-start | bytes 172040 | tf_op jit(solution)/shard_map/ppermute | solution.py:398
  7.1 6.8 %collective-permute-start.1 = (bf16[1,224,128]{2,1,0:T(8,128)(2,1)S(1)}, bf16[1,224,128]{2,1,0:T(8,128)(2,1)S(1)}, u32[]{:S(2)}, u32[]{:S(2)}) collective-permute-start(bf16[1,224,128]{2,1,0:T(8,128)(2,1)S(1)} %get-tuple-element.43), channel_id=1, source_target_pairs={{0,6},{1,7},{2,4},{3,5},{4,2},{5,3},{6,0},{7,1},{8,14},{9,15},{10,... | collective-permute-start | bytes 172040 | tf_op jit(solution)/shard_map/ppermute | solution.py:398
  9.1 6.7 %collective-permute-start.2 = (bf16[1,224,128]{2,1,0:T(8,128)(2,1)S(1)}, bf16[1,224,128]{2,1,0:T(8,128)(2,1)S(1)}, u32[]{:S(2)}, u32[]{:S(2)}) collective-permute-start(bf16[1,224,128]{2,1,0:T(8,128)(2,1)S(1)} %get-tuple-element.44), channel_id=1, source_target_pairs={{0,4},{1,2},{2,1},{3,7},{4,0},{5,6},{6,5},{7,3},{8,12},{9,10},{10,... | collective-permute-start | bytes 172040 | tf_op jit(solution)/shard_map/ppermute | solution.py:398
  9.5 6.3 %collective-permute-start.3 = (bf16[1,224,128]{2,1,0:T(8,128)(2,1)S(1)}, bf16[1,224,128]{2,1,0:T(8,128)(2,1)S(1)}, u32[]{:S(2)}, u32[]{:S(2)}) collective-permute-start(bf16[1,224,128]{2,1,0:T(8,128)(2,1)S(1)} %get-tuple-element.45), channel_id=1, source_target_pairs={{0,3},{1,5},{2,6},{3,0},{4,7},{5,1},{6,2},{7,4},{8,11},{9,13},{10,... | collective-permute-start | bytes 172040 | tf_op jit(solution)/shard_map/ppermute | solution.py:398
  12.6 5.6 %collective-permute-start.4 = (bf16[1,224,128]{2,1,0:T(8,128)(2,1)S(1)}, bf16[1,224,128]{2,1,0:T(8,128)(2,1)S(1)}, u32[]{:S(2)}, u32[]{:S(2)}) collective-permute-start(bf16[1,224,128]{2,1,0:T(8,128)(2,1)S(1)} %get-tuple-element.46), channel_id=1, source_target_pairs={{0,5},{1,3},{2,7},{3,1},{4,6},{5,0},{6,4},{7,2},{8,13},{9,11},{10,... | collective-permute-start | bytes 172040 | tf_op jit(solution)/shard_map/ppermute | solution.py:398
  12.6 5.6 %collective-permute-start.5 = (bf16[1,224,128]{2,1,0:T(8,128)(2,1)S(1)}, bf16[1,224,128]{2,1,0:T(8,128)(2,1)S(1)}, u32[]{:S(2)}, u32[]{:S(2)}) collective-permute-start(bf16[1,224,128]{2,1,0:T(8,128)(2,1)S(1)} %get-tuple-element.47), channel_id=1, source_target_pairs={{0,2},{1,4},{2,0},{3,6},{4,1},{5,7},{6,3},{7,5},{8,10},{9,12},{10,... | collective-permute-start | bytes 172040 | tf_op jit(solution)/shard_map/ppermute | solution.py:398
  13.8 4.4 %collective-permute-start.6 = (bf16[1,224,128]{2,1,0:T(8,128)(2,1)S(1)}, bf16[1,224,128]{2,1,0:T(8,128)(2,1)S(1)}, u32[]{:S(2)}, u32[]{:S(2)}) collective-permute-start(bf16[1,224,128]{2,1,0:T(8,128)(2,1)S(1)} %get-tuple-element.48), channel_id=1, source_target_pairs={{0,1},{1,0},{2,3},{3,2},{4,5},{5,4},{6,7},{7,6},{8,9},{9,8},{10,11... | collective-permute-start | bytes 172040 | tf_op jit(solution)/shard_map/ppermute | solution.py:398
  19.6 5.3 %collective-permute-start.7 = (bf16[2,32,512]{2,1,0:T(8,128)(2,1)S(1)}, bf16[2,32,512]{2,1,0:T(8,128)(2,1)S(1)}, u32[]{:S(2)}, u32[]{:S(2)}) collective-permute-start(bf16[2,32,512]{2,1,0:T(8,128)(2,1)S(1)} %get-tuple-element.49), channel_id=1, source_target_pairs={{0,24},{1,25},{2,26},{3,27},{4,28},{5,29},{6,30},{7,31},{8,16},{9,... | collective-permute-start | bytes 196616 | tf_op jit(solution)/shard_map/ppermute | solution.py:415
  22.1 4.3 %collective-permute-start.8 = (bf16[2,32,512]{2,1,0:T(8,128)(2,1)S(1)}, bf16[2,32,512]{2,1,0:T(8,128)(2,1)S(1)}, u32[]{:S(2)}, u32[]{:S(2)}) collective-permute-start(bf16[2,32,512]{2,1,0:T(8,128)(2,1)S(1)} %get-tuple-element.50), channel_id=1, source_target_pairs={{0,8},{1,17},{2,10},{3,19},{4,12},{5,21},{6,14},{7,23},{8,0},{9,25... | collective-permute-start | bytes 196616 | tf_op jit(solution)/shard_map/ppermute | solution.py:415
  22.7 4.3 %collective-permute-start.9 = (bf16[2,32,512]{2,1,0:T(8,128)(2,1)S(1)}, bf16[2,32,512]{2,1,0:T(8,128)(2,1)S(1)}, u32[]{:S(2)}, u32[]{:S(2)}) collective-permute-start(bf16[2,32,512]{2,1,0:T(8,128)(2,1)S(1)} %get-tuple-element.51), channel_id=1, source_target_pairs={{0,16},{1,9},{2,18},{3,11},{4,20},{5,13},{6,22},{7,15},{8,24},{9,1... | collective-permute-start | bytes 196616 | tf_op jit(solution)/shard_map/ppermute | solution.py:415
  27.3 5.8 %collective-permute-start.10 = (bf16[2,32,512]{2,1,0:T(8,128)(2,1)S(1)}, bf16[2,32,512]{2,1,0:T(8,128)(2,1)S(1)}, u32[]{:S(2)}, u32[]{:S(2)}) collective-permute-start(bf16[2,32,512]{2,1,0:T(8,128)(2,1)S(1)} %get-tuple-element.53), channel_id=1, source_target_pairs={{0,24},{1,25},{2,26},{3,27},{4,28},{5,29},{6,30},{7,31},{8,16},{9,... | collective-permute-start | bytes 196616 | tf_op jit(solution)/shard_map/ppermute | solution.py:415
  29.0 4.3 %collective-permute-start.11 = (bf16[2,32,512]{2,1,0:T(8,128)(2,1)S(1)}, bf16[2,32,512]{2,1,0:T(8,128)(2,1)S(1)}, u32[]{:S(2)}, u32[]{:S(2)}) collective-permute-start(bf16[2,32,512]{2,1,0:T(8,128)(2,1)S(1)} %get-tuple-element.54), channel_id=1, source_target_pairs={{0,8},{1,17},{2,10},{3,19},{4,12},{5,21},{6,14},{7,23},{8,0},{9,25... | collective-permute-start | bytes 196616 | tf_op jit(solution)/shard_map/ppermute | solution.py:415
  29.5 4.3 %collective-permute-start.12 = (bf16[2,32,512]{2,1,0:T(8,128)(2,1)S(1)}, bf16[2,32,512]{2,1,0:T(8,128)(2,1)S(1)}, u32[]{:S(2)}, u32[]{:S(2)}) collective-permute-start(bf16[2,32,512]{2,1,0:T(8,128)(2,1)S(1)} %get-tuple-element.55), channel_id=1, source_target_pairs={{0,16},{1,9},{2,18},{3,11},{4,20},{5,13},{6,22},{7,15},{8,24},{9,1... | collective-permute-start | bytes 196616 | tf_op jit(solution)/shard_map/ppermute | solution.py:415
  35.4 6.0 %collective-permute-start.16 = (bf16[1,224,128]{2,1,0:T(8,128)(2,1)S(1)}, bf16[1,224,128]{2,1,0:T(8,128)(2,1)S(1)}, u32[]{:S(2)}, u32[]{:S(2)}) collective-permute-start(bf16[1,224,128]{2,1,0:T(8,128)(2,1)S(1)} %get-tuple-element.60), channel_id=1, source_target_pairs={{0,7},{1,6},{2,5},{3,4},{4,3},{5,2},{6,1},{7,0},{8,15},{9,14},{10,... | collective-permute-start | bytes 172040 | tf_op jit(solution)/shard_map/ppermute | solution.py:398
  35.5 7.2 %collective-permute-start.17 = (bf16[1,224,128]{2,1,0:T(8,128)(2,1)S(1)}, bf16[1,224,128]{2,1,0:T(8,128)(2,1)S(1)}, u32[]{:S(2)}, u32[]{:S(2)}) collective-permute-start(bf16[1,224,128]{2,1,0:T(8,128)(2,1)S(1)} %get-tuple-element.61), channel_id=1, source_target_pairs={{0,6},{1,7},{2,4},{3,5},{4,2},{5,3},{6,0},{7,1},{8,14},{9,15},{10,... | collective-permute-start | bytes 172040 | tf_op jit(solution)/shard_map/ppermute | solution.py:398
  37.3 8.6 %collective-permute-start.18 = (bf16[1,224,128]{2,1,0:T(8,128)(2,1)S(1)}, bf16[1,224,128]{2,1,0:T(8,128)(2,1)S(1)}, u32[]{:S(2)}, u32[]{:S(2)}) collective-permute-start(bf16[1,224,128]{2,1,0:T(8,128)(2,1)S(1)} %get-tuple-element.62), channel_id=1, source_target_pairs={{0,4},{1,2},{2,1},{3,7},{4,0},{5,6},{6,5},{7,3},{8,12},{9,10},{10,... | collective-permute-start | bytes 172040 | tf_op jit(solution)/shard_map/ppermute | solution.py:398
  38.0 7.9 %collective-permute-start.19 = (bf16[1,224,128]{2,1,0:T(8,128)(2,1)S(1)}, bf16[1,224,128]{2,1,0:T(8,128)(2,1)S(1)}, u32[]{:S(2)}, u32[]{:S(2)}) collective-permute-start(bf16[1,224,128]{2,1,0:T(8,128)(2,1)S(1)} %get-tuple-element.63), channel_id=1, source_target_pairs={{0,3},{1,5},{2,6},{3,0},{4,7},{5,1},{6,2},{7,4},{8,11},{9,13},{10,... | collective-permute-start | bytes 172040 | tf_op jit(solution)/shard_map/ppermute | solution.py:398
  40.7 7.5 %collective-permute-start.13 = (bf16[1,224,128]{2,1,0:T(8,128)(2,1)S(1)}, bf16[1,224,128]{2,1,0:T(8,128)(2,1)S(1)}, u32[]{:S(2)}, u32[]{:S(2)}) collective-permute-start(bf16[1,224,128]{2,1,0:T(8,128)(2,1)S(1)} %get-tuple-element.57), channel_id=1, source_target_pairs={{0,5},{1,3},{2,7},{3,1},{4,6},{5,0},{6,4},{7,2},{8,13},{9,11},{10,... | collective-permute-start | bytes 172040 | tf_op jit(solution)/shard_map/ppermute | solution.py:398
  41.4 6.8 %collective-permute-start.14 = (bf16[1,224,128]{2,1,0:T(8,128)(2,1)S(1)}, bf16[1,224,128]{2,1,0:T(8,128)(2,1)S(1)}, u32[]{:S(2)}, u32[]{:S(2)}) collective-permute-start(bf16[1,224,128]{2,1,0:T(8,128)(2,1)S(1)} %get-tuple-element.58), channel_id=1, source_target_pairs={{0,2},{1,4},{2,0},{3,6},{4,1},{5,7},{6,3},{7,5},{8,10},{9,12},{10,... | collective-permute-start | bytes 172040 | tf_op jit(solution)/shard_map/ppermute | solution.py:398
  42.7 5.5 %collective-permute-start.15 = (bf16[1,224,128]{2,1,0:T(8,128)(2,1)S(1)}, bf16[1,224,128]{2,1,0:T(8,128)(2,1)S(1)}, u32[]{:S(2)}, u32[]{:S(2)}) collective-permute-start(bf16[1,224,128]{2,1,0:T(8,128)(2,1)S(1)} %get-tuple-element.59), channel_id=1, source_target_pairs={{0,1},{1,0},{2,3},{3,2},{4,5},{5,4},{6,7},{7,6},{8,9},{9,8},{10,11... | collective-permute-start | bytes 172040 | tf_op jit(solution)/shard_map/ppermute | solution.py:398

commit v4 on v3

--- a/solution.py
+++ b/solution.py
@@ -118,7 +118,7 @@
             for mask in range(3, devices, 2)
             if not parity(near, mask) and not parity(far, mask)
         ]
-        if found and len(spare) > 2:
+        if found and len(spare) > 3:
             far, mask = found[0]
             spare.remove(far)
             mixed += [(far, near, mask), (near, far, mask)]

time: 50.2 us -> 51 us (1.016)
  waiting for transfers between devices: 12 us -> 13.4 us
  starting transfers between devices: 25.9 us -> 25.2 us
    ppermute x14, waiting for transfers between devices: 5.27 us -> 6.77 us  [send(): lax.ppermute(value, axis, [(d, partner(d, slot)) for d in range(lax.axis_...]
    ppermute x14, starting transfers between devices: 18.8 us -> 18.1 us  [send(): lax.ppermute(value, axis, [(d, partner(d, slot)) for d in range(lax.axis_...]
  transfers between devices with their start and end apart: 20 -> 20, of which waited for: 9 -> 12; matrix products, arithmetic and copies ran while one was open for 0% -> 0% of each run, Pallas kernels for 9% -> 8%
where the time goes in v4:
time: 51 us; the launch traced here: 50.8 us
  starting transfers between devices  25.2 us (49%)
  waiting for transfers between devices  13.4 us (26%)
  Pallas kernels  12.2 us (24%)
    ppermute x14, starting transfers between devices, send(): lax.ppermute(value, axis, [(d, partner(d, slot)) for d in range(lax.axis_...  18.1 us
    pallas_call x8, Pallas kernels, call(): pl.pallas_call(kernel, in_specs=[spec for spec, _ in ins], out_specs=spec...  12.2 us
    ppermute x6, starting transfers between devices, to_owners(): value = lax.ppermute(value, ('freq', 'tile'), pairs)  7.11 us
    ppermute x14, waiting for transfers between devices, send(): lax.ppermute(value, axis, [(d, partner(d, slot)) for d in range(lax.axis_...  6.77 us
    ppermute x6, waiting for transfers between devices, to_owners(): value = lax.ppermute(value, ('freq', 'tile'), pairs)  6.61 us
  transfers between devices with their start and end apart: 20, of which 12 were waited for; matrix products, arithmetic and copies ran while one was open for 0% of the time, Pallas kernels for 8%

profile of v4, /device:TPU:0, one launch (start us, length us, event | category | flops | bytes accessed | tf_op | source)
XLA Modules:
  0.0 50.8 jit_solution(17558128134843144064)
XLA Ops:
  0.0 2.7 %adjoint.2 = (bf16[1,224,128]{2,1,0:T(8,128)(2,1)S(1)}, bf16[1,224,128]{2,1,0:T(8,128)(2,1)S(1)}, bf16[1,224,128]{2,1,0:T(8,128)(2,1)S(1)}, bf16[2,2,512,128]{3,...) custom-call(s32[2,16,16]{2,1,0:T(8,128)} %ranks_far.1, ...), custom_call_target="tpu_custom_call" | custom-call | flops 301989888 | bytes 1179648 | tf_op jit(solution)/shard_map/adjoint/pallas_call | solution.py:28
  2.7 4.6 %collective-permute-start = (bf16[1,224,128]{2,1,0:T(8,128)(2,1)S(1)}, bf16[1,224,128]{2,1,0:T(8,128)(2,1)S(1)}, u32[]{:S(2)}, u32[]{:S(2)}) collective-permute-start(bf16[1,224,128]{2,1,0:T(8,128)(2,1)S(1)} %get-tuple-element.42), channel_id=1, source_target_pairs={{0,7},{1,6},{2,5},{3,4},{4,3},{5,2},{6,1},{7,0},{8,15},{9,14},{10,... | collective-permute-start | bytes 172040 | tf_op jit(solution)/shard_map/ppermute | solution.py:398
  7.3 0.6 %collective-permute-start.1 = (bf16[1,224,128]{2,1,0:T(8,128)(2,1)S(1)}, bf16[1,224,128]{2,1,0:T(8,128)(2,1)S(1)}, u32[]{:S(2)}, u32[]{:S(2)}) collective-permute-start(bf16[1,224,128]{2,1,0:T(8,128)(2,1)S(1)} %get-tuple-element.43), channel_id=1, source_target_pairs={{0,6},{1,7},{2,4},{3,5},{4,2},{5,3},{6,0},{7,1},{8,14},{9,15},{10,... | collective-permute-start | bytes 172040 | tf_op jit(solution)/shard_map/ppermute | solution.py:398
  8.3 1.3 %adjoint.3 = (bf16[1,224,128]{2,1,0:T(8,128)(2,1)S(1)}, bf16[1,224,128]{2,1,0:T(8,128)(2,1)S(1)}, bf16[1,224,128]{2,1,0:T(8,128)(2,1)S(1)}, bf16[1,224,128]{2,1,0:T(8,128)(2,1)S(1)}, bf16[1,224,128]{2,1,0:T(8,128)(2,1)S(1)}) custom-call(s32[1,64]{1,0:T(1,128)S(1)} %get-tuple-element.35.short.ranks_near, ...), custom_call_target="tpu_custom_call" | custom-call | flops 503316480 | bytes 1966080 | tf_op jit(solution)/shard_map/adjoint/pallas_call | solution.py:28
  9.6 2.3 %collective-permute-start.3 = (bf16[1,224,128]{2,1,0:T(8,128)(2,1)S(1)}, bf16[1,224,128]{2,1,0:T(8,128)(2,1)S(1)}, u32[]{:S(2)}, u32[]{:S(2)}) collective-permute-start(bf16[1,224,128]{2,1,0:T(8,128)(2,1)S(1)} %get-tuple-element.45), channel_id=1, source_target_pairs={{0,4},{1,2},{2,1},{3,7},{4,0},{5,6},{6,5},{7,3},{8,12},{9,10},{10,... | collective-permute-start | bytes 172040 | tf_op jit(solution)/shard_map/ppermute | solution.py:398
  11.8 1.0 %collective-permute-start.4 = (bf16[1,224,128]{2,1,0:T(8,128)(2,1)S(1)}, bf16[1,224,128]{2,1,0:T(8,128)(2,1)S(1)}, u32[]{:S(2)}, u32[]{:S(2)}) collective-permute-start(bf16[1,224,128]{2,1,0:T(8,128)(2,1)S(1)} %get-tuple-element.46), channel_id=1, source_target_pairs={{0,3},{1,5},{2,6},{3,0},{4,7},{5,1},{6,2},{7,4},{8,11},{9,13},{10,... | collective-permute-start | bytes 172040 | tf_op jit(solution)/shard_map/ppermute | solution.py:398
  12.8 1.1 %collective-permute-start.5 = (bf16[1,224,128]{2,1,0:T(8,128)(2,1)S(1)}, bf16[1,224,128]{2,1,0:T(8,128)(2,1)S(1)}, u32[]{:S(2)}, u32[]{:S(2)}) collective-permute-start(bf16[1,224,128]{2,1,0:T(8,128)(2,1)S(1)} %get-tuple-element.47), channel_id=1, source_target_pairs={{0,2},{1,3},{2,0},{3,1},{4,6},{5,7},{6,4},{7,5},{8,10},{9,11},{10,... | collective-permute-start | bytes 172040 | tf_op jit(solution)/shard_map/ppermute | solution.py:398
  14.0 1.9 %prepare.1 = (bf16[2,8,2,2,2,48,256]{6,5,4,3,2,1,0:T(8,128)(2,1)S(1)}, bf16[256,256]{1,0:T(8,128)(2,1)S(1)}, bf16[256,256]{1,0:T(8,128)(2,1)S(1)}) custom-call(bf16[2,8,2,2,2,48,256]{6,5,4,3,2,1,0:T(8,128)(2,1)} %bitcast.2, s32[64,64]{1,0:T(8,128)S(1)} %copy-done.1, f32[64,128]{1,0:T(8,128)S(1)} %copy-done.2, f32[16,4096]{1,0:T(8,128)S(1)} %copy-done, ...), custom_call_target="tpu_custom_call" | custom-call | flops 6291456 | bytes 3145728 | tf_op jit(solution)/shard_map/prepare/pallas_call | solution.py:28
  15.9 1.1 %collective-permute-done.3.rest_3_ = bf16[1,224,128]{2,1,0:T(8,128)(2,1)S(1)} collective-permute-done((bf16[1,224,128]{2,1,0:T(8,128)(2,1)S(1)}, bf16[1,224,128]{2,1,0:T(8,128)(2,1)S(1)}, u32[]{:S(2)}, u32[]{:S(2)}) %collective-permute-start.3) | collective-permute-done | bytes 57376 | tf_op jit(solution)/shard_map/ppermute | solution.py:398
  17.1 0.7 %collective-permute-done.4.rest_4_ = bf16[1,224,128]{2,1,0:T(8,128)(2,1)S(1)} collective-permute-done((bf16[1,224,128]{2,1,0:T(8,128)(2,1)S(1)}, bf16[1,224,128]{2,1,0:T(8,128)(2,1)S(1)}, u32[]{:S(2)}, u32[]{:S(2)}) %collective-permute-start.4) | collective-permute-done | bytes 57376 | tf_op jit(solution)/shard_map/ppermute | solution.py:398
  17.8 1.0 %collective-permute-done.5.rest_5_ = bf16[1,224,128]{2,1,0:T(8,128)(2,1)S(1)} collective-permute-done((bf16[1,224,128]{2,1,0:T(8,128)(2,1)S(1)}, bf16[1,224,128]{2,1,0:T(8,128)(2,1)S(1)}, u32[]{:S(2)}, u32[]{:S(2)}) %collective-permute-start.5) | collective-permute-done | bytes 57376 | tf_op jit(solution)/shard_map/ppermute | solution.py:398
  18.7 1.4 %image.1 = (bf16[2,32,512]{2,1,0:T(8,128)(2,1)S(1)}, bf16[2,32,512]{2,1,0:T(8,128)(2,1)S(1)}, bf16[2,32,512]{2,1,0:T(8,128)(2,1)S(1)}, bf16[2,32,512]{2,1,0:T(8,128)(2,1)S(1)}) custom-call(s32[1,64]{1,0:T(1,128)S(1)} %get-tuple-element.35.short.ranks_near, bf16[2,8,2,2,2,48,256]{6,5,4,3,2,1,0:T(8,128)(2,1)S(1)} %get-tuple-element.39.basis, ...), custom_call_target="tpu_custom_call" | custom-call | flops 805306368 | bytes 3145728 | tf_op jit(solution)/shard_map/image/pallas_call | solution.py:28
  20.1 2.5 %collective-permute-start.7 = (bf16[2,32,512]{2,1,0:T(8,128)(2,1)S(1)}, bf16[2,32,512]{2,1,0:T(8,128)(2,1)S(1)}, u32[]{:S(2)}, u32[]{:S(2)}) collective-permute-start(bf16[2,32,512]{2,1,0:T(8,128)(2,1)S(1)} %get-tuple-element.49), channel_id=1, source_target_pairs={{0,24},{1,25},{2,26},{3,27},{4,28},{5,29},{6,30},{7,31},{8,16},{9,... | collective-permute-start | bytes 196616 | tf_op jit(solution)/shard_map/ppermute | solution.py:415
  22.6 0.5 collective-permute-start.8
  23.1 0.6 %collective-permute-start.9 = (bf16[2,32,512]{2,1,0:T(8,128)(2,1)S(1)}, bf16[2,32,512]{2,1,0:T(8,128)(2,1)S(1)}, u32[]{:S(2)}, u32[]{:S(2)}) collective-permute-start(bf16[2,32,512]{2,1,0:T(8,128)(2,1)S(1)} %get-tuple-element.51), channel_id=1, source_target_pairs={{0,16},{1,9},{2,18},{3,11},{4,20},{5,13},{6,22},{7,15},{8,24},{9,1... | collective-permute-start | bytes 196616 | tf_op jit(solution)/shard_map/ppermute | solution.py:415
  23.7 1.7 %collective-permute-done.7.rest_0_ = bf16[2,32,512]{2,1,0:T(8,128)(2,1)S(1)} collective-permute-done((bf16[2,32,512]{2,1,0:T(8,128)(2,1)S(1)}, bf16[2,32,512]{2,1,0:T(8,128)(2,1)S(1)}, u32[]{:S(2)}, u32[]{:S(2)}) %collective-permute-start.7) | collective-permute-done | bytes 65568 | tf_op jit(solution)/shard_map/ppermute | solution.py:415
  25.4 1.5 %collective-permute-done.8.rest_1_ = bf16[2,32,512]{2,1,0:T(8,128)(2,1)S(1)} collective-permute-done((bf16[2,32,512]{2,1,0:T(8,128)(2,1)S(1)}, bf16[2,32,512]{2,1,0:T(8,128)(2,1)S(1)}, u32[]{:S(2)}, u32[]{:S(2)}) %collective-permute-start.8) | collective-permute-done | bytes 65568 | tf_op jit(solution)/shard_map/ppermute | solution.py:415
  26.9 0.5 collective-permute-done.9.rest_2_
  27.7 1.7 %collective-permute-start.10 = (bf16[2,32,512]{2,1,0:T(8,128)(2,1)S(1)}, bf16[2,32,512]{2,1,0:T(8,128)(2,1)S(1)}, u32[]{:S(2)}, u32[]{:S(2)}) collective-permute-start(bf16[2,32,512]{2,1,0:T(8,128)(2,1)S(1)} %get-tuple-element.53), channel_id=1, source_target_pairs={{0,24},{1,25},{2,26},{3,27},{4,28},{5,29},{6,30},{7,31},{8,16},{9,... | collective-permute-start | bytes 196616 | tf_op jit(solution)/shard_map/ppermute | solution.py:415
  29.5 0.5 collective-permute-start.11
  30.0 1.3 %collective-permute-start.12 = (bf16[2,32,512]{2,1,0:T(8,128)(2,1)S(1)}, bf16[2,32,512]{2,1,0:T(8,128)(2,1)S(1)}, u32[]{:S(2)}, u32[]{:S(2)}) collective-permute-start(bf16[2,32,512]{2,1,0:T(8,128)(2,1)S(1)} %get-tuple-element.55), channel_id=1, source_target_pairs={{0,16},{1,9},{2,18},{3,11},{4,20},{5,13},{6,22},{7,15},{8,24},{9,1... | collective-permute-start | bytes 196616 | tf_op jit(solution)/shard_map/ppermute | solution.py:415
  31.3 2.2 %collective-permute-done.10.rest_0_ = bf16[2,32,512]{2,1,0:T(8,128)(2,1)S(1)} collective-permute-done((bf16[2,32,512]{2,1,0:T(8,128)(2,1)S(1)}, bf16[2,32,512]{2,1,0:T(8,128)(2,1)S(1)}, u32[]{:S(2)}, u32[]{:S(2)}) %collective-permute-start.10) | collective-permute-done | bytes 65568 | tf_op jit(solution)/shard_map/ppermute | solution.py:415
  33.7 0.5 collective-permute-done.12.rest_2_
  34.2 1.6 %forward.1 = (bf16[1,224,128]{2,1,0:T(8,128)(2,1)S(1)}, bf16[1,224,128]{2,1,0:T(8,128)(2,1)S(1)}, bf16[1,224,128]{2,1,0:T(8,128)(2,1)S(1)}, bf16[1,224,128]{2,1,...) custom-call(s32[1,64]{1,0:T(1,128)S(1)} %get-tuple-element.35.short., ...), custom_call_target="tpu_custom_call" | custom-call | flops 805306368 | bytes 3145728 | tf_op jit(solution)/shard_map/forward/pallas_call | solution.py:28
  35.9 3.0 %collective-permute-start.18 = (bf16[1,224,128]{2,1,0:T(8,128)(2,1)S(1)}, bf16[1,224,128]{2,1,0:T(8,128)(2,1)S(1)}, u32[]{:S(2)}, u32[]{:S(2)}) collective-permute-start(bf16[1,224,128]{2,1,0:T(8,128)(2,1)S(1)} %get-tuple-element.62), channel_id=1, source_target_pairs={{0,6},{1,7},{2,4},{3,5},{4,2},{5,3},{6,0},{7,1},{8,14},{9,15},{10,... | collective-permute-start | bytes 172040 | tf_op jit(solution)/shard_map/ppermute | solution.py:398
  38.9 3.2 %collective-permute-start.13 = (bf16[1,224,128]{2,1,0:T(8,128)(2,1)S(1)}, bf16[1,224,128]{2,1,0:T(8,128)(2,1)S(1)}, u32[]{:S(2)}, u32[]{:S(2)}) collective-permute-start(bf16[1,224,128]{2,1,0:T(8,128)(2,1)S(1)} %get-tuple-element.57), channel_id=1, source_target_pairs={{0,4},{1,2},{2,1},{3,7},{4,0},{5,6},{6,5},{7,3},{8,12},{9,10},{10,... | collective-permute-start | bytes 172040 | tf_op jit(solution)/shard_map/ppermute | solution.py:398
  42.4 1.2 %collective-permute-start.15 = (bf16[1,224,128]{2,1,0:T(8,128)(2,1)S(1)}, bf16[1,224,128]{2,1,0:T(8,128)(2,1)S(1)}, u32[]{:S(2)}, u32[]{:S(2)}) collective-permute-start(bf16[1,224,128]{2,1,0:T(8,128)(2,1)S(1)} %get-tuple-element.59), channel_id=1, source_target_pairs={{0,2},{1,3},{2,0},{3,1},{4,6},{5,7},{6,4},{7,5},{8,10},{9,11},{10,... | collective-permute-start | bytes 172040 | tf_op jit(solution)/shard_map/ppermute | solution.py:398
  43.9 2.5 %collective-permute-done.19.rest_2_ = bf16[1,224,128]{2,1,0:T(8,128)(2,1)S(1)} collective-permute-done((bf16[1,224,128]{2,1,0:T(8,128)(2,1)S(1)}, bf16[1,224,128]{2,1,0:T(8,128)(2,1)S(1)}, u32[]{:S(2)}, u32[]{:S(2)}) %collective-permute-start.19) | collective-permute-done | bytes 57376 | tf_op jit(solution)/shard_map/ppermute | solution.py:398
  46.4 1.1 %result.2.rest_4_ = f32[2,2,128,256]{3,2,1,0:T(8,128)S(1)} custom-call(s32[1,64]{1,0:T(1,128)S(1)} %get-tuple-element.35.short.ranks_near, bf16[2,2,8,2,2,48,256]{6,5,4,3,2,1,0:T(8,128)(2,1)S(1)} %get-tuple-element.36.basis, bf16[1,224,128]{2,1,0:T(8,128)(2,1)S(1)} %collective-permute-done.17.rest_0_, ...), custom_call_target="tpu_custom_call" | custom-call | flops 402653184 | bytes 1572864 | tf_op jit(solution)/shard_map/result/pallas_call | solution.py:28
  47.5 0.8 %collective-permute-done.13.rest_0_ = bf16[1,224,128]{2,1,0:T(8,128)(2,1)S(1)} collective-permute-done((bf16[1,224,128]{2,1,0:T(8,128)(2,1)S(1)}, bf16[1,224,128]{2,1,0:T(8,128)(2,1)S(1)}, u32[]{:S(2)}, u32[]{:S(2)}) %collective-permute-start.13) | collective-permute-done | bytes 57376 | tf_op jit(solution)/shard_map/ppermute | solution.py:398
  48.3 0.6 %collective-permute-done.15.rest_2_ = bf16[1,224,128]{2,1,0:T(8,128)(2,1)S(1)} collective-permute-done((bf16[1,224,128]{2,1,0:T(8,128)(2,1)S(1)}, bf16[1,224,128]{2,1,0:T(8,128)(2,1)S(1)}, u32[]{:S(2)}, u32[]{:S(2)}) %collective-permute-start.15) | collective-permute-done | bytes 57376 | tf_op jit(solution)/shard_map/ppermute | solution.py:398
  48.9 1.9 %result.3 = bf16[2,512,128]{2,1,0:T(8,128)(2,1)} custom-call(s32[1,64]{1,0:T(1,128)S(1)} %get-tuple-element.35.short.ranks_near, bf16[2,2,8,2,2,48,256]{6,5,4,3,2,1,0:T(8,128)(2,1)S(1)} %get-tuple-element.36.basis, bf16[1,224,128]{2,1,0:T(8,128)(2,1)S(1)} %collective-permute-done.13.rest_0_, bf16[1,224,128]{2,1,0:T(8,128)(2,1)S(1)} %collective-permute-done.14.rest_1_, ...), custom_call_target="tpu_custom_call" | custom-call | flops 402653184 | bytes 1572864 | tf_op jit(solution)/shard_map/result/pallas_call | solution.py:28
  (24 shorter events, 1.8 us)
Async XLA Ops:
  0.0 14.0 %copy-start = (f32[16,4096]{1,0:T(8,128)S(1)}, f32[16,4096]{1,0:T(8,128)}, u32[]{:S(2)}) copy-start(f32[16,4096]{1,0:T(8,128)} %constant.7.clone.choice) | copy-start | bytes 786436
  0.0 14.0 %copy-start.1 = (s32[64,64]{1,0:T(8,128)S(1)}, s32[64,64]{1,0:T(8,128)}, u32[]{:S(2)}) copy-start(s32[64,64]{1,0:T(8,128)} %mask.1) | copy-start | bytes 49156
  0.0 14.0 %copy-start.2 = (f32[64,128]{1,0:T(8,128)S(1)}, f32[64,128]{1,0:T(8,128)}, u32[]{:S(2)}) copy-start(f32[64,128]{1,0:T(8,128)} %constant.6.clone.table) | copy-start | bytes 98308
  0.0 14.0 %copy-start.3 = (f32[16,256]{1,0:T(8,128)S(1)}, f32[16,256]{1,0:T(8,128)}, u32[]{:S(2)}) copy-start(f32[16,256]{1,0:T(8,128)} %constant.8.clone.same) | copy-start | bytes 49156
  2.7 10.1 %collective-permute-start = (bf16[1,224,128]{2,1,0:T(8,128)(2,1)S(1)}, bf16[1,224,128]{2,1,0:T(8,128)(2,1)S(1)}, u32[]{:S(2)}, u32[]{:S(2)}) collective-permute-start(bf16[1,224,128]{2,1,0:T(8,128)(2,1)S(1)} %get-tuple-element.42), channel_id=1, source_target_pairs={{0,7},{1,6},{2,5},{3,4},{4,3},{5,2},{6,1},{7,0},{8,15},{9,14},{10,... | collective-permute-start | bytes 172040 | tf_op jit(solution)/shard_map/ppermute | solution.py:398
  7.3 6.7 %collective-permute-start.1 = (bf16[1,224,128]{2,1,0:T(8,128)(2,1)S(1)}, bf16[1,224,128]{2,1,0:T(8,128)(2,1)S(1)}, u32[]{:S(2)}, u32[]{:S(2)}) collective-permute-start(bf16[1,224,128]{2,1,0:T(8,128)(2,1)S(1)} %get-tuple-element.43), channel_id=1, source_target_pairs={{0,6},{1,7},{2,4},{3,5},{4,2},{5,3},{6,0},{7,1},{8,14},{9,15},{10,... | collective-permute-start | bytes 172040 | tf_op jit(solution)/shard_map/ppermute | solution.py:398
  7.9 8.0 %collective-permute-start.2 = (bf16[1,224,128]{2,1,0:T(8,128)(2,1)S(1)}, bf16[1,224,128]{2,1,0:T(8,128)(2,1)S(1)}, u32[]{:S(2)}, u32[]{:S(2)}) collective-permute-start(bf16[1,224,128]{2,1,0:T(8,128)(2,1)S(1)} %get-tuple-element.44), channel_id=1, source_target_pairs={{0,5},{1,4},{2,7},{3,6},{4,1},{5,0},{6,3},{7,2},{8,13},{9,12},{10,... | collective-permute-start | bytes 172040 | tf_op jit(solution)/shard_map/ppermute | solution.py:398
  9.6 7.5 %collective-permute-start.3 = (bf16[1,224,128]{2,1,0:T(8,128)(2,1)S(1)}, bf16[1,224,128]{2,1,0:T(8,128)(2,1)S(1)}, u32[]{:S(2)}, u32[]{:S(2)}) collective-permute-start(bf16[1,224,128]{2,1,0:T(8,128)(2,1)S(1)} %get-tuple-element.45), channel_id=1, source_target_pairs={{0,4},{1,2},{2,1},{3,7},{4,0},{5,6},{6,5},{7,3},{8,12},{9,10},{10,... | collective-permute-start | bytes 172040 | tf_op jit(solution)/shard_map/ppermute | solution.py:398
  11.8 5.9 %collective-permute-start.4 = (bf16[1,224,128]{2,1,0:T(8,128)(2,1)S(1)}, bf16[1,224,128]{2,1,0:T(8,128)(2,1)S(1)}, u32[]{:S(2)}, u32[]{:S(2)}) collective-permute-start(bf16[1,224,128]{2,1,0:T(8,128)(2,1)S(1)} %get-tuple-element.46), channel_id=1, source_target_pairs={{0,3},{1,5},{2,6},{3,0},{4,7},{5,1},{6,2},{7,4},{8,11},{9,13},{10,... | collective-permute-start | bytes 172040 | tf_op jit(solution)/shard_map/ppermute | solution.py:398
  12.8 5.9 %collective-permute-start.5 = (bf16[1,224,128]{2,1,0:T(8,128)(2,1)S(1)}, bf16[1,224,128]{2,1,0:T(8,128)(2,1)S(1)}, u32[]{:S(2)}, u32[]{:S(2)}) collective-permute-start(bf16[1,224,128]{2,1,0:T(8,128)(2,1)S(1)} %get-tuple-element.47), channel_id=1, source_target_pairs={{0,2},{1,3},{2,0},{3,1},{4,6},{5,7},{6,4},{7,5},{8,10},{9,11},{10,... | collective-permute-start | bytes 172040 | tf_op jit(solution)/shard_map/ppermute | solution.py:398
  14.0 4.8 %collective-permute-start.6 = (bf16[1,224,128]{2,1,0:T(8,128)(2,1)S(1)}, bf16[1,224,128]{2,1,0:T(8,128)(2,1)S(1)}, u32[]{:S(2)}, u32[]{:S(2)}) collective-permute-start(bf16[1,224,128]{2,1,0:T(8,128)(2,1)S(1)} %get-tuple-element.48), channel_id=1, source_target_pairs={{0,1},{1,0},{2,3},{3,2},{4,5},{5,4},{6,7},{7,6},{8,9},{9,8},{10,11... | collective-permute-start | bytes 172040 | tf_op jit(solution)/shard_map/ppermute | solution.py:398
  20.1 5.3 %collective-permute-start.7 = (bf16[2,32,512]{2,1,0:T(8,128)(2,1)S(1)}, bf16[2,32,512]{2,1,0:T(8,128)(2,1)S(1)}, u32[]{:S(2)}, u32[]{:S(2)}) collective-permute-start(bf16[2,32,512]{2,1,0:T(8,128)(2,1)S(1)} %get-tuple-element.49), channel_id=1, source_target_pairs={{0,24},{1,25},{2,26},{3,27},{4,28},{5,29},{6,30},{7,31},{8,16},{9,... | collective-permute-start | bytes 196616 | tf_op jit(solution)/shard_map/ppermute | solution.py:415
  22.6 4.3 %collective-permute-start.8 = (bf16[2,32,512]{2,1,0:T(8,128)(2,1)S(1)}, bf16[2,32,512]{2,1,0:T(8,128)(2,1)S(1)}, u32[]{:S(2)}, u32[]{:S(2)}) collective-permute-start(bf16[2,32,512]{2,1,0:T(8,128)(2,1)S(1)} %get-tuple-element.50), channel_id=1, source_target_pairs={{0,8},{1,17},{2,10},{3,19},{4,12},{5,21},{6,14},{7,23},{8,0},{9,25... | collective-permute-start | bytes 196616 | tf_op jit(solution)/shard_map/ppermute | solution.py:415
  23.1 4.3 %collective-permute-start.9 = (bf16[2,32,512]{2,1,0:T(8,128)(2,1)S(1)}, bf16[2,32,512]{2,1,0:T(8,128)(2,1)S(1)}, u32[]{:S(2)}, u32[]{:S(2)}) collective-permute-start(bf16[2,32,512]{2,1,0:T(8,128)(2,1)S(1)} %get-tuple-element.51), channel_id=1, source_target_pairs={{0,16},{1,9},{2,18},{3,11},{4,20},{5,13},{6,22},{7,15},{8,24},{9,1... | collective-permute-start | bytes 196616 | tf_op jit(solution)/shard_map/ppermute | solution.py:415
  27.7 5.8 %collective-permute-start.10 = (bf16[2,32,512]{2,1,0:T(8,128)(2,1)S(1)}, bf16[2,32,512]{2,1,0:T(8,128)(2,1)S(1)}, u32[]{:S(2)}, u32[]{:S(2)}) collective-permute-start(bf16[2,32,512]{2,1,0:T(8,128)(2,1)S(1)} %get-tuple-element.53), channel_id=1, source_target_pairs={{0,24},{1,25},{2,26},{3,27},{4,28},{5,29},{6,30},{7,31},{8,16},{9,... | collective-permute-start | bytes 196616 | tf_op jit(solution)/shard_map/ppermute | solution.py:415
  29.5 4.3 %collective-permute-start.11 = (bf16[2,32,512]{2,1,0:T(8,128)(2,1)S(1)}, bf16[2,32,512]{2,1,0:T(8,128)(2,1)S(1)}, u32[]{:S(2)}, u32[]{:S(2)}) collective-permute-start(bf16[2,32,512]{2,1,0:T(8,128)(2,1)S(1)} %get-tuple-element.54), channel_id=1, source_target_pairs={{0,8},{1,17},{2,10},{3,19},{4,12},{5,21},{6,14},{7,23},{8,0},{9,25... | collective-permute-start | bytes 196616 | tf_op jit(solution)/shard_map/ppermute | solution.py:415
  30.0 4.3 %collective-permute-start.12 = (bf16[2,32,512]{2,1,0:T(8,128)(2,1)S(1)}, bf16[2,32,512]{2,1,0:T(8,128)(2,1)S(1)}, u32[]{:S(2)}, u32[]{:S(2)}) collective-permute-start(bf16[2,32,512]{2,1,0:T(8,128)(2,1)S(1)} %get-tuple-element.55), channel_id=1, source_target_pairs={{0,16},{1,9},{2,18},{3,11},{4,20},{5,13},{6,22},{7,15},{8,24},{9,1... | collective-permute-start | bytes 196616 | tf_op jit(solution)/shard_map/ppermute | solution.py:415
  35.8 6.6 %collective-permute-start.17 = (bf16[1,224,128]{2,1,0:T(8,128)(2,1)S(1)}, bf16[1,224,128]{2,1,0:T(8,128)(2,1)S(1)}, u32[]{:S(2)}, u32[]{:S(2)}) collective-permute-start(bf16[1,224,128]{2,1,0:T(8,128)(2,1)S(1)} %get-tuple-element.61), channel_id=1, source_target_pairs={{0,7},{1,6},{2,5},{3,4},{4,3},{5,2},{6,1},{7,0},{8,15},{9,14},{10,... | collective-permute-start | bytes 172040 | tf_op jit(solution)/shard_map/ppermute | solution.py:398
  35.9 7.7 %collective-permute-start.18 = (bf16[1,224,128]{2,1,0:T(8,128)(2,1)S(1)}, bf16[1,224,128]{2,1,0:T(8,128)(2,1)S(1)}, u32[]{:S(2)}, u32[]{:S(2)}) collective-permute-start(bf16[1,224,128]{2,1,0:T(8,128)(2,1)S(1)} %get-tuple-element.62), channel_id=1, source_target_pairs={{0,6},{1,7},{2,4},{3,5},{4,2},{5,3},{6,0},{7,1},{8,14},{9,15},{10,... | collective-permute-start | bytes 172040 | tf_op jit(solution)/shard_map/ppermute | solution.py:398
  38.9 7.5 %collective-permute-start.19 = (bf16[1,224,128]{2,1,0:T(8,128)(2,1)S(1)}, bf16[1,224,128]{2,1,0:T(8,128)(2,1)S(1)}, u32[]{:S(2)}, u32[]{:S(2)}) collective-permute-start(bf16[1,224,128]{2,1,0:T(8,128)(2,1)S(1)} %get-tuple-element.63), channel_id=1, source_target_pairs={{0,5},{1,4},{2,7},{3,6},{4,1},{5,0},{6,3},{7,2},{8,13},{9,12},{10,... | collective-permute-start | bytes 172040 | tf_op jit(solution)/shard_map/ppermute | solution.py:398
  38.9 9.4 %collective-permute-start.13 = (bf16[1,224,128]{2,1,0:T(8,128)(2,1)S(1)}, bf16[1,224,128]{2,1,0:T(8,128)(2,1)S(1)}, u32[]{:S(2)}, u32[]{:S(2)}) collective-permute-start(bf16[1,224,128]{2,1,0:T(8,128)(2,1)S(1)} %get-tuple-element.57), channel_id=1, source_target_pairs={{0,4},{1,2},{2,1},{3,7},{4,0},{5,6},{6,5},{7,3},{8,12},{9,10},{10,... | collective-permute-start | bytes 172040 | tf_op jit(solution)/shard_map/ppermute | solution.py:398
  42.1 6.3 %collective-permute-start.14 = (bf16[1,224,128]{2,1,0:T(8,128)(2,1)S(1)}, bf16[1,224,128]{2,1,0:T(8,128)(2,1)S(1)}, u32[]{:S(2)}, u32[]{:S(2)}) collective-permute-start(bf16[1,224,128]{2,1,0:T(8,128)(2,1)S(1)} %get-tuple-element.58), channel_id=1, source_target_pairs={{0,3},{1,5},{2,6},{3,0},{4,7},{5,1},{6,2},{7,4},{8,11},{9,13},{10,... | collective-permute-start | bytes 172040 | tf_op jit(solution)/shard_map/ppermute | solution.py:398
  42.4 6.5 %collective-permute-start.15 = (bf16[1,224,128]{2,1,0:T(8,128)(2,1)S(1)}, bf16[1,224,128]{2,1,0:T(8,128)(2,1)S(1)}, u32[]{:S(2)}, u32[]{:S(2)}) collective-permute-start(bf16[1,224,128]{2,1,0:T(8,128)(2,1)S(1)} %get-tuple-element.59), channel_id=1, source_target_pairs={{0,2},{1,3},{2,0},{3,1},{4,6},{5,7},{6,4},{7,5},{8,10},{9,11},{10,... | collective-permute-start | bytes 172040 | tf_op jit(solution)/shard_map/ppermute | solution.py:398
  43.6 5.4 %collective-permute-start.16 = (bf16[1,224,128]{2,1,0:T(8,128)(2,1)S(1)}, bf16[1,224,128]{2,1,0:T(8,128)(2,1)S(1)}, u32[]{:S(2)}, u32[]{:S(2)}) collective-permute-start(bf16[1,224,128]{2,1,0:T(8,128)(2,1)S(1)} %get-tuple-element.60), channel_id=1, source_target_pairs={{0,1},{1,0},{2,3},{3,2},{4,5},{5,4},{6,7},{7,6},{8,9},{9,8},{10,11... | collective-permute-start | bytes 172040 | tf_op jit(solution)/shard_map/ppermute | solution.py:398

commit v5 on v4

--- a/solution.py
+++ b/solution.py
@@ -111,21 +111,21 @@
     half = devices // 2
     spare, mixed = list(range(half, devices)), []
     alone = []
-    for near in reversed(range(2, half)):
+    for near in reversed(range(1, half)):
         found = [
             (far, mask)
             for far in spare
-            for mask in range(3, devices, 2)
+            for mask in range(1, devices)
             if not parity(near, mask) and not parity(far, mask)
         ]
-        if found and len(spare) > 3:
+        if found and len(spare) > 1:
             far, mask = found[0]
             spare.remove(far)
             mixed += [(far, near, mask), (near, far, mask)]
         else:
             alone.append((near, near, 1))
     first = [(far, far, 1) for far in reversed(spare)]
-    return first, mixed + alone + [(1, 1, 1)] * (devices > 1) + [(0, 0, 1)]
+    return first, mixed + alone + [(0, 0, 1)]
 
 
 def partner(me, slot):

time: 51 us -> 50.9 us (level)
  starting transfers between devices: 25.2 us -> 24.5 us
  waiting for transfers between devices: 13.4 us -> 14 us
    ppermute x14, waiting for transfers between devices: 6.77 us -> 7.46 us  [send(): lax.ppermute(value, axis, [(d, partner(d, slot)) for d in range(lax.axis_...]
    ppermute x14, starting transfers between devices: 18.1 us -> 17.4 us  [send(): lax.ppermute(value, axis, [(d, partner(d, slot)) for d in range(lax.axis_...]
  transfers between devices with their start and end apart: 20 -> 20, of which waited for: 12 -> 12; matrix products, arithmetic and copies ran while one was open for 0% -> 0% of each run, Pallas kernels for 8% -> 9%
where the time goes in v5:
time: 50.9 us; the launch traced here: 50.8 us
  starting transfers between devices  24.5 us (48%)
  waiting for transfers between devices  14 us (28%)
  Pallas kernels  12.1 us (24%)
    ppermute x14, starting transfers between devices, send(): lax.ppermute(value, axis, [(d, partner(d, slot)) for d in range(lax.axis_...  17.4 us
    pallas_call x8, Pallas kernels, call(): pl.pallas_call(kernel, in_specs=[spec for spec, _ in ins], out_specs=spec...  12.1 us
    ppermute x14, waiting for transfers between devices, send(): lax.ppermute(value, axis, [(d, partner(d, slot)) for d in range(lax.axis_...  7.46 us
    ppermute x6, starting transfers between devices, to_owners(): value = lax.ppermute(value, ('freq', 'tile'), pairs)  7.11 us
    ppermute x6, waiting for transfers between devices, to_owners(): value = lax.ppermute(value, ('freq', 'tile'), pairs)  6.58 us
  transfers between devices with their start and end apart: 20, of which 12 were waited for; matrix products, arithmetic and copies ran while one was open for 0% of the time, Pallas kernels for 9%

profile of v5, /device:TPU:0, one launch (start us, length us, event | category | flops | bytes accessed | tf_op | source)
XLA Modules:
  0.0 50.8 jit_solution(14658427863606253129)
XLA Ops:
  0.0 2.4 %adjoint.2 = (bf16[1,224,128]{2,1,0:T(8,128)(2,1)S(1)}, bf16[2,2,512,128]{3,2,1,0:T(8,128)(2,1)S(1)}, bf16[2,2,8,2,2,48,256]{6,5,4,3,2,1,0:T(8,128)(2,1)S(1)}, s32[1,64]{1,0:T(1,128)S(1)}) custom-call(s32[2,16,16]{2,1,0:T(8,128)} %ranks_far.1, bf16[2,512,128]{2,1,0:T(8,128)(2,1)} %u_far.1, bf16[2,2,8,2,2,48,256]{6,5,4,3,2,1,0:T(8,128)(2,1)} %bitcast.3), custom_call_target="tpu_custom_call" | custom-call | flops 100663296 | bytes 393216 | tf_op jit(solution)/shard_map/adjoint/pallas_call | solution.py:28
  2.4 4.6 %collective-permute-start = (bf16[1,224,128]{2,1,0:T(8,128)(2,1)S(1)}, bf16[1,224,128]{2,1,0:T(8,128)(2,1)S(1)}, u32[]{:S(2)}, u32[]{:S(2)}) collective-permute-start(bf16[1,224,128]{2,1,0:T(8,128)(2,1)S(1)} %get-tuple-element.42), channel_id=1, source_target_pairs={{0,7},{1,6},{2,5},{3,4},{4,3},{5,2},{6,1},{7,0},{8,15},{9,14},{10,... | collective-permute-start | bytes 172040 | tf_op jit(solution)/shard_map/ppermute | solution.py:398
  7.0 1.5 %adjoint.3 = (bf16[1,224,128]{2,1,0:T(8,128)(2,1)S(1)}, bf16[1,224,128]{2,1,0:T(8,128)(2,1)S(1)}, bf16[1,224,128]{2,1,0:T(8,128)(2,1)S(1)}, bf16[1,224,128]{2,1,...) custom-call(s32[1,64]{1,0:T(1,128)S(1)} %get-tuple-element.35.short., ...), custom_call_target="tpu_custom_call" | custom-call | flops 704643072 | bytes 2752512 | tf_op jit(solution)/shard_map/adjoint/pallas_call | solution.py:28
  8.8 2.7 %collective-permute-start.3 = (bf16[1,224,128]{2,1,0:T(8,128)(2,1)S(1)}, bf16[1,224,128]{2,1,0:T(8,128)(2,1)S(1)}, u32[]{:S(2)}, u32[]{:S(2)}) collective-permute-start(bf16[1,224,128]{2,1,0:T(8,128)(2,1)S(1)} %get-tuple-element.45), channel_id=1, source_target_pairs={{0,5},{1,3},{2,7},{3,1},{4,6},{5,0},{6,4},{7,2},{8,13},{9,11},{10,... | collective-permute-start | bytes 172040 | tf_op jit(solution)/shard_map/ppermute | solution.py:398
  11.5 1.7 %collective-permute-start.4 = (bf16[1,224,128]{2,1,0:T(8,128)(2,1)S(1)}, bf16[1,224,128]{2,1,0:T(8,128)(2,1)S(1)}, u32[]{:S(2)}, u32[]{:S(2)}) collective-permute-start(bf16[1,224,128]{2,1,0:T(8,128)(2,1)S(1)} %get-tuple-element.46), channel_id=1, source_target_pairs={{0,2},{1,4},{2,0},{3,6},{4,1},{5,7},{6,3},{7,5},{8,10},{9,12},{10,... | collective-permute-start | bytes 172040 | tf_op jit(solution)/shard_map/ppermute | solution.py:398
  13.2 0.5 %collective-permute-start.5 = (bf16[1,224,128]{2,1,0:T(8,128)(2,1)S(1)}, bf16[1,224,128]{2,1,0:T(8,128)(2,1)S(1)}, u32[]{:S(2)}, u32[]{:S(2)}) collective-permute-start(bf16[1,224,128]{2,1,0:T(8,128)(2,1)S(1)} %get-tuple-element.47), channel_id=1, source_target_pairs={{0,6},{1,7},{2,3},{3,2},{4,5},{5,4},{6,0},{7,1},{8,14},{9,15},{10,... | collective-permute-start | bytes 172040 | tf_op jit(solution)/shard_map/ppermute | solution.py:398
  13.7 0.6 %collective-permute-done.1.rest_1_ = bf16[1,224,128]{2,1,0:T(8,128)(2,1)S(1)} collective-permute-done((bf16[1,224,128]{2,1,0:T(8,128)(2,1)S(1)}, bf16[1,224,128]{2,1,0:T(8,128)(2,1)S(1)}, u32[]{:S(2)}, u32[]{:S(2)}) %collective-permute-start.1) | collective-permute-done | bytes 57376 | tf_op jit(solution)/shard_map/ppermute | solution.py:398
  14.3 1.0 %collective-permute-start.6 = (bf16[1,224,128]{2,1,0:T(8,128)(2,1)S(1)}, bf16[1,224,128]{2,1,0:T(8,128)(2,1)S(1)}, u32[]{:S(2)}, u32[]{:S(2)}) collective-permute-start(bf16[1,224,128]{2,1,0:T(8,128)(2,1)S(1)} %get-tuple-element.48), channel_id=1, source_target_pairs={{0,1},{1,0},{2,4},{3,5},{4,2},{5,3},{6,7},{7,6},{8,9},{9,8},{10,12... | collective-permute-start | bytes 172040 | tf_op jit(solution)/shard_map/ppermute | solution.py:398
  15.3 1.9 %prepare.1 = (bf16[2,8,2,2,2,48,256]{6,5,4,3,2,1,0:T(8,128)(2,1)S(1)}, bf16[256,256]{1,0:T(8,128)(2,1)S(1)}, bf16[256,256]{1,0:T(8,128)(2,1)S(1)}) custom-call(bf16[2,8,2,2,2,48,256]{6,5,4,3,2,1,0:T(8,128)(2,1)} %bitcast.2, s32[64,64]{1,0:T(8,128)S(1)} %copy-done.1, f32[64,128]{1,0:T(8,128)S(1)} %copy-done.2, f32[16,4096]{1,0:T(8,128)S(1)} %copy-done, ...), custom_call_target="tpu_custom_call" | custom-call | flops 6291456 | bytes 3145728 | tf_op jit(solution)/shard_map/prepare/pallas_call | solution.py:28
  17.3 2.3 %collective-permute-done.5.rest_5_ = bf16[1,224,128]{2,1,0:T(8,128)(2,1)S(1)} collective-permute-done((bf16[1,224,128]{2,1,0:T(8,128)(2,1)S(1)}, bf16[1,224,128]{2,1,0:T(8,128)(2,1)S(1)}, u32[]{:S(2)}, u32[]{:S(2)}) %collective-permute-start.5) | collective-permute-done | bytes 57376 | tf_op jit(solution)/shard_map/ppermute | solution.py:398
  19.6 1.4 %image.1 = (bf16[2,32,512]{2,1,0:T(8,128)(2,1)S(1)}, bf16[2,32,512]{2,1,0:T(8,128)(2,1)S(1)}, bf16[2,32,512]{2,1,0:T(8,128)(2,1)S(1)}, bf16[2,32,512]{2,1,0:T(8,128)(2,1)S(1)}) custom-call(s32[1,64]{1,0:T(1,128)S(1)} %get-tuple-element.35.short.ranks_near, bf16[2,8,2,2,2,48,256]{6,5,4,3,2,1,0:T(8,128)(2,1)S(1)} %get-tuple-element.39.basis, ...), custom_call_target="tpu_custom_call" | custom-call | flops 805306368 | bytes 3145728 | tf_op jit(solution)/shard_map/image/pallas_call | solution.py:28
  21.0 2.5 %collective-permute-start.7 = (bf16[2,32,512]{2,1,0:T(8,128)(2,1)S(1)}, bf16[2,32,512]{2,1,0:T(8,128)(2,1)S(1)}, u32[]{:S(2)}, u32[]{:S(2)}) collective-permute-start(bf16[2,32,512]{2,1,0:T(8,128)(2,1)S(1)} %get-tuple-element.49), channel_id=1, source_target_pairs={{0,24},{1,25},{2,26},{3,27},{4,28},{5,29},{6,30},{7,31},{8,16},{9,... | collective-permute-start | bytes 196616 | tf_op jit(solution)/shard_map/ppermute | solution.py:415
  23.5 0.5 %collective-permute-start.8 = (bf16[2,32,512]{2,1,0:T(8,128)(2,1)S(1)}, bf16[2,32,512]{2,1,0:T(8,128)(2,1)S(1)}, u32[]{:S(2)}, u32[]{:S(2)}) collective-permute-start(bf16[2,32,512]{2,1,0:T(8,128)(2,1)S(1)} %get-tuple-element.50), channel_id=1, source_target_pairs={{0,8},{1,17},{2,10},{3,19},{4,12},{5,21},{6,14},{7,23},{8,0},{9,25... | collective-permute-start | bytes 196616 | tf_op jit(solution)/shard_map/ppermute | solution.py:415
  24.5 1.7 %collective-permute-done.7.rest_0_ = bf16[2,32,512]{2,1,0:T(8,128)(2,1)S(1)} collective-permute-done((bf16[2,32,512]{2,1,0:T(8,128)(2,1)S(1)}, bf16[2,32,512]{2,1,0:T(8,128)(2,1)S(1)}, u32[]{:S(2)}, u32[]{:S(2)}) %collective-permute-start.7) | collective-permute-done | bytes 65568 | tf_op jit(solution)/shard_map/ppermute | solution.py:415
  26.3 1.5 %collective-permute-done.8.rest_1_ = bf16[2,32,512]{2,1,0:T(8,128)(2,1)S(1)} collective-permute-done((bf16[2,32,512]{2,1,0:T(8,128)(2,1)S(1)}, bf16[2,32,512]{2,1,0:T(8,128)(2,1)S(1)}, u32[]{:S(2)}, u32[]{:S(2)}) %collective-permute-start.8) | collective-permute-done | bytes 65568 | tf_op jit(solution)/shard_map/ppermute | solution.py:415
  27.8 0.5 %collective-permute-done.9.rest_2_ = bf16[2,32,512]{2,1,0:T(8,128)(2,1)S(1)} collective-permute-done((bf16[2,32,512]{2,1,0:T(8,128)(2,1)S(1)}, bf16[2,32,512]{2,1,0:T(8,128)(2,1)S(1)}, u32[]{:S(2)}, u32[]{:S(2)}) %collective-permute-start.9) | collective-permute-done | bytes 65568 | tf_op jit(solution)/shard_map/ppermute | solution.py:415
  28.7 1.5 %collective-permute-start.10 = (bf16[2,32,512]{2,1,0:T(8,128)(2,1)S(1)}, bf16[2,32,512]{2,1,0:T(8,128)(2,1)S(1)}, u32[]{:S(2)}, u32[]{:S(2)}) collective-permute-start(bf16[2,32,512]{2,1,0:T(8,128)(2,1)S(1)} %get-tuple-element.53), channel_id=1, source_target_pairs={{0,24},{1,25},{2,26},{3,27},{4,28},{5,29},{6,30},{7,31},{8,16},{9,... | collective-permute-start | bytes 196616 | tf_op jit(solution)/shard_map/ppermute | solution.py:415
  30.2 0.6 %collective-permute-start.11 = (bf16[2,32,512]{2,1,0:T(8,128)(2,1)S(1)}, bf16[2,32,512]{2,1,0:T(8,128)(2,1)S(1)}, u32[]{:S(2)}, u32[]{:S(2)}) collective-permute-start(bf16[2,32,512]{2,1,0:T(8,128)(2,1)S(1)} %get-tuple-element.54), channel_id=1, source_target_pairs={{0,8},{1,17},{2,10},{3,19},{4,12},{5,21},{6,14},{7,23},{8,0},{9,25... | collective-permute-start | bytes 196616 | tf_op jit(solution)/shard_map/ppermute | solution.py:415
  30.8 1.4 %collective-permute-start.12 = (bf16[2,32,512]{2,1,0:T(8,128)(2,1)S(1)}, bf16[2,32,512]{2,1,0:T(8,128)(2,1)S(1)}, u32[]{:S(2)}, u32[]{:S(2)}) collective-permute-start(bf16[2,32,512]{2,1,0:T(8,128)(2,1)S(1)} %get-tuple-element.55), channel_id=1, source_target_pairs={{0,16},{1,9},{2,18},{3,11},{4,20},{5,13},{6,22},{7,15},{8,24},{9,1... | collective-permute-start | bytes 196616 | tf_op jit(solution)/shard_map/ppermute | solution.py:415
  32.2 1.9 %collective-permute-done.10.rest_0_ = bf16[2,32,512]{2,1,0:T(8,128)(2,1)S(1)} collective-permute-done((bf16[2,32,512]{2,1,0:T(8,128)(2,1)S(1)}, bf16[2,32,512]{2,1,0:T(8,128)(2,1)S(1)}, u32[]{:S(2)}, u32[]{:S(2)}) %collective-permute-start.10) | collective-permute-done | bytes 65568 | tf_op jit(solution)/shard_map/ppermute | solution.py:415
  34.4 0.6 %collective-permute-done.12.rest_2_ = bf16[2,32,512]{2,1,0:T(8,128)(2,1)S(1)} collective-permute-done((bf16[2,32,512]{2,1,0:T(8,128)(2,1)S(1)}, bf16[2,32,512]{2,1,0:T(8,128)(2,1)S(1)}, u32[]{:S(2)}, u32[]{:S(2)}) %collective-permute-start.12) | collective-permute-done | bytes 65568 | tf_op jit(solution)/shard_map/ppermute | solution.py:415
  35.1 1.6 %forward.1 = (bf16[1,224,128]{2,1,0:T(8,128)(2,1)S(1)}, bf16[1,224,128]{2,1,0:T(8,128)(2,1)S(1)}, bf16[1,224,128]{2,1,0:T(8,128)(2,1)S(1)}, bf16[1,224,128]{2,1,...) custom-call(s32[1,64]{1,0:T(1,128)S(1)} %get-tuple-element.35.short., ...), custom_call_target="tpu_custom_call" | custom-call | flops 805306368 | bytes 3145728 | tf_op jit(solution)/shard_map/forward/pallas_call | solution.py:28
  36.7 1.5 %collective-permute-start.18 = (bf16[1,224,128]{2,1,0:T(8,128)(2,1)S(1)}, bf16[1,224,128]{2,1,0:T(8,128)(2,1)S(1)}, u32[]{:S(2)}, u32[]{:S(2)}) collective-permute-start(bf16[1,224,128]{2,1,0:T(8,128)(2,1)S(1)} %get-tuple-element.62), channel_id=1, source_target_pairs={{0,4},{1,2},{2,1},{3,7},{4,0},{5,6},{6,5},{7,3},{8,12},{9,10},{10,... | collective-permute-start | bytes 172040 | tf_op jit(solution)/shard_map/ppermute | solution.py:398
  38.2 2.3 %collective-permute-start.19 = (bf16[1,224,128]{2,1,0:T(8,128)(2,1)S(1)}, bf16[1,224,128]{2,1,0:T(8,128)(2,1)S(1)}, u32[]{:S(2)}, u32[]{:S(2)}) collective-permute-start(bf16[1,224,128]{2,1,0:T(8,128)(2,1)S(1)} %get-tuple-element.63), channel_id=1, source_target_pairs={{0,3},{1,5},{2,6},{3,0},{4,7},{5,1},{6,2},{7,4},{8,11},{9,13},{10,... | collective-permute-start | bytes 172040 | tf_op jit(solution)/shard_map/ppermute | solution.py:398
  40.6 0.9 %collective-permute-start.14 = (bf16[1,224,128]{2,1,0:T(8,128)(2,1)S(1)}, bf16[1,224,128]{2,1,0:T(8,128)(2,1)S(1)}, u32[]{:S(2)}, u32[]{:S(2)}) collective-permute-start(bf16[1,224,128]{2,1,0:T(8,128)(2,1)S(1)} %get-tuple-element.58), channel_id=1, source_target_pairs={{0,2},{1,4},{2,0},{3,6},{4,1},{5,7},{6,3},{7,5},{8,10},{9,12},{10,... | collective-permute-start | bytes 172040 | tf_op jit(solution)/shard_map/ppermute | solution.py:398
  41.4 1.4 %collective-permute-done.17.rest_0_ = bf16[1,224,128]{2,1,0:T(8,128)(2,1)S(1)} collective-permute-done((bf16[1,224,128]{2,1,0:T(8,128)(2,1)S(1)}, bf16[1,224,128]{2,1,0:T(8,128)(2,1)S(1)}, u32[]{:S(2)}, u32[]{:S(2)}) %collective-permute-start.17) | collective-permute-done | bytes 57376 | tf_op jit(solution)/shard_map/ppermute | solution.py:398
  42.8 0.9 %collective-permute-start.15 = (bf16[1,224,128]{2,1,0:T(8,128)(2,1)S(1)}, bf16[1,224,128]{2,1,0:T(8,128)(2,1)S(1)}, u32[]{:S(2)}, u32[]{:S(2)}) collective-permute-start(bf16[1,224,128]{2,1,0:T(8,128)(2,1)S(1)} %get-tuple-element.59), channel_id=1, source_target_pairs={{0,6},{1,7},{2,3},{3,2},{4,5},{5,4},{6,0},{7,1},{8,14},{9,15},{10,... | collective-permute-start | bytes 172040 | tf_op jit(solution)/shard_map/ppermute | solution.py:398
  43.8 0.9 %collective-permute-start.16 = (bf16[1,224,128]{2,1,0:T(8,128)(2,1)S(1)}, bf16[1,224,128]{2,1,0:T(8,128)(2,1)S(1)}, u32[]{:S(2)}, u32[]{:S(2)}) collective-permute-start(bf16[1,224,128]{2,1,0:T(8,128)(2,1)S(1)} %get-tuple-element.60), channel_id=1, source_target_pairs={{0,1},{1,0},{2,4},{3,5},{4,2},{5,3},{6,7},{7,6},{8,9},{9,8},{10,12... | collective-permute-start | bytes 172040 | tf_op jit(solution)/shard_map/ppermute | solution.py:398
  44.7 1.1 %result.2.rest_4_ = f32[2,2,128,256]{3,2,1,0:T(8,128)S(1)} custom-call(s32[1,64]{1,0:T(1,128)S(1)} %get-tuple-element.35.short.ranks_near, bf16[2,2,8,2,2,48,256]{6,5,4,3,2,1,0:T(8,128)(2,1)S(1)} %get-tuple-element.36.basis, bf16[1,224,128]{2,1,0:T(8,128)(2,1)S(1)} %collective-permute-done.17.rest_0_, ...), custom_call_target="tpu_custom_call" | custom-call | flops 402653184 | bytes 1572864 | tf_op jit(solution)/shard_map/result/pallas_call | solution.py:28
  45.8 1.2 %collective-permute-done.13.rest_0_ = bf16[1,224,128]{2,1,0:T(8,128)(2,1)S(1)} collective-permute-done((bf16[1,224,128]{2,1,0:T(8,128)(2,1)S(1)}, bf16[1,224,128]{2,1,0:T(8,128)(2,1)S(1)}, u32[]{:S(2)}, u32[]{:S(2)}) %collective-permute-start.13) | collective-permute-done | bytes 57376 | tf_op jit(solution)/shard_map/ppermute | solution.py:398
  47.0 1.9 %collective-permute-done.15.rest_2_ = bf16[1,224,128]{2,1,0:T(8,128)(2,1)S(1)} collective-permute-done((bf16[1,224,128]{2,1,0:T(8,128)(2,1)S(1)}, bf16[1,224,128]{2,1,0:T(8,128)(2,1)S(1)}, u32[]{:S(2)}, u32[]{:S(2)}) %collective-permute-start.15) | collective-permute-done | bytes 57376 | tf_op jit(solution)/shard_map/ppermute | solution.py:398
  48.9 1.9 %result.3 = bf16[2,512,128]{2,1,0:T(8,128)(2,1)} custom-call(s32[1,64]{1,0:T(1,128)S(1)} %get-tuple-element.35.short.ranks_near, bf16[2,2,8,2,2,48,256]{6,5,4,3,2,1,0:T(8,128)(2,1)S(1)} %get-tuple-element.36.basis, bf16[1,224,128]{2,1,0:T(8,128)(2,1)S(1)} %collective-permute-done.13.rest_0_, bf16[1,224,128]{2,1,0:T(8,128)(2,1)S(1)} %collective-permute-done.14.rest_1_, ...), custom_call_target="tpu_custom_call" | custom-call | flops 402653184 | bytes 1572864 | tf_op jit(solution)/shard_map/result/pallas_call | solution.py:28
  (24 shorter events, 1.8 us)
Async XLA Ops:
  0.0 15.3 %copy-start = (f32[16,4096]{1,0:T(8,128)S(1)}, f32[16,4096]{1,0:T(8,128)}, u32[]{:S(2)}) copy-start(f32[16,4096]{1,0:T(8,128)} %constant.7.clone.choice) | copy-start | bytes 786436
  0.0 15.3 %copy-start.1 = (s32[64,64]{1,0:T(8,128)S(1)}, s32[64,64]{1,0:T(8,128)}, u32[]{:S(2)}) copy-start(s32[64,64]{1,0:T(8,128)} %mask.1) | copy-start | bytes 49156
  0.0 15.3 %copy-start.2 = (f32[64,128]{1,0:T(8,128)S(1)}, f32[64,128]{1,0:T(8,128)}, u32[]{:S(2)}) copy-start(f32[64,128]{1,0:T(8,128)} %constant.6.clone.table) | copy-start | bytes 98308
  0.0 15.3 %copy-start.3 = (f32[16,256]{1,0:T(8,128)S(1)}, f32[16,256]{1,0:T(8,128)}, u32[]{:S(2)}) copy-start(f32[16,256]{1,0:T(8,128)} %constant.8.clone.same) | copy-start | bytes 49156
  2.4 10.8 %collective-permute-start = (bf16[1,224,128]{2,1,0:T(8,128)(2,1)S(1)}, bf16[1,224,128]{2,1,0:T(8,128)(2,1)S(1)}, u32[]{:S(2)}, u32[]{:S(2)}) collective-permute-start(bf16[1,224,128]{2,1,0:T(8,128)(2,1)S(1)} %get-tuple-element.42), channel_id=1, source_target_pairs={{0,7},{1,6},{2,5},{3,4},{4,3},{5,2},{6,1},{7,0},{8,15},{9,14},{10,... | collective-permute-start | bytes 172040 | tf_op jit(solution)/shard_map/ppermute | solution.py:398
  8.5 5.9 %collective-permute-start.1 = (bf16[1,224,128]{2,1,0:T(8,128)(2,1)S(1)}, bf16[1,224,128]{2,1,0:T(8,128)(2,1)S(1)}, u32[]{:S(2)}, u32[]{:S(2)}) collective-permute-start(bf16[1,224,128]{2,1,0:T(8,128)(2,1)S(1)} %get-tuple-element.43), channel_id=1, source_target_pairs={{0,4},{1,2},{2,1},{3,7},{4,0},{5,6},{6,5},{7,3},{8,12},{9,10},{10,... | collective-permute-start | bytes 172040 | tf_op jit(solution)/shard_map/ppermute | solution.py:398
  8.5 8.7 %collective-permute-start.2 = (bf16[1,224,128]{2,1,0:T(8,128)(2,1)S(1)}, bf16[1,224,128]{2,1,0:T(8,128)(2,1)S(1)}, u32[]{:S(2)}, u32[]{:S(2)}) collective-permute-start(bf16[1,224,128]{2,1,0:T(8,128)(2,1)S(1)} %get-tuple-element.44), channel_id=1, source_target_pairs={{0,3},{1,5},{2,6},{3,0},{4,7},{5,1},{6,2},{7,4},{8,11},{9,13},{10,... | collective-permute-start | bytes 172040 | tf_op jit(solution)/shard_map/ppermute | solution.py:398
  8.8 8.4 %collective-permute-start.3 = (bf16[1,224,128]{2,1,0:T(8,128)(2,1)S(1)}, bf16[1,224,128]{2,1,0:T(8,128)(2,1)S(1)}, u32[]{:S(2)}, u32[]{:S(2)}) collective-permute-start(bf16[1,224,128]{2,1,0:T(8,128)(2,1)S(1)} %get-tuple-element.45), channel_id=1, source_target_pairs={{0,5},{1,3},{2,7},{3,1},{4,6},{5,0},{6,4},{7,2},{8,13},{9,11},{10,... | collective-permute-start | bytes 172040 | tf_op jit(solution)/shard_map/ppermute | solution.py:398
  11.5 5.7 %collective-permute-start.4 = (bf16[1,224,128]{2,1,0:T(8,128)(2,1)S(1)}, bf16[1,224,128]{2,1,0:T(8,128)(2,1)S(1)}, u32[]{:S(2)}, u32[]{:S(2)}) collective-permute-start(bf16[1,224,128]{2,1,0:T(8,128)(2,1)S(1)} %get-tuple-element.46), channel_id=1, source_target_pairs={{0,2},{1,4},{2,0},{3,6},{4,1},{5,7},{6,3},{7,5},{8,10},{9,12},{10,... | collective-permute-start | bytes 172040 | tf_op jit(solution)/shard_map/ppermute | solution.py:398
  13.2 6.4 %collective-permute-start.5 = (bf16[1,224,128]{2,1,0:T(8,128)(2,1)S(1)}, bf16[1,224,128]{2,1,0:T(8,128)(2,1)S(1)}, u32[]{:S(2)}, u32[]{:S(2)}) collective-permute-start(bf16[1,224,128]{2,1,0:T(8,128)(2,1)S(1)} %get-tuple-element.47), channel_id=1, source_target_pairs={{0,6},{1,7},{2,3},{3,2},{4,5},{5,4},{6,0},{7,1},{8,14},{9,15},{10,... | collective-permute-start | bytes 172040 | tf_op jit(solution)/shard_map/ppermute | solution.py:398
  14.3 5.3 %collective-permute-start.6 = (bf16[1,224,128]{2,1,0:T(8,128)(2,1)S(1)}, bf16[1,224,128]{2,1,0:T(8,128)(2,1)S(1)}, u32[]{:S(2)}, u32[]{:S(2)}) collective-permute-start(bf16[1,224,128]{2,1,0:T(8,128)(2,1)S(1)} %get-tuple-element.48), channel_id=1, source_target_pairs={{0,1},{1,0},{2,4},{3,5},{4,2},{5,3},{6,7},{7,6},{8,9},{9,8},{10,12... | collective-permute-start | bytes 172040 | tf_op jit(solution)/shard_map/ppermute | solution.py:398
  21.0 5.3 %collective-permute-start.7 = (bf16[2,32,512]{2,1,0:T(8,128)(2,1)S(1)}, bf16[2,32,512]{2,1,0:T(8,128)(2,1)S(1)}, u32[]{:S(2)}, u32[]{:S(2)}) collective-permute-start(bf16[2,32,512]{2,1,0:T(8,128)(2,1)S(1)} %get-tuple-element.49), channel_id=1, source_target_pairs={{0,24},{1,25},{2,26},{3,27},{4,28},{5,29},{6,30},{7,31},{8,16},{9,... | collective-permute-start | bytes 196616 | tf_op jit(solution)/shard_map/ppermute | solution.py:415
  23.5 4.3 %collective-permute-start.8 = (bf16[2,32,512]{2,1,0:T(8,128)(2,1)S(1)}, bf16[2,32,512]{2,1,0:T(8,128)(2,1)S(1)}, u32[]{:S(2)}, u32[]{:S(2)}) collective-permute-start(bf16[2,32,512]{2,1,0:T(8,128)(2,1)S(1)} %get-tuple-element.50), channel_id=1, source_target_pairs={{0,8},{1,17},{2,10},{3,19},{4,12},{5,21},{6,14},{7,23},{8,0},{9,25... | collective-permute-start | bytes 196616 | tf_op jit(solution)/shard_map/ppermute | solution.py:415
  24.0 4.3 %collective-permute-start.9 = (bf16[2,32,512]{2,1,0:T(8,128)(2,1)S(1)}, bf16[2,32,512]{2,1,0:T(8,128)(2,1)S(1)}, u32[]{:S(2)}, u32[]{:S(2)}) collective-permute-start(bf16[2,32,512]{2,1,0:T(8,128)(2,1)S(1)} %get-tuple-element.51), channel_id=1, source_target_pairs={{0,16},{1,9},{2,18},{3,11},{4,20},{5,13},{6,22},{7,15},{8,24},{9,1... | collective-permute-start | bytes 196616 | tf_op jit(solution)/shard_map/ppermute | solution.py:415
  28.7 5.4 %collective-permute-start.10 = (bf16[2,32,512]{2,1,0:T(8,128)(2,1)S(1)}, bf16[2,32,512]{2,1,0:T(8,128)(2,1)S(1)}, u32[]{:S(2)}, u32[]{:S(2)}) collective-permute-start(bf16[2,32,512]{2,1,0:T(8,128)(2,1)S(1)} %get-tuple-element.53), channel_id=1, source_target_pairs={{0,24},{1,25},{2,26},{3,27},{4,28},{5,29},{6,30},{7,31},{8,16},{9,... | collective-permute-start | bytes 196616 | tf_op jit(solution)/shard_map/ppermute | solution.py:415
  30.2 4.3 %collective-permute-start.11 = (bf16[2,32,512]{2,1,0:T(8,128)(2,1)S(1)}, bf16[2,32,512]{2,1,0:T(8,128)(2,1)S(1)}, u32[]{:S(2)}, u32[]{:S(2)}) collective-permute-start(bf16[2,32,512]{2,1,0:T(8,128)(2,1)S(1)} %get-tuple-element.54), channel_id=1, source_target_pairs={{0,8},{1,17},{2,10},{3,19},{4,12},{5,21},{6,14},{7,23},{8,0},{9,25... | collective-permute-start | bytes 196616 | tf_op jit(solution)/shard_map/ppermute | solution.py:415
  30.8 4.3 %collective-permute-start.12 = (bf16[2,32,512]{2,1,0:T(8,128)(2,1)S(1)}, bf16[2,32,512]{2,1,0:T(8,128)(2,1)S(1)}, u32[]{:S(2)}, u32[]{:S(2)}) collective-permute-start(bf16[2,32,512]{2,1,0:T(8,128)(2,1)S(1)} %get-tuple-element.55), channel_id=1, source_target_pairs={{0,16},{1,9},{2,18},{3,11},{4,20},{5,13},{6,22},{7,15},{8,24},{9,1... | collective-permute-start | bytes 196616 | tf_op jit(solution)/shard_map/ppermute | solution.py:415
  36.6 6.2 %collective-permute-start.17 = (bf16[1,224,128]{2,1,0:T(8,128)(2,1)S(1)}, bf16[1,224,128]{2,1,0:T(8,128)(2,1)S(1)}, u32[]{:S(2)}, u32[]{:S(2)}) collective-permute-start(bf16[1,224,128]{2,1,0:T(8,128)(2,1)S(1)} %get-tuple-element.61), channel_id=1, source_target_pairs={{0,7},{1,6},{2,5},{3,4},{4,3},{5,2},{6,1},{7,0},{8,15},{9,14},{10,... | collective-permute-start | bytes 172040 | tf_op jit(solution)/shard_map/ppermute | solution.py:398
  36.7 7.1 %collective-permute-start.18 = (bf16[1,224,128]{2,1,0:T(8,128)(2,1)S(1)}, bf16[1,224,128]{2,1,0:T(8,128)(2,1)S(1)}, u32[]{:S(2)}, u32[]{:S(2)}) collective-permute-start(bf16[1,224,128]{2,1,0:T(8,128)(2,1)S(1)} %get-tuple-element.62), channel_id=1, source_target_pairs={{0,4},{1,2},{2,1},{3,7},{4,0},{5,6},{6,5},{7,3},{8,12},{9,10},{10,... | collective-permute-start | bytes 172040 | tf_op jit(solution)/shard_map/ppermute | solution.py:398
  38.2 6.4 %collective-permute-start.19 = (bf16[1,224,128]{2,1,0:T(8,128)(2,1)S(1)}, bf16[1,224,128]{2,1,0:T(8,128)(2,1)S(1)}, u32[]{:S(2)}, u32[]{:S(2)}) collective-permute-start(bf16[1,224,128]{2,1,0:T(8,128)(2,1)S(1)} %get-tuple-element.63), channel_id=1, source_target_pairs={{0,3},{1,5},{2,6},{3,0},{4,7},{5,1},{6,2},{7,4},{8,11},{9,13},{10,... | collective-permute-start | bytes 172040 | tf_op jit(solution)/shard_map/ppermute | solution.py:398
  40.5 6.4 %collective-permute-start.13 = (bf16[1,224,128]{2,1,0:T(8,128)(2,1)S(1)}, bf16[1,224,128]{2,1,0:T(8,128)(2,1)S(1)}, u32[]{:S(2)}, u32[]{:S(2)}) collective-permute-start(bf16[1,224,128]{2,1,0:T(8,128)(2,1)S(1)} %get-tuple-element.57), channel_id=1, source_target_pairs={{0,5},{1,3},{2,7},{3,1},{4,6},{5,0},{6,4},{7,2},{8,13},{9,11},{10,... | collective-permute-start | bytes 172040 | tf_op jit(solution)/shard_map/ppermute | solution.py:398
  40.6 6.4 %collective-permute-start.14 = (bf16[1,224,128]{2,1,0:T(8,128)(2,1)S(1)}, bf16[1,224,128]{2,1,0:T(8,128)(2,1)S(1)}, u32[]{:S(2)}, u32[]{:S(2)}) collective-permute-start(bf16[1,224,128]{2,1,0:T(8,128)(2,1)S(1)} %get-tuple-element.58), channel_id=1, source_target_pairs={{0,2},{1,4},{2,0},{3,6},{4,1},{5,7},{6,3},{7,5},{8,10},{9,12},{10,... | collective-permute-start | bytes 172040 | tf_op jit(solution)/shard_map/ppermute | solution.py:398
  42.8 6.0 %collective-permute-start.15 = (bf16[1,224,128]{2,1,0:T(8,128)(2,1)S(1)}, bf16[1,224,128]{2,1,0:T(8,128)(2,1)S(1)}, u32[]{:S(2)}, u32[]{:S(2)}) collective-permute-start(bf16[1,224,128]{2,1,0:T(8,128)(2,1)S(1)} %get-tuple-element.59), channel_id=1, source_target_pairs={{0,6},{1,7},{2,3},{3,2},{4,5},{5,4},{6,0},{7,1},{8,14},{9,15},{10,... | collective-permute-start | bytes 172040 | tf_op jit(solution)/shard_map/ppermute | solution.py:398
  43.8 5.1 %collective-permute-start.16 = (bf16[1,224,128]{2,1,0:T(8,128)(2,1)S(1)}, bf16[1,224,128]{2,1,0:T(8,128)(2,1)S(1)}, u32[]{:S(2)}, u32[]{:S(2)}) collective-permute-start(bf16[1,224,128]{2,1,0:T(8,128)(2,1)S(1)} %get-tuple-element.60), channel_id=1, source_target_pairs={{0,1},{1,0},{2,4},{3,5},{4,2},{5,3},{6,7},{7,6},{8,9},{9,8},{10,12... | collective-permute-start | bytes 172040 | tf_op jit(solution)/shard_map/ppermute | solution.py:398

commit v6 on v3

--- a/solution.py
+++ b/solution.py
@@ -111,7 +111,7 @@
     half = devices // 2
     spare, mixed = list(range(half, devices)), []
     alone = []
-    for near in reversed(range(2, half)):
+    for near in range(2, half):
         found = [
             (far, mask)
             for far in spare

time: 50.2 us -> 50.2 us (level)
  waiting for transfers between devices: 12 us -> 12.8 us
  starting transfers between devices: 25.9 us -> 25.1 us
    ppermute x14, waiting for transfers between devices: 5.27 us -> 6.16 us  [send(): lax.ppermute(value, axis, [(d, partner(d, slot)) for d in range(lax.axis_...]
    ppermute x14, starting transfers between devices: 18.8 us -> 18 us  [send(): lax.ppermute(value, axis, [(d, partner(d, slot)) for d in range(lax.axis_...]
  transfers between devices with their start and end apart: 20 -> 20, of which waited for: 9 -> 11; matrix products, arithmetic and copies ran while one was open for 0% -> 0% of each run, Pallas kernels for 9% -> 9%
where the time goes in v6:
time: 50.2 us; the launch traced here: 50.1 us
  starting transfers between devices  25.1 us (50%)
  waiting for transfers between devices  12.8 us (25%)
  Pallas kernels  12.1 us (24%)
    ppermute x14, starting transfers between devices, send(): lax.ppermute(value, axis, [(d, partner(d, slot)) for d in range(lax.axis_...  18 us
    pallas_call x8, Pallas kernels, call(): pl.pallas_call(kernel, in_specs=[spec for spec, _ in ins], out_specs=spec...  12.1 us
    ppermute x6, starting transfers between devices, to_owners(): value = lax.ppermute(value, ('freq', 'tile'), pairs)  7.11 us
    ppermute x6, waiting for transfers between devices, to_owners(): value = lax.ppermute(value, ('freq', 'tile'), pairs)  6.61 us
    ppermute x14, waiting for transfers between devices, send(): lax.ppermute(value, axis, [(d, partner(d, slot)) for d in range(lax.axis_...  6.16 us
  transfers between devices with their start and end apart: 20, of which 11 were waited for; matrix products, arithmetic and copies ran while one was open for 0% of the time, Pallas kernels for 9%

profile of v6, /device:TPU:0, one launch (start us, length us, event | category | flops | bytes accessed | tf_op | source)
XLA Modules:
  0.0 50.1 jit_solution(4988626725161110539)
XLA Ops:
  0.0 2.5 %adjoint.2 = (bf16[1,224,128]{2,1,0:T(8,128)(2,1)S(1)}, bf16[1,224,128]{2,1,0:T(8,128)(2,1)S(1)}, bf16[2,2,512,128]{3,2,1,0:T(8,128)(2,1)S(1)}, bf16[2,2,8,2,2,4...) custom-call(s32[2,16,16]{2,1,0:T(8,128)} %ranks_far.1, bf16[2,512,128]{2,1,0:T(8,128)(2,1)} %u_far.1, ...), custom_call_target="tpu_custom_call" | custom-call | flops 201326592 | bytes 786432 | tf_op jit(solution)/shard_map/adjoint/pallas_call | solution.py:28
  2.5 4.6 %collective-permute-start = (bf16[1,224,128]{2,1,0:T(8,128)(2,1)S(1)}, bf16[1,224,128]{2,1,0:T(8,128)(2,1)S(1)}, u32[]{:S(2)}, u32[]{:S(2)}) collective-permute-start(bf16[1,224,128]{2,1,0:T(8,128)(2,1)S(1)} %get-tuple-element.42), channel_id=1, source_target_pairs={{0,7},{1,6},{2,5},{3,4},{4,3},{5,2},{6,1},{7,0},{8,15},{9,14},{10,... | collective-permute-start | bytes 172040 | tf_op jit(solution)/shard_map/ppermute | solution.py:398
  7.1 0.6 %collective-permute-start.1 = (bf16[1,224,128]{2,1,0:T(8,128)(2,1)S(1)}, bf16[1,224,128]{2,1,0:T(8,128)(2,1)S(1)}, u32[]{:S(2)}, u32[]{:S(2)}) collective-permute-start(bf16[1,224,128]{2,1,0:T(8,128)(2,1)S(1)} %get-tuple-element.43), channel_id=1, source_target_pairs={{0,6},{1,7},{2,4},{3,5},{4,2},{5,3},{6,0},{7,1},{8,14},{9,15},{10,... | collective-permute-start | bytes 172040 | tf_op jit(solution)/shard_map/ppermute | solution.py:398
  7.7 1.4 %adjoint.3 = (bf16[1,224,128]{2,1,0:T(8,128)(2,1)S(1)}, bf16[1,224,128]{2,1,0:T(8,128)(2,1)S(1)}, bf16[1,224,128]{2,1,0:T(8,128)(2,1)S(1)}, bf16[1,224,128]{2,1,...) custom-call(s32[1,64]{1,0:T(1,128)S(1)} %get-tuple-element.35.short.ranks_near, ...), custom_call_target="tpu_custom_call" | custom-call | flops 603979776 | bytes 2359296 | tf_op jit(solution)/shard_map/adjoint/pallas_call | solution.py:28
  9.1 0.4 collective-permute-start.2
  9.5 3.4 %collective-permute-start.3 = (bf16[1,224,128]{2,1,0:T(8,128)(2,1)S(1)}, bf16[1,224,128]{2,1,0:T(8,128)(2,1)S(1)}, u32[]{:S(2)}, u32[]{:S(2)}) collective-permute-start(bf16[1,224,128]{2,1,0:T(8,128)(2,1)S(1)} %get-tuple-element.45), channel_id=1, source_target_pairs={{0,2},{1,4},{2,0},{3,6},{4,1},{5,7},{6,3},{7,5},{8,10},{9,12},{10,... | collective-permute-start | bytes 172040 | tf_op jit(solution)/shard_map/ppermute | solution.py:398
  12.9 0.3 collective-permute-start.5
  13.5 1.9 %prepare.1 = (bf16[2,8,2,2,2,48,256]{6,5,4,3,2,1,0:T(8,128)(2,1)S(1)}, bf16[256,256]{1,0:T(8,128)(2,1)S(1)}, bf16[256,256]{1,0:T(8,128)(2,1)S(1)}) custom-call(bf16[2,8,2,2,2,48,256]{6,5,4,3,2,1,0:T(8,128)(2,1)} %bitcast.2, s32[64,64]{1,0:T(8,128)S(1)} %copy-done.1, f32[64,128]{1,0:T(8,128)S(1)} %copy-done.2, f32[16,4096]{1,0:T(8,128)S(1)} %copy-done, ...), custom_call_target="tpu_custom_call" | custom-call | flops 6291456 | bytes 3145728 | tf_op jit(solution)/shard_map/prepare/pallas_call | solution.py:28
  15.4 0.4 collective-permute-done.3.rest_3_
  15.8 2.4 %collective-permute-done.4.rest_4_ = bf16[1,224,128]{2,1,0:T(8,128)(2,1)S(1)} collective-permute-done((bf16[1,224,128]{2,1,0:T(8,128)(2,1)S(1)}, bf16[1,224,128]{2,1,0:T(8,128)(2,1)S(1)}, u32[]{:S(2)}, u32[]{:S(2)}) %collective-permute-start.4) | collective-permute-done | bytes 57376 | tf_op jit(solution)/shard_map/ppermute | solution.py:398
  18.2 1.4 %image.1 = (bf16[2,32,512]{2,1,0:T(8,128)(2,1)S(1)}, bf16[2,32,512]{2,1,0:T(8,128)(2,1)S(1)}, bf16[2,32,512]{2,1,0:T(8,128)(2,1)S(1)}, bf16[2,32,512]{2,1,0:T(8,128)(2,1)S(1)}) custom-call(s32[1,64]{1,0:T(1,128)S(1)} %get-tuple-element.35.short.ranks_near, bf16[2,8,2,2,2,48,256]{6,5,4,3,2,1,0:T(8,128)(2,1)S(1)} %get-tuple-element.39.basis, ...), custom_call_target="tpu_custom_call" | custom-call | flops 805306368 | bytes 3145728 | tf_op jit(solution)/shard_map/image/pallas_call | solution.py:28
  19.6 2.5 %collective-permute-start.7 = (bf16[2,32,512]{2,1,0:T(8,128)(2,1)S(1)}, bf16[2,32,512]{2,1,0:T(8,128)(2,1)S(1)}, u32[]{:S(2)}, u32[]{:S(2)}) collective-permute-start(bf16[2,32,512]{2,1,0:T(8,128)(2,1)S(1)} %get-tuple-element.49), channel_id=1, source_target_pairs={{0,24},{1,25},{2,26},{3,27},{4,28},{5,29},{6,30},{7,31},{8,16},{9,... | collective-permute-start | bytes 196616 | tf_op jit(solution)/shard_map/ppermute | solution.py:415
  22.1 0.5 %collective-permute-start.8 = (bf16[2,32,512]{2,1,0:T(8,128)(2,1)S(1)}, bf16[2,32,512]{2,1,0:T(8,128)(2,1)S(1)}, u32[]{:S(2)}, u32[]{:S(2)}) collective-permute-start(bf16[2,32,512]{2,1,0:T(8,128)(2,1)S(1)} %get-tuple-element.50), channel_id=1, source_target_pairs={{0,8},{1,17},{2,10},{3,19},{4,12},{5,21},{6,14},{7,23},{8,0},{9,25... | collective-permute-start | bytes 196616 | tf_op jit(solution)/shard_map/ppermute | solution.py:415
  22.7 0.5 %collective-permute-start.9 = (bf16[2,32,512]{2,1,0:T(8,128)(2,1)S(1)}, bf16[2,32,512]{2,1,0:T(8,128)(2,1)S(1)}, u32[]{:S(2)}, u32[]{:S(2)}) collective-permute-start(bf16[2,32,512]{2,1,0:T(8,128)(2,1)S(1)} %get-tuple-element.51), channel_id=1, source_target_pairs={{0,16},{1,9},{2,18},{3,11},{4,20},{5,13},{6,22},{7,15},{8,24},{9,1... | collective-permute-start | bytes 196616 | tf_op jit(solution)/shard_map/ppermute | solution.py:415
  23.2 1.7 %collective-permute-done.7.rest_0_ = bf16[2,32,512]{2,1,0:T(8,128)(2,1)S(1)} collective-permute-done((bf16[2,32,512]{2,1,0:T(8,128)(2,1)S(1)}, bf16[2,32,512]{2,1,0:T(8,128)(2,1)S(1)}, u32[]{:S(2)}, u32[]{:S(2)}) %collective-permute-start.7) | collective-permute-done | bytes 65568 | tf_op jit(solution)/shard_map/ppermute | solution.py:415
  24.9 1.5 %collective-permute-done.8.rest_1_ = bf16[2,32,512]{2,1,0:T(8,128)(2,1)S(1)} collective-permute-done((bf16[2,32,512]{2,1,0:T(8,128)(2,1)S(1)}, bf16[2,32,512]{2,1,0:T(8,128)(2,1)S(1)}, u32[]{:S(2)}, u32[]{:S(2)}) %collective-permute-start.8) | collective-permute-done | bytes 65568 | tf_op jit(solution)/shard_map/ppermute | solution.py:415
  26.4 0.5 %collective-permute-done.9.rest_2_ = bf16[2,32,512]{2,1,0:T(8,128)(2,1)S(1)} collective-permute-done((bf16[2,32,512]{2,1,0:T(8,128)(2,1)S(1)}, bf16[2,32,512]{2,1,0:T(8,128)(2,1)S(1)}, u32[]{:S(2)}, u32[]{:S(2)}) %collective-permute-start.9) | collective-permute-done | bytes 65568 | tf_op jit(solution)/shard_map/ppermute | solution.py:415
  26.9 0.4 mix.1
  27.3 1.6 %collective-permute-start.10 = (bf16[2,32,512]{2,1,0:T(8,128)(2,1)S(1)}, bf16[2,32,512]{2,1,0:T(8,128)(2,1)S(1)}, u32[]{:S(2)}, u32[]{:S(2)}) collective-permute-start(bf16[2,32,512]{2,1,0:T(8,128)(2,1)S(1)} %get-tuple-element.53), channel_id=1, source_target_pairs={{0,24},{1,25},{2,26},{3,27},{4,28},{5,29},{6,30},{7,31},{8,16},{9,... | collective-permute-start | bytes 196616 | tf_op jit(solution)/shard_map/ppermute | solution.py:415
  28.9 0.5 %collective-permute-start.11 = (bf16[2,32,512]{2,1,0:T(8,128)(2,1)S(1)}, bf16[2,32,512]{2,1,0:T(8,128)(2,1)S(1)}, u32[]{:S(2)}, u32[]{:S(2)}) collective-permute-start(bf16[2,32,512]{2,1,0:T(8,128)(2,1)S(1)} %get-tuple-element.54), channel_id=1, source_target_pairs={{0,8},{1,17},{2,10},{3,19},{4,12},{5,21},{6,14},{7,23},{8,0},{9,25... | collective-permute-start | bytes 196616 | tf_op jit(solution)/shard_map/ppermute | solution.py:415
  29.5 1.4 %collective-permute-start.12 = (bf16[2,32,512]{2,1,0:T(8,128)(2,1)S(1)}, bf16[2,32,512]{2,1,0:T(8,128)(2,1)S(1)}, u32[]{:S(2)}, u32[]{:S(2)}) collective-permute-start(bf16[2,32,512]{2,1,0:T(8,128)(2,1)S(1)} %get-tuple-element.55), channel_id=1, source_target_pairs={{0,16},{1,9},{2,18},{3,11},{4,20},{5,13},{6,22},{7,15},{8,24},{9,1... | collective-permute-start | bytes 196616 | tf_op jit(solution)/shard_map/ppermute | solution.py:415
  30.9 2.1 %collective-permute-done.10.rest_0_ = bf16[2,32,512]{2,1,0:T(8,128)(2,1)S(1)} collective-permute-done((bf16[2,32,512]{2,1,0:T(8,128)(2,1)S(1)}, bf16[2,32,512]{2,1,0:T(8,128)(2,1)S(1)}, u32[]{:S(2)}, u32[]{:S(2)}) %collective-permute-start.10) | collective-permute-done | bytes 65568 | tf_op jit(solution)/shard_map/ppermute | solution.py:415
  33.2 0.5 %collective-permute-done.12.rest_2_ = bf16[2,32,512]{2,1,0:T(8,128)(2,1)S(1)} collective-permute-done((bf16[2,32,512]{2,1,0:T(8,128)(2,1)S(1)}, bf16[2,32,512]{2,1,0:T(8,128)(2,1)S(1)}, u32[]{:S(2)}, u32[]{:S(2)}) %collective-permute-start.12) | collective-permute-done | bytes 65568 | tf_op jit(solution)/shard_map/ppermute | solution.py:415
  33.7 1.6 %forward.1 = (bf16[1,224,128]{2,1,0:T(8,128)(2,1)S(1)}, bf16[1,224,128]{2,1,0:T(8,128)(2,1)S(1)}, bf16[1,224,128]{2,1,0:T(8,128)(2,1)S(1)}, bf16[1,224,128]{2,1,...) custom-call(s32[1,64]{1,0:T(1,128)S(1)} %get-tuple-element.35.short., ...), custom_call_target="tpu_custom_call" | custom-call | flops 805306368 | bytes 3145728 | tf_op jit(solution)/shard_map/forward/pallas_call | solution.py:28
  35.6 1.7 %collective-permute-start.17 = (bf16[1,224,128]{2,1,0:T(8,128)(2,1)S(1)}, bf16[1,224,128]{2,1,0:T(8,128)(2,1)S(1)}, u32[]{:S(2)}, u32[]{:S(2)}) collective-permute-start(bf16[1,224,128]{2,1,0:T(8,128)(2,1)S(1)} %get-tuple-element.61), channel_id=1, source_target_pairs={{0,6},{1,7},{2,4},{3,5},{4,2},{5,3},{6,0},{7,1},{8,14},{9,15},{10,... | collective-permute-start | bytes 172040 | tf_op jit(solution)/shard_map/ppermute | solution.py:398
  37.3 1.1 %collective-permute-start.18 = (bf16[1,224,128]{2,1,0:T(8,128)(2,1)S(1)}, bf16[1,224,128]{2,1,0:T(8,128)(2,1)S(1)}, u32[]{:S(2)}, u32[]{:S(2)}) collective-permute-start(bf16[1,224,128]{2,1,0:T(8,128)(2,1)S(1)} %get-tuple-element.62), channel_id=1, source_target_pairs={{0,5},{1,3},{2,7},{3,1},{4,6},{5,0},{6,4},{7,2},{8,13},{9,11},{10,... | collective-permute-start | bytes 172040 | tf_op jit(solution)/shard_map/ppermute | solution.py:398
  38.4 2.6 %collective-permute-start.19 = (bf16[1,224,128]{2,1,0:T(8,128)(2,1)S(1)}, bf16[1,224,128]{2,1,0:T(8,128)(2,1)S(1)}, u32[]{:S(2)}, u32[]{:S(2)}) collective-permute-start(bf16[1,224,128]{2,1,0:T(8,128)(2,1)S(1)} %get-tuple-element.63), channel_id=1, source_target_pairs={{0,2},{1,4},{2,0},{3,6},{4,1},{5,7},{6,3},{7,5},{8,10},{9,12},{10,... | collective-permute-start | bytes 172040 | tf_op jit(solution)/shard_map/ppermute | solution.py:398
  41.0 0.5 %collective-permute-start.13 = (bf16[1,224,128]{2,1,0:T(8,128)(2,1)S(1)}, bf16[1,224,128]{2,1,0:T(8,128)(2,1)S(1)}, u32[]{:S(2)}, u32[]{:S(2)}) collective-permute-start(bf16[1,224,128]{2,1,0:T(8,128)(2,1)S(1)} %get-tuple-element.57), channel_id=1, source_target_pairs={{0,4},{1,2},{2,1},{3,7},{4,0},{5,6},{6,5},{7,3},{8,12},{9,10},{10,... | collective-permute-start | bytes 172040 | tf_op jit(solution)/shard_map/ppermute | solution.py:398
  41.7 2.3 %collective-permute-start.15 = (bf16[1,224,128]{2,1,0:T(8,128)(2,1)S(1)}, bf16[1,224,128]{2,1,0:T(8,128)(2,1)S(1)}, u32[]{:S(2)}, u32[]{:S(2)}) collective-permute-start(bf16[1,224,128]{2,1,0:T(8,128)(2,1)S(1)} %get-tuple-element.59), channel_id=1, source_target_pairs={{0,1},{1,0},{2,3},{3,2},{4,5},{5,4},{6,7},{7,6},{8,9},{9,8},{10,11... | collective-permute-start | bytes 172040 | tf_op jit(solution)/shard_map/ppermute | solution.py:398
  44.0 3.0 %collective-permute-done.18.rest_2_ = bf16[1,224,128]{2,1,0:T(8,128)(2,1)S(1)} collective-permute-done((bf16[1,224,128]{2,1,0:T(8,128)(2,1)S(1)}, bf16[1,224,128]{2,1,0:T(8,128)(2,1)S(1)}, u32[]{:S(2)}, u32[]{:S(2)}) %collective-permute-start.18) | collective-permute-done | bytes 57376 | tf_op jit(solution)/shard_map/ppermute | solution.py:398
  47.0 1.1 %result.2.rest_3_ = f32[2,2,128,256]{3,2,1,0:T(8,128)S(1)} custom-call(s32[1,64]{1,0:T(1,128)S(1)} %get-tuple-element.35.short.ranks_near, bf16[2,2,8,2,2,48,256]{6,5,4,3,2,1,0:T(8,128)(2,1)S(1)} %get-tuple-element.36.basis, bf16[1,224,128]{2,1,0:T(8,128)(2,1)S(1)} %collective-permute-done.16.rest_0_, ...), custom_call_target="tpu_custom_call" | custom-call | flops 503316480 | bytes 1966080 | tf_op jit(solution)/shard_map/result/pallas_call | solution.py:28
  48.2 1.9 %result.3 = bf16[2,512,128]{2,1,0:T(8,128)(2,1)} custom-call(s32[1,64]{1,0:T(1,128)S(1)} %get-tuple-element.35.short.ranks_near, bf16[2,2,8,2,2,48,256]{6,5,4,3,2,1,0:T(8,128)(2,1)S(1)} %get-tuple-element.36.basis, bf16[1,224,128]{2,1,0:T(8,128)(2,1)S(1)} %collective-permute-done.13.rest_0_, bf16[1,224,128]{2,1,0:T(8,128)(2,1)S(1)} %collective-permute-done.14.rest_1_, ...), custom_call_target="tpu_custom_call" | custom-call | flops 301989888 | bytes 1179648 | tf_op jit(solution)/shard_map/result/pallas_call | solution.py:28
  (24 shorter events, 0.9 us)
Async XLA Ops:
  0.0 13.5 %copy-start = (f32[16,4096]{1,0:T(8,128)S(1)}, f32[16,4096]{1,0:T(8,128)}, u32[]{:S(2)}) copy-start(f32[16,4096]{1,0:T(8,128)} %constant.7.clone.choice) | copy-start | bytes 786436
  0.0 13.5 %copy-start.1 = (s32[64,64]{1,0:T(8,128)S(1)}, s32[64,64]{1,0:T(8,128)}, u32[]{:S(2)}) copy-start(s32[64,64]{1,0:T(8,128)} %mask.1) | copy-start | bytes 49156
  0.0 13.5 %copy-start.2 = (f32[64,128]{1,0:T(8,128)S(1)}, f32[64,128]{1,0:T(8,128)}, u32[]{:S(2)}) copy-start(f32[64,128]{1,0:T(8,128)} %constant.6.clone.table) | copy-start | bytes 98308
  0.0 13.5 %copy-start.3 = (f32[16,256]{1,0:T(8,128)S(1)}, f32[16,256]{1,0:T(8,128)}, u32[]{:S(2)}) copy-start(f32[16,256]{1,0:T(8,128)} %constant.8.clone.same) | copy-start | bytes 49156
  2.5 10.4 %collective-permute-start = (bf16[1,224,128]{2,1,0:T(8,128)(2,1)S(1)}, bf16[1,224,128]{2,1,0:T(8,128)(2,1)S(1)}, u32[]{:S(2)}, u32[]{:S(2)}) collective-permute-start(bf16[1,224,128]{2,1,0:T(8,128)(2,1)S(1)} %get-tuple-element.42), channel_id=1, source_target_pairs={{0,7},{1,6},{2,5},{3,4},{4,3},{5,2},{6,1},{7,0},{8,15},{9,14},{10,... | collective-permute-start | bytes 172040 | tf_op jit(solution)/shard_map/ppermute | solution.py:398
  7.1 6.4 %collective-permute-start.1 = (bf16[1,224,128]{2,1,0:T(8,128)(2,1)S(1)}, bf16[1,224,128]{2,1,0:T(8,128)(2,1)S(1)}, u32[]{:S(2)}, u32[]{:S(2)}) collective-permute-start(bf16[1,224,128]{2,1,0:T(8,128)(2,1)S(1)} %get-tuple-element.43), channel_id=1, source_target_pairs={{0,6},{1,7},{2,4},{3,5},{4,2},{5,3},{6,0},{7,1},{8,14},{9,15},{10,... | collective-permute-start | bytes 172040 | tf_op jit(solution)/shard_map/ppermute | solution.py:398
  9.1 6.4 %collective-permute-start.2 = (bf16[1,224,128]{2,1,0:T(8,128)(2,1)S(1)}, bf16[1,224,128]{2,1,0:T(8,128)(2,1)S(1)}, u32[]{:S(2)}, u32[]{:S(2)}) collective-permute-start(bf16[1,224,128]{2,1,0:T(8,128)(2,1)S(1)} %get-tuple-element.44), channel_id=1, source_target_pairs={{0,5},{1,3},{2,7},{3,1},{4,6},{5,0},{6,4},{7,2},{8,13},{9,11},{10,... | collective-permute-start | bytes 172040 | tf_op jit(solution)/shard_map/ppermute | solution.py:398
  9.5 6.3 %collective-permute-start.3 = (bf16[1,224,128]{2,1,0:T(8,128)(2,1)S(1)}, bf16[1,224,128]{2,1,0:T(8,128)(2,1)S(1)}, u32[]{:S(2)}, u32[]{:S(2)}) collective-permute-start(bf16[1,224,128]{2,1,0:T(8,128)(2,1)S(1)} %get-tuple-element.45), channel_id=1, source_target_pairs={{0,2},{1,4},{2,0},{3,6},{4,1},{5,7},{6,3},{7,5},{8,10},{9,12},{10,... | collective-permute-start | bytes 172040 | tf_op jit(solution)/shard_map/ppermute | solution.py:398
  12.9 5.3 %collective-permute-start.4 = (bf16[1,224,128]{2,1,0:T(8,128)(2,1)S(1)}, bf16[1,224,128]{2,1,0:T(8,128)(2,1)S(1)}, u32[]{:S(2)}, u32[]{:S(2)}) collective-permute-start(bf16[1,224,128]{2,1,0:T(8,128)(2,1)S(1)} %get-tuple-element.46), channel_id=1, source_target_pairs={{0,4},{1,2},{2,1},{3,7},{4,0},{5,6},{6,5},{7,3},{8,12},{9,10},{10,... | collective-permute-start | bytes 172040 | tf_op jit(solution)/shard_map/ppermute | solution.py:398
  12.9 5.3 %collective-permute-start.5 = (bf16[1,224,128]{2,1,0:T(8,128)(2,1)S(1)}, bf16[1,224,128]{2,1,0:T(8,128)(2,1)S(1)}, u32[]{:S(2)}, u32[]{:S(2)}) collective-permute-start(bf16[1,224,128]{2,1,0:T(8,128)(2,1)S(1)} %get-tuple-element.47), channel_id=1, source_target_pairs={{0,3},{1,5},{2,6},{3,0},{4,7},{5,1},{6,2},{7,4},{8,11},{9,13},{10,... | collective-permute-start | bytes 172040 | tf_op jit(solution)/shard_map/ppermute | solution.py:398
  13.5 4.7 %collective-permute-start.6 = (bf16[1,224,128]{2,1,0:T(8,128)(2,1)S(1)}, bf16[1,224,128]{2,1,0:T(8,128)(2,1)S(1)}, u32[]{:S(2)}, u32[]{:S(2)}) collective-permute-start(bf16[1,224,128]{2,1,0:T(8,128)(2,1)S(1)} %get-tuple-element.48), channel_id=1, source_target_pairs={{0,1},{1,0},{2,3},{3,2},{4,5},{5,4},{6,7},{7,6},{8,9},{9,8},{10,11... | collective-permute-start | bytes 172040 | tf_op jit(solution)/shard_map/ppermute | solution.py:398
  19.6 5.3 %collective-permute-start.7 = (bf16[2,32,512]{2,1,0:T(8,128)(2,1)S(1)}, bf16[2,32,512]{2,1,0:T(8,128)(2,1)S(1)}, u32[]{:S(2)}, u32[]{:S(2)}) collective-permute-start(bf16[2,32,512]{2,1,0:T(8,128)(2,1)S(1)} %get-tuple-element.49), channel_id=1, source_target_pairs={{0,24},{1,25},{2,26},{3,27},{4,28},{5,29},{6,30},{7,31},{8,16},{9,... | collective-permute-start | bytes 196616 | tf_op jit(solution)/shard_map/ppermute | solution.py:415
  22.1 4.3 %collective-permute-start.8 = (bf16[2,32,512]{2,1,0:T(8,128)(2,1)S(1)}, bf16[2,32,512]{2,1,0:T(8,128)(2,1)S(1)}, u32[]{:S(2)}, u32[]{:S(2)}) collective-permute-start(bf16[2,32,512]{2,1,0:T(8,128)(2,1)S(1)} %get-tuple-element.50), channel_id=1, source_target_pairs={{0,8},{1,17},{2,10},{3,19},{4,12},{5,21},{6,14},{7,23},{8,0},{9,25... | collective-permute-start | bytes 196616 | tf_op jit(solution)/shard_map/ppermute | solution.py:415
  22.7 4.3 %collective-permute-start.9 = (bf16[2,32,512]{2,1,0:T(8,128)(2,1)S(1)}, bf16[2,32,512]{2,1,0:T(8,128)(2,1)S(1)}, u32[]{:S(2)}, u32[]{:S(2)}) collective-permute-start(bf16[2,32,512]{2,1,0:T(8,128)(2,1)S(1)} %get-tuple-element.51), channel_id=1, source_target_pairs={{0,16},{1,9},{2,18},{3,11},{4,20},{5,13},{6,22},{7,15},{8,24},{9,1... | collective-permute-start | bytes 196616 | tf_op jit(solution)/shard_map/ppermute | solution.py:415
  27.3 5.7 %collective-permute-start.10 = (bf16[2,32,512]{2,1,0:T(8,128)(2,1)S(1)}, bf16[2,32,512]{2,1,0:T(8,128)(2,1)S(1)}, u32[]{:S(2)}, u32[]{:S(2)}) collective-permute-start(bf16[2,32,512]{2,1,0:T(8,128)(2,1)S(1)} %get-tuple-element.53), channel_id=1, source_target_pairs={{0,24},{1,25},{2,26},{3,27},{4,28},{5,29},{6,30},{7,31},{8,16},{9,... | collective-permute-start | bytes 196616 | tf_op jit(solution)/shard_map/ppermute | solution.py:415
  28.9 4.3 %collective-permute-start.11 = (bf16[2,32,512]{2,1,0:T(8,128)(2,1)S(1)}, bf16[2,32,512]{2,1,0:T(8,128)(2,1)S(1)}, u32[]{:S(2)}, u32[]{:S(2)}) collective-permute-start(bf16[2,32,512]{2,1,0:T(8,128)(2,1)S(1)} %get-tuple-element.54), channel_id=1, source_target_pairs={{0,8},{1,17},{2,10},{3,19},{4,12},{5,21},{6,14},{7,23},{8,0},{9,25... | collective-permute-start | bytes 196616 | tf_op jit(solution)/shard_map/ppermute | solution.py:415
  29.5 4.3 %collective-permute-start.12 = (bf16[2,32,512]{2,1,0:T(8,128)(2,1)S(1)}, bf16[2,32,512]{2,1,0:T(8,128)(2,1)S(1)}, u32[]{:S(2)}, u32[]{:S(2)}) collective-permute-start(bf16[2,32,512]{2,1,0:T(8,128)(2,1)S(1)} %get-tuple-element.55), channel_id=1, source_target_pairs={{0,16},{1,9},{2,18},{3,11},{4,20},{5,13},{6,22},{7,15},{8,24},{9,1... | collective-permute-start | bytes 196616 | tf_op jit(solution)/shard_map/ppermute | solution.py:415
  35.3 6.3 %collective-permute-start.16 = (bf16[1,224,128]{2,1,0:T(8,128)(2,1)S(1)}, bf16[1,224,128]{2,1,0:T(8,128)(2,1)S(1)}, u32[]{:S(2)}, u32[]{:S(2)}) collective-permute-start(bf16[1,224,128]{2,1,0:T(8,128)(2,1)S(1)} %get-tuple-element.60), channel_id=1, source_target_pairs={{0,7},{1,6},{2,5},{3,4},{4,3},{5,2},{6,1},{7,0},{8,15},{9,14},{10,... | collective-permute-start | bytes 172040 | tf_op jit(solution)/shard_map/ppermute | solution.py:398
  35.6 6.0 %collective-permute-start.17 = (bf16[1,224,128]{2,1,0:T(8,128)(2,1)S(1)}, bf16[1,224,128]{2,1,0:T(8,128)(2,1)S(1)}, u32[]{:S(2)}, u32[]{:S(2)}) collective-permute-start(bf16[1,224,128]{2,1,0:T(8,128)(2,1)S(1)} %get-tuple-element.61), channel_id=1, source_target_pairs={{0,6},{1,7},{2,4},{3,5},{4,2},{5,3},{6,0},{7,1},{8,14},{9,15},{10,... | collective-permute-start | bytes 172040 | tf_op jit(solution)/shard_map/ppermute | solution.py:398
  37.3 9.7 %collective-permute-start.18 = (bf16[1,224,128]{2,1,0:T(8,128)(2,1)S(1)}, bf16[1,224,128]{2,1,0:T(8,128)(2,1)S(1)}, u32[]{:S(2)}, u32[]{:S(2)}) collective-permute-start(bf16[1,224,128]{2,1,0:T(8,128)(2,1)S(1)} %get-tuple-element.62), channel_id=1, source_target_pairs={{0,5},{1,3},{2,7},{3,1},{4,6},{5,0},{6,4},{7,2},{8,13},{9,11},{10,... | collective-permute-start | bytes 172040 | tf_op jit(solution)/shard_map/ppermute | solution.py:398
  38.4 8.6 %collective-permute-start.19 = (bf16[1,224,128]{2,1,0:T(8,128)(2,1)S(1)}, bf16[1,224,128]{2,1,0:T(8,128)(2,1)S(1)}, u32[]{:S(2)}, u32[]{:S(2)}) collective-permute-start(bf16[1,224,128]{2,1,0:T(8,128)(2,1)S(1)} %get-tuple-element.63), channel_id=1, source_target_pairs={{0,2},{1,4},{2,0},{3,6},{4,1},{5,7},{6,3},{7,5},{8,10},{9,12},{10,... | collective-permute-start | bytes 172040 | tf_op jit(solution)/shard_map/ppermute | solution.py:398
  41.0 7.1 %collective-permute-start.13 = (bf16[1,224,128]{2,1,0:T(8,128)(2,1)S(1)}, bf16[1,224,128]{2,1,0:T(8,128)(2,1)S(1)}, u32[]{:S(2)}, u32[]{:S(2)}) collective-permute-start(bf16[1,224,128]{2,1,0:T(8,128)(2,1)S(1)} %get-tuple-element.57), channel_id=1, source_target_pairs={{0,4},{1,2},{2,1},{3,7},{4,0},{5,6},{6,5},{7,3},{8,12},{9,10},{10,... | collective-permute-start | bytes 172040 | tf_op jit(solution)/shard_map/ppermute | solution.py:398
  41.6 6.6 %collective-permute-start.14 = (bf16[1,224,128]{2,1,0:T(8,128)(2,1)S(1)}, bf16[1,224,128]{2,1,0:T(8,128)(2,1)S(1)}, u32[]{:S(2)}, u32[]{:S(2)}) collective-permute-start(bf16[1,224,128]{2,1,0:T(8,128)(2,1)S(1)} %get-tuple-element.58), channel_id=1, source_target_pairs={{0,3},{1,5},{2,6},{3,0},{4,7},{5,1},{6,2},{7,4},{8,11},{9,13},{10,... | collective-permute-start | bytes 172040 | tf_op jit(solution)/shard_map/ppermute | solution.py:398
  41.7 6.5 %collective-permute-start.15 = (bf16[1,224,128]{2,1,0:T(8,128)(2,1)S(1)}, bf16[1,224,128]{2,1,0:T(8,128)(2,1)S(1)}, u32[]{:S(2)}, u32[]{:S(2)}) collective-permute-start(bf16[1,224,128]{2,1,0:T(8,128)(2,1)S(1)} %get-tuple-element.59), channel_id=1, source_target_pairs={{0,1},{1,0},{2,3},{3,2},{4,5},{5,4},{6,7},{7,6},{8,9},{9,8},{10,11... | collective-permute-start | bytes 172040 | tf_op jit(solution)/shard_map/ppermute | solution.py:398
